TPU v7x, 128 devices: a whole 4x4x4 slice. The times are simulated.
128 devices in a mesh: dom: 8 (over y, core), col: 16 (over z, x).
Axes of the slice: x: 4, y: 4, z: 4, core: 2. Of those that a mesh axis runs over, the one named last changes fastest.
Arguments:
- orbitals: bfloat16 [128, 16, 128, 1024], P(('dom', 'col')), may hold values from -1 to 1
- potential: float32 [128, 1024], P(('dom', 'col')), may hold values from -6 to 6
- domain_start: int32 [128], P(('dom', 'col')), may hold values from 0 to 31
- margin_pairs: int32 [128, 2, 228], P(('dom', 'col')), may hold values from 0 to 15, as said below
- coefficients: bfloat16 [4, 8, 128, 16, 128], P(None, 'dom', None, 'col'), may hold values from -0.25 to 0.25
Outputs:
- potential_blocks: bfloat16 [4, 8, 2, 16, 128, 128], P(None, 'dom', None, 'col')
- product: float32 [2, 16, 128, 16, 128], P(None, 'col', None, 'dom')
Inputs may be any that keep to these rules, and one draw needn't show every extreme that they name: `margin_pairs`: each domain lists 228 distinct ordered pairs; if (a, b) is listed so is (b, a); every pair with |a - b| <= 8 is listed.
All inputs are finite; a program needn't handle non-finite values.
Results may differ from a plain program's by a relative error of at most 0.0057.
Values may be sent and summed in bfloat16 or wider, within the bound.
No kernel may reach another device: no remote copies, remote signals or barrier semaphores. Data moves between devices by JAX's collectives and lax.ppermute only.
A program may use at most 128 MiB of HBM per device.

v0:
```python
import jax
import jax.numpy as jnp
from jax import lax
from jax.sharding import PartitionSpec as P


def shards(orbitals, potential, domain_start, margin_pairs, coefficients):
    dom_count = lax.axis_size("dom")
    col_count = lax.axis_size("col")
    devices = dom_count * col_count
    local_count = orbitals.shape[1]
    block_size = orbitals.shape[2]
    row_blocks = coefficients.shape[0]
    total_blocks = row_blocks * dom_count
    col_blocks = total_blocks // col_count
    capacity = (
        (local_count + dom_count - 1) // dom_count * ((local_count + col_count - 1) // col_count)
    )
    owned_count = row_blocks * col_blocks
    weighted = (orbitals[0] * potential[0][None, None, :]).astype(jnp.bfloat16)
    dense_blocks = jnp.einsum(
        "aig,bjg->abij", weighted, orbitals[0], preferred_element_type=jnp.float32
    )
    pair_rows = margin_pairs[0, 0]
    pair_cols = margin_pairs[0, 1]
    picked = dense_blocks[pair_rows, pair_cols].astype(jnp.bfloat16)
    first_block = domain_start[0]
    row_block = (first_block + pair_rows) % total_blocks
    col_block = (first_block + pair_cols) % total_blocks
    owner_index = row_block % dom_count * col_count + col_block % col_count
    owner_slot = row_block // dom_count * col_blocks + col_block // col_count
    pair_count = pair_rows.shape[0]
    same_owner = owner_index[:, None] == owner_index[None, :]
    earlier = jnp.arange(pair_count)[:, None] > jnp.arange(pair_count)[None, :]
    slot_rank = jnp.sum((same_owner & earlier).astype(jnp.int32), axis=1)
    target = owner_index * capacity + slot_rank
    outgoing = (
        jnp.zeros((devices * capacity, block_size, block_size), jnp.bfloat16).at[target].set(picked)
    )
    positions = jnp.full((devices * capacity,), owned_count, jnp.int32).at[target].set(owner_slot)
    incoming, arrived_at = (
        lax.all_to_all(
            outgoing.reshape(devices, capacity, block_size, block_size),
            ("dom", "col"),
            split_axis=0,
            concat_axis=0,
            tiled=True,
        ),
        lax.all_to_all(
            positions.reshape(devices, capacity),
            ("dom", "col"),
            split_axis=0,
            concat_axis=0,
            tiled=True,
        ),
    )
    selector = (arrived_at.reshape(-1)[None, :] == jnp.arange(owned_count)[:, None]).astype(
        jnp.bfloat16
    )
    summed = jnp.dot(
        selector,
        incoming.reshape(devices * capacity, block_size * block_size),
        preferred_element_type=jnp.float32,
    )
    owned = summed.astype(jnp.bfloat16)
    potential_blocks = owned.reshape(row_blocks, 1, col_blocks, 1, block_size, block_size)
    owned_grid = owned.reshape(row_blocks, col_blocks, block_size, block_size)
    shard_rows = lax.all_gather(coefficients, "col", axis=3, tiled=True)
    flat_panel = shard_rows.reshape(
        shard_rows.shape[0], shard_rows.shape[2], shard_rows.shape[3] * shard_rows.shape[4]
    )
    applied = jnp.einsum(
        "rcij,rim->cjm", owned_grid, flat_panel, preferred_element_type=jnp.float32
    )
    partial_sums = applied.reshape(
        col_blocks, 1, block_size, shard_rows.shape[3], shard_rows.shape[4]
    )
    product = lax.psum_scatter(partial_sums, "dom", scatter_dimension=3, tiled=True)
    return (potential_blocks, product)


def solution(mesh):
    placed = (
        P(("dom", "col"), None, None, None),
        P(("dom", "col"), None),
        P(("dom", "col")),
        P(("dom", "col"), None, None),
        P(None, "dom", None, "col", None),
    )
    return jax.shard_map(
        shards,
        mesh=mesh,
        in_specs=placed,
        out_specs=(P(None, "dom", None, "col", None, None), P(None, "col", None, "dom", None)),
        check_vma=False,
    )
```

profile of v0, /device:TPU:1, one launch (start us, length us, event | category | flops | bytes accessed | tf_op | source)
XLA Modules:
  0.0 299.9 jit_solution(2971712123880036097)
XLA Ops:
  7.8 0.8 broadcast_add_fusion
  8.6 0.2 convert_reduce_fusion
  8.8 0.8 fusion.31
  9.6 1.3 scatter_custom_fusion
  10.9 0.8 all_to_all.9
  11.7 11.5 %all-to-all-start = ((s32[128,1,2]{2,1,0:T(1,128)}), s32[128,1,2]{2,1,0:T(1,128)S(1)}, u32[]{:S(2)}, u32[]{:S(2)}) async-start(s32[128,1,2]{2,1,0:T(1,128)} %bitcast.7), calls=%async_computation | async-start | bytes 131072 | tf_op jit(solution)/shard_map/all_to_all | solution.py:49
  23.2 13.7 %convolution_bitcast_fusion = bf16[16,16,128,128]{3,2,1,0:T(8,128)(2,1)} fusion(bf16[1,16,128,1024]{3,2,1,0:T(8,128)(2,1)} %param.5, f32[1024]{0:T(1024)} %bitcast.96), kind=kOutput, calls=%fused_computation.4 | convolution fusion | flops 8596226048 | bytes 12587008 | tf_op jit(solution)/shard_map/aig,bjg->abij/dot_general | solution.py:21
  36.9 15.5 %gather_fusion = bf16[228,128,128]{2,1,0:T(8,128)(2,1)} fusion(bf16[16,16,128,128]{3,2,1,0:T(8,128)(2,1)} %convolution_bitcast_fusion, s32[228]{0:T(256)S(1)} %bitcast.88), kind=kCustom, calls=%fused_computation | custom fusion | bytes 14944032 | tf_op jit(solution)/shard_map/gather | solution.py:26
  52.4 5.3 %broadcast_in_dim.5 = bf16[256,128,128]{2,1,0:T(8,128)(2,1)} broadcast(bf16[]{:T(256)} %constant.85.clone.1), dimensions={} | broadcast | bytes 8388610 | tf_op jit(solution)/shard_map/broadcast_in_dim | solution.py:38
  57.8 35.5 %scatter_fusion = bf16[256,128,128]{2,1,0:T(8,128)(2,1)} fusion(bf16[256,128,128]{2,1,0:T(8,128)(2,1)} %broadcast_in_dim.5, s32[228]{0:T(256)S(1)} %bitcast.92, bf16[228,128,128]{2,1,0:T(8,128)(2,1)} %gather_fusion), kind=kCustom, calls=%fused_computation.2 | custom fusion | bytes 22414224 | tf_op jit(solution)/shard_map/scatter | solution.py:38
  93.3 0.0 all-to-all-done
  93.3 10.3 %all-to-all-start.1 = ((bf16[128,2,128,128]{3,2,1,0:T(8,128)(2,1)}), bf16[128,2,128,128]{3,2,1,0:T(8,128)(2,1)}, u32[]{:S(2)}, u32[]{:S(2)}) async-start(bf16[128,2,128,128]{3,2,1,0:T(8,128)(2,1)} %bitcast.87), calls=%async_computation.1 | async-start | bytes 16777216 | tf_op jit(solution)/shard_map/all_to_all | solution.py:42
  103.6 0.0 all-gather.2.cloned.1.call-start
  103.6 0.0 copy-done.1
  103.6 0.8 copy.23
  104.4 0.0 all-gather.2.cloned.1.call-update
  104.4 0.2 all-reduce.3.cloned.1.call-start
  104.6 0.5 broadcast.499
  105.2 0.8 reduce.3
  106.0 0.1 eq.36
  106.1 99.8 %all-to-all-done.1 = bf16[128,2,128,128]{3,2,1,0:T(8,128)(2,1)} async-done(((bf16[128,2,128,128]{3,2,1,0:T(8,128)(2,1)}), bf16[128,2,128,128]{3,2,1,0:T(8,128)(2,1)}, u32[]{:S(2)}, u32[]{:S(2)}) %all-to-all-start.1) | async-done | bytes 8388640 | tf_op jit(solution)/shard_map/all_to_all | solution.py:42
  205.9 7.9 %fusion.12 = bf16[1,8,128,128]{3,1,2,0:T(8,128)(2,1)S(1)} fusion(bf16[32,8,128,128]{3,2,1,0:T(8,128)(2,1)} %bitcast.43, s32[256]{0:T(256)S(1)} %eq.36), kind=kOutput, calls=%fused_computation.15 | convolution fusion | flops 67241984 | bytes 8651776 | tf_op jit(solution)/shard_map/dot_general | solution.py:60
  213.8 0.0 copy-start
  213.8 0.2 copy.22
  214.0 10.0 %all-gather.2.cloned.1.call-done = bf16[4,1,128,16,128]{2,4,3,0,1:T(8,128)(2,1)} async-done(((bf16[4,1,128,1,128]{2,4,3,0,1:T(8,128)(2,1)}), bf16[4,1,128,16,128]{2,4,3,0,1:T(8,128)(2,1)}) %all-gather.2.cloned.1.call-update) | async-done | bytes 2097168 | tf_op jit(solution)/shard_map/all_gather | solution.py:68
  224.0 3.7 %fusion.9 = f32[2,1,128,16,128]{4,2,3,0,1:T(8,128)} fusion(bf16[4,2,128,128]{2,3,0,1:T(8,128)(2,1)S(1)} %copy.22, bf16[4,1,128,16,128]{2,4,3,0,1:T(8,128)(2,1)} %all-gather.2.cloned.1.call-done), kind=kOutput, calls=%fused_computation.14 | convolution fusion | flops 536870912 | bytes 4456448 | tf_op jit(solution)/shard_map/rcij,rim->cjm/dot_general | solution.py:72
  227.7 0.0 all-reduce.3.cloned.1.call-update
  227.7 0.0 copy-done.2
  227.7 0.6 dynamic-slice
  228.9 62.3 %all-reduce.3.cloned.1.call-done = f32[2,1,128,16,128]{4,2,3,0,1:T(8,128)} async-done(((f32[2,1,128,16,128]{4,2,3,0,1:T(8,128)}), f32[2,1,128,16,128]{4,2,3,0,1:T(8,128)}) %all-reduce.3.cloned.1.call-update) | async-done | bytes 2097168
  291.2 1.0 constant_dynamic-slice_fusion
  292.2 0.9 copy.26
  (5 shorter events, 0.1 us)
Async XLA Ops:
  11.7 81.6 %all-to-all-start = ((s32[128,1,2]{2,1,0:T(1,128)}), s32[128,1,2]{2,1,0:T(1,128)S(1)}, u32[]{:S(2)}, u32[]{:S(2)}) async-start(s32[128,1,2]{2,1,0:T(1,128)} %bitcast.7), calls=%async_computation | async-start | bytes 131072 | tf_op jit(solution)/shard_map/all_to_all | solution.py:49
  93.3 10.3 %copy-start.1 = (bf16[4,1,128,1,128]{4,2,3,1,0:T(8,128)(2,1)S(1)}, bf16[4,1,128,1,128]{4,2,3,1,0:T(8,128)(2,1)}, u32[]{:S(2)}) copy-start(bf16[4,1,128,1,128]{4,2,3,1,0:T(8,128)(2,1)} %param.9) | copy-start | bytes 393220
  93.3 112.6 %all-to-all-start.1 = ((bf16[128,2,128,128]{3,2,1,0:T(8,128)(2,1)}), bf16[128,2,128,128]{3,2,1,0:T(8,128)(2,1)}, u32[]{:S(2)}, u32[]{:S(2)}) async-start(bf16[128,2,128,128]{3,2,1,0:T(8,128)(2,1)} %bitcast.87), calls=%async_computation.1 | async-start | bytes 16777216 | tf_op jit(solution)/shard_map/all_to_all | solution.py:42
  103.6 120.4 %all-gather.2.cloned.1.call-start = ((), (), s32[]{:S(2)}) async-start(), calls=%async_computation.2 | async-start | bytes 2228224 | tf_op jit(solution)/shard_map/all_gather | solution.py:68
  104.4 186.8 %all-reduce.3.cloned.1.call-start = ((), (), s32[]{:S(2)}) async-start(), calls=%async_computation.3 | async-start | bytes 4194304
  205.9 21.8 %copy-start.2 = (u32[128]{0:T(128)S(1)}, u32[128]{0:T(128)}, u32[]{:S(2)}) copy-start(u32[128]{0:T(128)} %constant.106) | copy-start | bytes 1540
  213.8 79.3 %copy-start = (bf16[1,8,128,128]{3,2,1,0:T(8,128)(2,1)}, bf16[1,8,128,128]{3,2,1,0:T(8,128)(2,1)S(1)}, u32[]{:S(2)}) copy-start(bf16[1,8,128,128]{3,2,1,0:T(8,128)(2,1)S(1)} %copy.33) | copy-start | bytes 786436
Sparse Core Ops, SparseCore 0:
  107.1 116.8 all-gather.1
  227.8 63.3 all-reduce.2
where the time goes:
time: 302 us; the launch traced here: 300 us
  waiting for transfers between devices  172 us (57%)
  local copies, waits for them, and re-layouts  62.6 us (21%)
  matrix products  25.2 us (8%)
  starting transfers between devices  22 us (7%)
  between operations  15.4 us (5%)
    all_to_all x1, waiting for transfers between devices, shards(): lax.all_to_all(outgoing.reshape(devices, capacity, block_size, block_size...  99.8 us
    unnamed x3, waiting for transfers between devices  62.3 us
    scatter x1, local copies, waits for them, and re-layouts, shards(): jnp.zeros((devices * capacity, block_size, block_size), jnp.bfloat16)  35.5 us
    gather x1, local copies, waits for them, and re-layouts, shards(): picked = dense_blocks[pair_rows, pair_cols].astype(jnp.bfloat16)  15.5 us
    dot_general x1, matrix products, shards(): jnp.einsum('aig,bjg->abij', weighted, orbitals[0], preferred_element_type...  13.7 us
    all_to_all x1, starting transfers between devices, shards(): lax.all_to_all(positions.reshape(devices, capacity), ('dom', 'col'), spli...  11.5 us
    all_to_all x1, starting transfers between devices, shards(): lax.all_to_all(outgoing.reshape(devices, capacity, block_size, block_size...  10.3 us
    all_gather x1, waiting for transfers between devices, shards(): shard_rows = lax.all_gather(coefficients, 'col', axis=3, tiled=True)  9.98 us
  transfers between devices with their start and end apart: 4, of which 3 were waited for; matrix products, arithmetic and copies ran while one was open for 27% of the time, Pallas kernels for 0%

commit v1 on v0

v1 whole, which is shorter than its diff:
```python
import functools

import jax
import jax.numpy as jnp
from jax import lax
from jax.experimental import pallas as pl
from jax.experimental.pallas import tpu as pltpu
from jax.sharding import PartitionSpec as P

F32 = jnp.float32
BF16 = jnp.bfloat16
AXES = ("dom", "col")
NB = 128
LOC = 16
NBLK = 32
NDOM = 8
NCOL = 16
NDEV = NDOM * NCOL
ROWS = NB + 8
HELD = 4 * NB + 16
CHUNK = 8
VMEM = pl.BlockSpec(memory_space=pltpu.VMEM)
SMEM = pl.BlockSpec(memory_space=pltpu.SMEM)


def upper(strict):
    row = lax.broadcasted_iota(jnp.int32, (NB, NB), 0)
    col = lax.broadcasted_iota(jnp.int32, (NB, NB), 1)
    return row < col if strict else row <= col


def message_kernel(start_ref, pairs_ref, potential_ref, orbitals_ref, out_ref, held, weighted, diagonal, sems):
    step_rows = 2 * NB
    steps = LOC // 2
    copies = [
        pltpu.make_async_copy(
            orbitals_ref.at[pl.ds(k * step_rows, step_rows)], held.at[pl.ds(k * step_rows, step_rows)], sems.at[k]
        )
        for k in range(steps)
    ]
    for copy in copies:
        copy.start()
    start = start_ref[0]
    codes = pairs_ref[0:1, :] * LOC + pairs_ref[1:2, :]
    scale = potential_ref[...]
    tail_row = lax.broadcasted_iota(jnp.int32, (8, NB), 0)
    tail = jnp.where(tail_row == 1, start.astype(F32), 0.0)
    eye = upper(False) & ~upper(True)

    def send(row, col, block, last_rows):
        target = lax.rem(row, NDOM) * NCOL + lax.rem(col, NCOL)
        out_ref[target, 0:NB, :] = block.astype(BF16)
        out_ref[target, NB:ROWS, :] = last_rows.astype(BF16)

    for right in range(steps):
        copies[right].wait()
        right_rows = pl.ds(right * step_rows, step_rows)
        right_side = held[right_rows, :]
        weighted[right_rows, :] = (right_side.astype(F32) * scale).astype(BF16)
        for left in range(right + 1):
            tile = lax.dot_general(
                weighted[pl.ds(left * step_rows, step_rows), :],
                right_side,
                (((1,), (1,)), ((), ())),
                preferred_element_type=F32,
            )
            for a in (2 * left, 2 * left + 1):
                for b in (2 * right, 2 * right + 1):
                    block = tile[(a % 2) * NB : (a % 2 + 1) * NB, (b % 2) * NB : (b % 2 + 1) * NB]
                    gap = b - a
                    if gap < 0:
                        continue
                    if gap == 0 and a < LOC // 2:
                        diagonal[a] = block
                    elif gap == 0:
                        low = a - LOC // 2
                        packed = jnp.where(upper(False), diagonal[low], block)
                        extra = jnp.sum(jnp.where(eye, block, 0.0), axis=0, keepdims=True)
                        send(start + low, start + low, packed, jnp.where(tail_row == 0, extra, tail))
                    elif gap < LOC // 2:
                        send(start + a, start + b, block, tail)
                    elif gap == LOC // 2:
                        send(start + b, start + b, block, tail)
                    else:
                        listed = jnp.max(jnp.where(codes == a * LOC + b, 1.0, 0.0), axis=1, keepdims=True)
                        send(start + b, start + a, block * listed, tail)


def messages(domain_start, margin_pairs, potential, orbitals):
    rows = LOC * NB
    grid_points = orbitals.shape[-1]
    return pl.pallas_call(
        message_kernel,
        out_shape=jax.ShapeDtypeStruct((NDEV, ROWS, NB), BF16),
        in_specs=[SMEM, VMEM, VMEM, pl.BlockSpec(memory_space=pl.ANY)],
        out_specs=VMEM,
        scratch_shapes=[
            pltpu.VMEM((rows, grid_points), BF16),
            pltpu.VMEM((rows, grid_points), BF16),
            pltpu.VMEM((LOC // 2, NB, NB), F32),
            pltpu.SemaphoreType.DMA((LOC // 2,)),
        ],
        compiler_params=pltpu.CompilerParams(vmem_limit_bytes=40 << 20),
        cost_estimate=pl.CostEstimate(flops=5_000_000_000, bytes_accessed=9_000_000, transcendentals=0),
        name="blocks",
    )(domain_start, margin_pairs, potential, orbitals.reshape(rows, grid_points))


def wrap(value, size):
    return lax.rem(value + 2 * size, size)


def place():
    dom, col = lax.axis_index("dom"), lax.axis_index("col")
    return dom, col, wrap(col - dom, NDOM)


def sum_kernel(in_ref, direct_ref, turned_ref, total, extra_total):
    step = pl.program_id(0)
    _, col, kind = place()
    near = jnp.where(kind == 0, LOC // 2, kind)

    @pl.when(step == 0)
    def _():
        total[...] = jnp.zeros_like(total)
        extra_total[...] = jnp.zeros_like(extra_total)

    ends = in_ref[:, NB:ROWS, :].astype(F32)
    start = ends[:, 1, :].astype(jnp.int32)
    position = (col + NBLK - start) & (LOC - 1)
    half = ((start + position) & (NBLK - 1)) // LOC
    key = jnp.where(position >= near, 0, 2) + half
    chosen = [jnp.where(key == k, 1.0, 0.0) for k in range(4)]
    for k in (2, 3):
        extra_total[k - 2 : k - 1, :] += jnp.sum(ends[:, 0, :] * chosen[k], axis=0, keepdims=True)
    for tile in range(NB // 16):
        rows = pl.ds(tile * 16, 16)
        sums = [total[k, rows, :] for k in range(4)]
        for m in range(CHUNK):
            value = in_ref[m, rows, :].astype(F32)
            sums = [sums[k] + value * chosen[k][m : m + 1, :] for k in range(4)]
        for k in range(4):
            total[k, rows, :] = sums[k]

    @pl.when(step == NDEV // CHUNK - 1)
    def _():
        row = lax.broadcasted_iota(jnp.int32, (16, NB), 0)
        extra = jnp.where(row == 0, extra_total[0:1, :], jnp.where(row == 1, extra_total[1:2, :], 0.0)).astype(BF16)
        for k in range(4):
            plain = total[k]
            flipped = plain.T
            rows = pl.ds(k * NB, NB)
            direct_ref[rows, :] = (flipped if k < 2 else plain).astype(BF16)
            turned_ref[rows, :] = (plain if k < 2 else flipped).astype(BF16)
        direct_ref[4 * NB : HELD, :] = extra
        turned_ref[4 * NB : HELD, :] = extra


def sums(incoming):
    shape = jax.ShapeDtypeStruct((HELD, NB), BF16)
    return pl.pallas_call(
        sum_kernel,
        out_shape=(shape, shape),
        grid=(NDEV // CHUNK,),
        in_specs=[pl.BlockSpec((CHUNK, ROWS, NB), lambda i: (i, 0, 0))],
        out_specs=(pl.BlockSpec((HELD, NB), lambda i: (0, 0)),) * 2,
        scratch_shapes=[pltpu.VMEM((4, NB, NB), F32), pltpu.VMEM((2, NB), F32)],
        cost_estimate=pl.CostEstimate(flops=20_000_000, bytes_accessed=4_700_000, transcendentals=0),
        name="sums",
    )(incoming)


def diagonal_block(col, half, direct, turned):
    other = lax.rem(col + LOC * half + NBLK - NDOM, NBLK) // LOC
    first = direct[pl.ds((2 + half) * NB, NB), :].astype(F32)
    second = turned[pl.ds(pl.multiple_of((2 + other) * NB, NB), NB), :].astype(F32)
    ends = turned[4 * NB : HELD, :].astype(F32)
    extra = jnp.where(other == 0, ends[0:1, :], ends[1:2, :])
    above = jnp.where(upper(True), first + second, 0.0)
    eye = upper(False) & ~upper(True)
    return jnp.where(eye, first + extra, above + above.T)


def owned_blocks(dom, col, direct, turned, put):
    kind = wrap(col - dom, NDOM)
    near = jnp.where(kind == 0, LOC // 2, kind)
    other_near = NDOM - kind
    other_col = wrap(col - kind - NDOM, NCOL)
    for half in range(2):
        mine = col + LOC * half
        theirs = other_col + LOC * half
        put(wrap(mine - near, NBLK) // NDOM, half, direct[pl.ds(half * NB, NB), :])
        put(theirs // NDOM, wrap(theirs - other_near, NBLK) // LOC, turned[pl.ds(half * NB, NB), :])

    @pl.when(kind > 0)
    def _():
        for half in range(2):
            mine = col + LOC * half
            theirs = other_col + LOC * half
            rows = pl.ds((2 + half) * NB, NB)
            put(wrap(mine + LOC - kind, NBLK) // NDOM, half, direct[rows, :])
            put(theirs // NDOM, wrap(theirs + NDOM + kind, NBLK) // LOC, turned[rows, :])

    @pl.when(kind == 0)
    def _():
        for half in range(2):
            mine = col + LOC * half
            put(mine // NDOM, half, diagonal_block(col, half, direct, turned).astype(BF16))
            put(wrap(mine + LOC, NBLK) // NDOM, half, jnp.zeros((NB, NB), BF16))


def owned_kernel(direct_ref, turned_ref, out_ref):
    dom, col, _ = place()

    def put(row, half, block):
        out_ref[row, half] = block.astype(F32).T.astype(BF16)

    owned_blocks(dom, col, direct_ref, turned_ref, put)


def owned(direct, turned):
    return pl.pallas_call(
        owned_kernel,
        out_shape=jax.ShapeDtypeStruct((4, 2, NB, NB), BF16),
        in_specs=[VMEM, VMEM],
        out_specs=VMEM,
        cost_estimate=pl.CostEstimate(flops=1_000_000, bytes_accessed=550_000, transcendentals=0),
        name="owned",
    )(direct, turned)


def product_kernel(panel_ref, *refs):
    direct, turned = refs[0:4], refs[4:8]
    mine_ref, other_ref, left = refs[8:11]
    dom, col, _ = place()
    y, core = dom // 2, lax.rem(dom, 2)
    for k in range(4):
        their_y = wrap(y - k, 4)

        def put(row, half, block, their_y=their_y):
            place_of = pl.multiple_of((their_y * 4 + row) * NB, NB)
            left[pl.ds(half * NB, NB) if isinstance(half, int) else pl.ds(pl.multiple_of(half * NB, NB), NB),
                 pl.ds(place_of, NB)] = block

        owned_blocks(2 * their_y + core, col, direct[k], turned[k], put)
    depth = 4 * NB
    for j in range(4):
        part = jnp.zeros((2 * NB, NB), F32)
        for their_y in range(4):
            part = part + jnp.dot(
                left[:, their_y * depth : (their_y + 1) * depth],
                panel_ref[their_y * 4 + j],
                preferred_element_type=F32,
            )
        part = part.reshape(2, NB, NB)

        @pl.when(core == j // 2)
        def _():
            mine_ref[:, j % 2] = part

        @pl.when(core != j // 2)
        def _():
            other_ref[:, j % 2] = part


def product_parts(panel, direct, turned):
    shape = jax.ShapeDtypeStruct((2, 2, NB, NB), F32)
    return pl.pallas_call(
        product_kernel,
        out_shape=(shape, shape),
        in_specs=[VMEM] * 9,
        out_specs=(VMEM, VMEM),
        scratch_shapes=[pltpu.VMEM((2 * NB, 16 * NB), BF16)],
        compiler_params=pltpu.CompilerParams(vmem_limit_bytes=32 << 20),
        cost_estimate=pl.CostEstimate(flops=540_000_000, bytes_accessed=4_000_000, transcendentals=0),
        name="product",
    )(panel, *direct, *turned)


def device(y, core, col):
    return (2 * y + core) * NCOL + col


def partner(dom, col):
    kind = (col - dom) % NDOM
    return (col % NDOM) * NCOL + (col - kind - NDOM) % NCOL


PLACES = [(y, core, col) for y in range(4) for core in range(2) for col in range(NCOL)]


def around(step):
    return [(device(y, core, col), device((y + step) % 4, core, col)) for y, core, col in PLACES]


def from_partner(step):
    return [(partner(2 * y + core, col), device((y + step) % 4, core, col)) for y, core, col in PLACES]


def shards(orbitals, potential, domain_start, margin_pairs, coefficients):
    to_row = [(device(y, core, s), device(s // 4, core, 4 * y + s % 4)) for y, core, s in PLACES]
    rows = lax.ppermute(coefficients.reshape(4 * NB, NB), AXES, to_row)
    panel = lax.all_gather(rows, "col", axis=0, tiled=False)
    outgoing = messages(domain_start, margin_pairs[0], potential, orbitals)
    incoming = lax.all_to_all(outgoing, AXES, split_axis=0, concat_axis=0, tiled=True)
    direct, turned = sums(incoming)
    near = [direct] + [lax.ppermute(direct, AXES, around(k)) for k in (1, 2, 3)]
    far = [lax.ppermute(turned, AXES, from_partner(k)) for k in range(4)]
    potential_blocks = owned(direct, far[0]).reshape(4, 1, 2, 1, NB, NB)
    mine, other = product_parts(panel, near, far)
    swap = [(device(y, core, col), device(y, 1 - core, col)) for y, core, col in PLACES]
    product = mine + lax.ppermute(other, AXES, swap)
    return potential_blocks, jnp.swapaxes(product, 1, 2).reshape(2, 1, NB, 2, NB)


def solution(mesh):
    placed = (
        P(AXES, None, None, None),
        P(AXES, None),
        P(AXES),
        P(AXES, None, None),
        P(None, "dom", None, "col", None),
    )
    return jax.shard_map(
        shards,
        mesh=mesh,
        in_specs=placed,
        out_specs=(P(None, "dom", None, "col", None, None), P(None, "col", None, "dom", None)),
        check_vma=False,
    )
```

time: 302 us -> 157 us (0.52)
  waiting for transfers between devices: 172 us -> 72.8 us
  local copies, waits for them, and re-layouts: 62.6 us -> 9.66 us
  matrix products: 25.2 us -> 0 us
  Pallas kernels: 0 us -> 22.2 us
  starting transfers between devices: 22 us -> 37.4 us
    unnamed x3 -> x1, waiting for transfers between devices: 62.3 us -> 0.02 us
    all_to_all x2 -> x1, waiting for transfers between devices: 99.8 us -> 52.6 us  [shards(): lax.all_to_all(outgoing, AXES, split_axis=0, concat_axis=0, tiled=True)]
    scatter x2 -> x0, local copies, waits for them, and re-layouts: 36.8 us -> none  [the longest x1 35.5 us: shards(): jnp.zeros((devices * capacity, block_size, block_size), jnp.bfloat16)]
    ppermute x0 -> x9, starting transfers between devices: none -> 25.5 us  [the longest x4 17.1 us: shards(): far = [lax.ppermute(turned, AXES, from_partner(k)) for k in range(4)]]
    dot_general x3 -> x0, matrix products: 25.2 us -> none  [the longest x1 13.7 us: shards(): jnp.einsum('aig,bjg->abij', weighted, orbitals[0], preferred_element_type...]
    pallas_call x0 -> x4, Pallas kernels: none -> 22.2 us  [the longest x1 10.6 us: sums(): pl.pallas_call(sum_kernel, out_shape=(shape, shape), grid=(NDEV // CHUNK,...]
    gather x1 -> x0, local copies, waits for them, and re-layouts: 15.5 us -> none  [shards(): picked = dense_blocks[pair_rows, pair_cols].astype(jnp.bfloat16)]
    all_gather x1, waiting for transfers between devices: 9.98 us -> 20.1 us  [shards(): panel = lax.all_gather(rows, 'col', axis=0, tiled=False)]
  transfers between devices with their start and end apart: 4 -> 11, of which waited for: 3 -> 2; matrix products, arithmetic and copies ran while one was open for 27% -> 0% of each run, Pallas kernels for 0% -> 8%
where the time goes in v1:
time: 157 us
  waiting for transfers between devices  72.8 us (46%)
  starting transfers between devices  37.4 us (24%)
  Pallas kernels  22.2 us (14%)
  between operations  14.8 us (9%)
  local copies, waits for them, and re-layouts  9.66 us (6%)
    all_to_all x1, waiting for transfers between devices, shards(): lax.all_to_all(outgoing, AXES, split_axis=0, concat_axis=0, tiled=True)  52.6 us
    all_gather x1, waiting for transfers between devices, shards(): panel = lax.all_gather(rows, 'col', axis=0, tiled=False)  20.1 us
    ppermute x4, starting transfers between devices, shards(): far = [lax.ppermute(turned, AXES, from_partner(k)) for k in range(4)]  17.1 us
    all_to_all x1, starting transfers between devices, shards(): lax.all_to_all(outgoing, AXES, split_axis=0, concat_axis=0, tiled=True)  11.9 us
    pallas_call x1, Pallas kernels, sums(): pl.pallas_call(sum_kernel, out_shape=(shape, shape), grid=(NDEV // CHUNK,...  10.6 us
    unnamed x19, local copies, waits for them, and re-layouts  9.66 us
    pallas_call x1, Pallas kernels, messages(): pl.pallas_call(message_kernel, out_shape=jax.ShapeDtypeStruct((NDEV, ROWS...  7.53 us
    ppermute x3, starting transfers between devices, shards(): near = [direct] + [lax.ppermute(direct, AXES, around(k)) for k in (1, 2, 3)]  5.85 us
  transfers between devices with their start and end apart: 11, of which 2 were waited for; matrix products, arithmetic and copies ran while one was open for 0% of the time, Pallas kernels for 8%

profile of v1, /device:TPU:1, one launch (start us, length us, event | category | flops | bytes accessed | tf_op | source)
XLA Modules:
  0.0 156.8 jit_solution(4857455879161972595)
XLA Ops:
  7.8 2.2 %copy-done.4 = bf16[1,16,128,1024]{3,2,1,0:T(8,128)(2,1)S(1)} copy-done((bf16[1,16,128,1024]{3,2,1,0:T(8,128)(2,1)S(1)}, bf16[1,16,128,1024]{3,2,1,0:T(8,128)(2,1)}, u32[]{:S(2)}) %copy-start.4) | copy-done | bytes 4194328
  10.0 0.7 copy-done.5
  10.7 0.7 copy-done.6
  11.4 7.5 %blocks.1 = bf16[128,136,128]{2,1,0:T(8,128)(2,1)S(1)} custom-call(s32[1]{0:T(128)S(6)} %copy.9.start_ref, s32[2,228]{1,0:T(2,128)S(1)} %bitcast.13, f32[1,1024]{1,0:T(1,128)S(1)} %copy-done.5, bf16[2048,1024]{1,0:T(8,128)(2,1)S(1)} %bitcast.12), custom_call_target="tpu_custom_call" | custom-call | flops 5000000000 | bytes 9000000 | tf_op jit(solution)/shard_map/blocks/pallas_call | solution.py:92
  18.9 2.1 %copy-done = bf16[128,136,128]{2,1,0:T(8,128)(2,1)} copy-done((bf16[128,136,128]{2,1,0:T(8,128)(2,1)}, bf16[128,136,128]{2,1,0:T(8,128)(2,1)S(1)}, u32[]{:S(2)}) %copy-start) | copy-done | bytes 4456472
  21.0 11.9 %all-to-all-start = ((bf16[128,136,128]{2,1,0:T(8,128)(2,1)}), bf16[128,136,128]{2,1,0:T(8,128)(2,1)}, u32[]{:S(2)}, u32[]{:S(2)}) async-start(bf16[128,136,128]{2,1,0:T(8,128)(2,1)} %copy-done), calls=%async_computation | async-start | bytes 8912896 | tf_op jit(solution)/shard_map/all_to_all | solution.py:305
  32.9 0.0 all-gather.3.cloned.1.call-start
  33.0 0.7 collective-permute-start.1
  33.6 0.0 collective-permute-done.1
  33.7 0.6 copy-done.7
  34.3 0.0 all-gather.3.cloned.1.call-update
  34.3 52.6 %all-to-all-done.in_ref = bf16[128,136,128]{2,1,0:T(8,128)(2,1)} async-done(((bf16[128,136,128]{2,1,0:T(8,128)(2,1)}), bf16[128,136,128]{2,1,0:T(8,128)(2,1)}, u32[]{:S(2)}, u32[]{:S(2)}) %all-to-all-start) | async-done | bytes 4456480 | tf_op jit(solution)/shard_map/all_to_all | solution.py:305
  87.0 10.6 %sums.1 = (bf16[528,128]{1,0:T(8,128)(2,1)}, bf16[528,128]{1,0:T(8,128)(2,1)}) custom-call(bf16[128,136,128]{2,1,0:T(8,128)(2,1)} %all-to-all-done.in_ref), custom_call_target="tpu_custom_call" | custom-call | flops 20000000 | bytes 4700000 | tf_op jit(solution)/shard_map/sums/pallas_call | solution.py:161
  97.6 6.7 %collective-permute-start = (bf16[528,128]{1,0:T(8,128)(2,1)}, bf16[528,128]{1,0:T(8,128)(2,1)S(1)}, u32[]{:S(2)}, u32[]{:S(2)}) collective-permute-start(bf16[528,128]{1,0:T(8,128)(2,1)} %get-tuple-element.7), channel_id=1, source_target_pairs={{8,0},{24,1},{40,2},{56,3},{72,4},{88,5},{104,6},{120,7},{0,8},{16... | collective-permute-start | bytes 405512 | tf_op jit(solution)/shard_map/ppermute | solution.py:308
  104.3 2.4 %collective-permute-start.2 = (bf16[528,128]{1,0:T(8,128)(2,1)}, bf16[528,128]{1,0:T(8,128)(2,1)S(1)}, u32[]{:S(2)}, u32[]{:S(2)}) collective-permute-start(bf16[528,128]{1,0:T(8,128)(2,1)} %get-tuple-element.6.direct_ref.refs_0_), channel_id=1, source_target_pairs={{0,32},{1,33},{2,34},{3,35},{4,36},{5,37},{6,38},{7,39},{8,40},{9,... | collective-permute-start | bytes 405512 | tf_op jit(solution)/shard_map/ppermute | solution.py:307
  106.8 3.4 %collective-permute-start.3 = (bf16[528,128]{1,0:T(8,128)(2,1)}, bf16[528,128]{1,0:T(8,128)(2,1)S(1)}, u32[]{:S(2)}, u32[]{:S(2)}) collective-permute-start(bf16[528,128]{1,0:T(8,128)(2,1)} %get-tuple-element.6.direct_ref.refs_0_), channel_id=1, source_target_pairs={{0,64},{1,65},{2,66},{3,67},{4,68},{5,69},{6,70},{7,71},{8,72},{9,... | collective-permute-start | bytes 405512 | tf_op jit(solution)/shard_map/ppermute | solution.py:307
  110.2 0.0 collective-permute-start.4
  110.2 0.5 collective-permute-start.5
  110.7 0.0 collective-permute-done.turned_ref.refs_4_
  110.7 3.9 %collective-permute-start.6 = (bf16[528,128]{1,0:T(8,128)(2,1)}, bf16[528,128]{1,0:T(8,128)(2,1)S(1)}, u32[]{:S(2)}, u32[]{:S(2)}) collective-permute-start(bf16[528,128]{1,0:T(8,128)(2,1)} %get-tuple-element.7), channel_id=1, source_target_pairs={{8,64},{24,65},{40,66},{56,67},{72,68},{88,69},{104,70},{120,71},{... | collective-permute-start | bytes 405512 | tf_op jit(solution)/shard_map/ppermute | solution.py:308
  114.6 5.9 %collective-permute-start.7 = (bf16[528,128]{1,0:T(8,128)(2,1)}, bf16[528,128]{1,0:T(8,128)(2,1)S(1)}, u32[]{:S(2)}, u32[]{:S(2)}) collective-permute-start(bf16[528,128]{1,0:T(8,128)(2,1)} %get-tuple-element.7), channel_id=1, source_target_pairs={{8,96},{24,97},{40,98},{56,99},{72,100},{88,101},{104,102},{120,10... | collective-permute-start | bytes 405512 | tf_op jit(solution)/shard_map/ppermute | solution.py:308
  120.5 20.1 %all-gather.3.cloned.1.call-done = bf16[8192,128]{1,0:T(8,128)(2,1)} async-done(((bf16[512,128]{1,0:T(8,128)(2,1)}), bf16[8192,128]{1,0:T(8,128)(2,1)}) %all-gather.3.cloned.1.call-update) | async-done | bytes 2097168 | tf_op jit(solution)/shard_map/all_gather | solution.py:303
  140.6 0.0 collective-permute-done.3.refs_2_
  140.6 0.0 collective-permute-done.4.refs_3_
  140.6 0.0 collective-permute-done.5.refs_5_
  140.6 0.0 collective-permute-done.7.refs_7_
  140.6 1.6 %copy-done.1 = bf16[8192,128]{1,0:T(8,128)(2,1)S(1)} copy-done((bf16[8192,128]{1,0:T(8,128)(2,1)S(1)}, bf16[8192,128]{1,0:T(8,128)(2,1)}, u32[]{:S(2)}) %copy-start.1) | copy-done | bytes 2097176
  142.2 0.9 copy-done.2
  143.1 2.1 %product.1 = (f32[2,2,128,128]{3,2,1,0:T(8,128)S(1)}, f32[2,2,128,128]{3,2,1,0:T(8,128)S(1)}) custom-call(bf16[16,512,128]{2,1,0:T(8,128)(2,1)S(1)} %bitcast.11, bf16[528,128]{1,0:T(8,128)(2,1)S(1)} %copy-done.2, bf16[528,128]{1,0:T(8,128)(2,1)S(1)} %collective-permute-done.2.refs_1_, bf16[528,128]{1,0:T(8,128)(2,1)S(1)} %collective-permute-done.3.refs_2_, ...), custom_call_target="tpu_custom_call" | custom-call | flops 540000000 | bytes 4000000 | tf_op jit(solution)/shard_map/product/pallas_call | solution.py:268
  145.3 1.9 %collective-permute-start.8 = (f32[2,2,128,128]{3,2,1,0:T(8,128)S(1)}, f32[2,2,128,128]{3,2,1,0:T(8,128)S(1)}, u32[]{:S(2)}, u32[]{:S(2)}) collective-permute-start(f32[2,2,128,128]{3,2,1,0:T(8,128)S(1)} %get-tuple-element.9), channel_id=1, source_target_pairs={{0,16},{1,17},{2,18},{3,19},{4,20},{5,21},{6,22},{7,23},{8,24},{9,... | collective-permute-start | bytes 786440 | tf_op jit(solution)/shard_map/ppermute | solution.py:312
  147.2 1.9 %owned.1 = bf16[4,2,128,128]{3,2,1,0:T(8,128)(2,1)} custom-call(bf16[528,128]{1,0:T(8,128)(2,1)} %get-tuple-element.6.direct_ref.refs_0_, bf16[528,128]{1,0:T(8,128)(2,1)} %copy-done.3), custom_call_target="tpu_custom_call" | custom-call | flops 1000000 | bytes 550000 | tf_op jit(solution)/shard_map/owned/pallas_call | solution.py:222
  149.1 0.9 copy.8
  (15 shorter events, 0.1 us)
Async XLA Ops:
  7.8 2.2 %copy-start.4 = (bf16[1,16,128,1024]{3,2,1,0:T(8,128)(2,1)S(1)}, bf16[1,16,128,1024]{3,2,1,0:T(8,128)(2,1)}, u32[]{:S(2)}) copy-start(bf16[1,16,128,1024]{3,2,1,0:T(8,128)(2,1)} %param.5) | copy-start | bytes 12582916
  10.0 0.7 copy-start.5
  10.7 0.7 copy-start.6
  18.9 2.1 %copy-start = (bf16[128,136,128]{2,1,0:T(8,128)(2,1)}, bf16[128,136,128]{2,1,0:T(8,128)(2,1)S(1)}, u32[]{:S(2)}) copy-start(bf16[128,136,128]{2,1,0:T(8,128)(2,1)S(1)} %blocks.1) | copy-start | bytes 13369348
  21.0 12.0 %copy-start.8 = (bf16[4,1,128,1,128]{4,2,3,1,0:T(8,128)(2,1)S(1)}, bf16[4,1,128,1,128]{4,2,3,1,0:T(8,128)(2,1)}, u32[]{:S(2)}) copy-start(bf16[4,1,128,1,128]{4,2,3,1,0:T(8,128)(2,1)} %param.9) | copy-start | bytes 393220
  21.0 66.0 %all-to-all-start = ((bf16[128,136,128]{2,1,0:T(8,128)(2,1)}), bf16[128,136,128]{2,1,0:T(8,128)(2,1)}, u32[]{:S(2)}, u32[]{:S(2)}) async-start(bf16[128,136,128]{2,1,0:T(8,128)(2,1)} %copy-done), calls=%async_computation | async-start | bytes 8912896 | tf_op jit(solution)/shard_map/all_to_all | solution.py:305
  32.9 107.7 %all-gather.3.cloned.1.call-start = ((), (), s32[]{:S(2)}) async-start(), calls=%async_computation.1 | async-start | bytes 2228224 | tf_op jit(solution)/shard_map/all_gather | solution.py:303
  33.0 0.7 collective-permute-start.1
  33.6 0.6 copy-start.7
  97.6 13.1 %collective-permute-start = (bf16[528,128]{1,0:T(8,128)(2,1)}, bf16[528,128]{1,0:T(8,128)(2,1)S(1)}, u32[]{:S(2)}, u32[]{:S(2)}) collective-permute-start(bf16[528,128]{1,0:T(8,128)(2,1)} %get-tuple-element.7), channel_id=1, source_target_pairs={{8,0},{24,1},{40,2},{56,3},{72,4},{88,5},{104,6},{120,7},{0,8},{16... | collective-permute-start | bytes 405512 | tf_op jit(solution)/shard_map/ppermute | solution.py:308
  104.3 10.3 %collective-permute-start.2 = (bf16[528,128]{1,0:T(8,128)(2,1)}, bf16[528,128]{1,0:T(8,128)(2,1)S(1)}, u32[]{:S(2)}, u32[]{:S(2)}) collective-permute-start(bf16[528,128]{1,0:T(8,128)(2,1)} %get-tuple-element.6.direct_ref.refs_0_), channel_id=1, source_target_pairs={{0,32},{1,33},{2,34},{3,35},{4,36},{5,37},{6,38},{7,39},{8,40},{9,... | collective-permute-start | bytes 405512 | tf_op jit(solution)/shard_map/ppermute | solution.py:307
  106.8 33.8 %collective-permute-start.3 = (bf16[528,128]{1,0:T(8,128)(2,1)}, bf16[528,128]{1,0:T(8,128)(2,1)S(1)}, u32[]{:S(2)}, u32[]{:S(2)}) collective-permute-start(bf16[528,128]{1,0:T(8,128)(2,1)} %get-tuple-element.6.direct_ref.refs_0_), channel_id=1, source_target_pairs={{0,64},{1,65},{2,66},{3,67},{4,68},{5,69},{6,70},{7,71},{8,72},{9,... | collective-permute-start | bytes 405512 | tf_op jit(solution)/shard_map/ppermute | solution.py:307
  110.2 30.4 %collective-permute-start.4 = (bf16[528,128]{1,0:T(8,128)(2,1)}, bf16[528,128]{1,0:T(8,128)(2,1)S(1)}, u32[]{:S(2)}, u32[]{:S(2)}) collective-permute-start(bf16[528,128]{1,0:T(8,128)(2,1)} %get-tuple-element.6.direct_ref.refs_0_), channel_id=1, source_target_pairs={{0,96},{1,97},{2,98},{3,99},{4,100},{5,101},{6,102},{7,103},{8,104... | collective-permute-start | bytes 405512 | tf_op jit(solution)/shard_map/ppermute | solution.py:307
  110.2 30.4 %collective-permute-start.5 = (bf16[528,128]{1,0:T(8,128)(2,1)}, bf16[528,128]{1,0:T(8,128)(2,1)S(1)}, u32[]{:S(2)}, u32[]{:S(2)}) collective-permute-start(bf16[528,128]{1,0:T(8,128)(2,1)} %get-tuple-element.7), channel_id=1, source_target_pairs={{8,32},{24,33},{40,34},{56,35},{72,36},{88,37},{104,38},{120,39},{... | collective-permute-start | bytes 405512 | tf_op jit(solution)/shard_map/ppermute | solution.py:308
  110.7 36.4 %copy-start.3 = (bf16[528,128]{1,0:T(8,128)(2,1)}, bf16[528,128]{1,0:T(8,128)(2,1)S(1)}, u32[]{:S(2)}) copy-start(bf16[528,128]{1,0:T(8,128)(2,1)S(1)} %collective-permute-done.turned_ref.refs_4_) | copy-start | bytes 405508
  110.7 29.9 %collective-permute-start.6 = (bf16[528,128]{1,0:T(8,128)(2,1)}, bf16[528,128]{1,0:T(8,128)(2,1)S(1)}, u32[]{:S(2)}, u32[]{:S(2)}) collective-permute-start(bf16[528,128]{1,0:T(8,128)(2,1)} %get-tuple-element.7), channel_id=1, source_target_pairs={{8,64},{24,65},{40,66},{56,67},{72,68},{88,69},{104,70},{120,71},{... | collective-permute-start | bytes 405512 | tf_op jit(solution)/shard_map/ppermute | solution.py:308
  114.6 26.0 %collective-permute-start.7 = (bf16[528,128]{1,0:T(8,128)(2,1)}, bf16[528,128]{1,0:T(8,128)(2,1)S(1)}, u32[]{:S(2)}, u32[]{:S(2)}) collective-permute-start(bf16[528,128]{1,0:T(8,128)(2,1)} %get-tuple-element.7), channel_id=1, source_target_pairs={{8,96},{24,97},{40,98},{56,99},{72,100},{88,101},{104,102},{120,10... | collective-permute-start | bytes 405512 | tf_op jit(solution)/shard_map/ppermute | solution.py:308
  140.6 1.6 %copy-start.1 = (bf16[8192,128]{1,0:T(8,128)(2,1)S(1)}, bf16[8192,128]{1,0:T(8,128)(2,1)}, u32[]{:S(2)}) copy-start(bf16[8192,128]{1,0:T(8,128)(2,1)} %all-gather.3.cloned.1.call-done) | copy-start | bytes 6291460
  142.2 0.9 copy-start.2
  145.3 3.8 %collective-permute-start.8 = (f32[2,2,128,128]{3,2,1,0:T(8,128)S(1)}, f32[2,2,128,128]{3,2,1,0:T(8,128)S(1)}, u32[]{:S(2)}, u32[]{:S(2)}) collective-permute-start(f32[2,2,128,128]{3,2,1,0:T(8,128)S(1)} %get-tuple-element.9), channel_id=1, source_target_pairs={{0,16},{1,17},{2,18},{3,19},{4,20},{5,21},{6,22},{7,23},{8,24},{9,... | collective-permute-start | bytes 786440 | tf_op jit(solution)/shard_map/ppermute | solution.py:312
Sparse Core Ops, SparseCore 0:
  35.9 104.6 all-gather.2

commit v2 on v1

v2 whole, which is shorter than its diff:
```python
import functools

import jax
import jax.numpy as jnp
from jax import lax
from jax.experimental import pallas as pl
from jax.experimental.pallas import tpu as pltpu
from jax.sharding import PartitionSpec as P

F32 = jnp.float32
BF16 = jnp.bfloat16
AXES = ("dom", "col")
NB = 128
LOC = 16
NBLK = 32
NDOM = 8
NCOL = 16
NDEV = NDOM * NCOL
HELD = 4 * NB
ROWS = NB + 8
CHUNK = 64
TILE = 16
VMEM = pl.BlockSpec(memory_space=pltpu.VMEM)
HBM = pl.BlockSpec(memory_space=pltpu.HBM)
SMEM = pl.BlockSpec(memory_space=pltpu.SMEM)


def upper(strict):
    row = lax.broadcasted_iota(jnp.int32, (NB, NB), 0)
    col = lax.broadcasted_iota(jnp.int32, (NB, NB), 1)
    return row < col if strict else row <= col


def home(kind, col):
    return kind ^ (col & 1)


def message_kernel(
    start_ref, pairs_ref, potential_ref, orbitals_ref, out_ref, held, weighted, diagonal, pairs, potential, sems
):
    step_rows = 2 * NB
    steps = LOC // 2
    small = [
        pltpu.make_async_copy(pairs_ref, pairs, sems.at[steps]),
        pltpu.make_async_copy(potential_ref, potential, sems.at[steps + 1]),
    ]
    copies = [
        pltpu.make_async_copy(
            orbitals_ref.at[pl.ds(k * step_rows, step_rows)], held.at[pl.ds(k * step_rows, step_rows)], sems.at[k]
        )
        for k in range(steps)
    ]
    for copy in small + copies:
        copy.start()
    start = start_ref[0]
    tail_row = lax.broadcasted_iota(jnp.int32, (8, NB), 0)
    tail = jnp.where(tail_row == 1, start.astype(F32), 0.0)
    eye = upper(False) & ~upper(True)
    for copy in small:
        copy.wait()
    codes = pairs[0:1, :] * LOC + pairs[1:2, :]
    scale = potential[...]

    def send(kind, col, block, last_rows):
        col = lax.rem(col, NCOL)
        target = home(kind, col) * NCOL + col
        if block is not None:
            out_ref[target, 0:NB, :] = block.astype(BF16)
        if last_rows is not None:
            out_ref[target, NB:ROWS, :] = last_rows.astype(BF16)

    for right in range(steps):
        copies[right].wait()
        right_rows = pl.ds(right * step_rows, step_rows)
        right_side = held[right_rows, :]
        weighted[right_rows, :] = (right_side.astype(F32) * scale).astype(BF16)
        for left in range(right + 1):
            tile = lax.dot_general(
                weighted[pl.ds(left * step_rows, step_rows), :],
                right_side,
                (((1,), (1,)), ((), ())),
                preferred_element_type=F32,
            )
            for a in (2 * left, 2 * left + 1):
                for b in (2 * right, 2 * right + 1):
                    block = tile[(a % 2) * NB : (a % 2 + 1) * NB, (b % 2) * NB : (b % 2 + 1) * NB]
                    gap = b - a
                    if gap < 0:
                        continue
                    if gap == 0 and a < LOC // 2:
                        diagonal[a] = block
                    elif gap == 0:
                        low = a - LOC // 2
                        send(0, start + low, jnp.where(upper(False), diagonal[low], block), tail)
                        extra = jnp.sum(jnp.where(eye, block, 0.0), axis=0, keepdims=True)
                        send(0, start + a, None, jnp.where(tail_row == 0, extra, tail))
                    elif gap < LOC // 2:
                        send(gap, start + b, block, tail)
                    elif gap == LOC // 2:
                        send(0, start + b, block, None)
                    else:
                        listed = jnp.max(jnp.where(codes == a * LOC + b, 1.0, 0.0), axis=1, keepdims=True)
                        send(LOC - gap, start + a, block * listed, tail)


def in_hbm(value):
    return pltpu.with_memory_space_constraint(value, pltpu.HBM)


def messages(domain_start, margin_pairs, potential, orbitals):
    rows = LOC * NB
    grid_points = orbitals.shape[-1]
    return pl.pallas_call(
        message_kernel,
        out_shape=pltpu.HBM((NDEV, ROWS, NB), BF16),
        in_specs=[SMEM, HBM, HBM, HBM],
        out_specs=VMEM,
        scratch_shapes=[
            pltpu.VMEM((rows, grid_points), BF16),
            pltpu.VMEM((rows, grid_points), BF16),
            pltpu.VMEM((LOC // 2, NB, NB), F32),
            pltpu.VMEM(margin_pairs.shape, jnp.int32),
            pltpu.VMEM(potential.shape, F32),
            pltpu.SemaphoreType.DMA((LOC // 2 + 2,)),
        ],
        compiler_params=pltpu.CompilerParams(vmem_limit_bytes=40 << 20),
        cost_estimate=pl.CostEstimate(flops=5_000_000_000, bytes_accessed=9_000_000, transcendentals=0),
        name="blocks",
    )(domain_start, in_hbm(margin_pairs), in_hbm(potential), in_hbm(orbitals.reshape(rows, grid_points)))


def wrap(value, size):
    return lax.rem(value + 2 * size, size)


def place():
    dom, col = lax.axis_index("dom"), lax.axis_index("col")
    return dom, col, home(dom, col)


def sum_kernel(in_ref, direct_ref, turned_ref, total, extra_total):
    step = pl.program_id(0)
    _, col, kind = place()
    near = jnp.where(kind == 0, LOC // 2, kind)

    @pl.when(step == 0)
    def _():
        total[...] = jnp.zeros_like(total)
        extra_total[...] = jnp.zeros_like(extra_total)

    ends = in_ref[:, NB:ROWS, :].astype(F32)
    start = ends[:, 1, :].astype(jnp.int32)
    position = (col + NBLK - start) & (LOC - 1)
    half = ((start + position) & (NBLK - 1)) // LOC
    key = jnp.where(position >= near, 0, 2) + half
    for k in range(2):
        extra_total[k : k + 1, :] += jnp.sum(jnp.where(key == k, ends[:, 0, :], 0.0), axis=0, keepdims=True)
    depth = CHUNK * TILE
    sublane = lax.broadcasted_iota(jnp.int32, (CHUNK, depth), 0)
    lane = lax.broadcasted_iota(jnp.int32, (CHUNK, depth), 1)
    keys = jnp.concatenate([key] * (depth // NB), axis=1)
    lane_key = jnp.sum(jnp.where(sublane == lane // TILE, keys, 0), axis=0, keepdims=True)
    row = lax.broadcasted_iota(jnp.int32, (4 * TILE, depth), 0)
    lane = lax.broadcasted_iota(jnp.int32, (4 * TILE, depth), 1)
    chosen = jnp.where((row // TILE == lane_key) & ((row & (TILE - 1)) == (lane & (TILE - 1))), 1.0, 0.0).astype(BF16)
    for pair in range(NB // TILE // 2):
        first = pair * 2 * TILE
        sides = [in_ref[:, first + t * TILE : first + (t + 1) * TILE, :].reshape(depth, NB) for t in range(2)]
        total[:, pair * 2 * NB : (pair + 1) * 2 * NB] += jnp.dot(
            chosen, jnp.concatenate(sides, axis=1), preferred_element_type=F32
        )

    @pl.when(step == NDEV // CHUNK - 1)
    def _():
        eye = upper(False) & ~upper(True)
        for k in range(4):
            plain = jnp.concatenate(
                [total[k * TILE : (k + 1) * TILE, t * NB : (t + 1) * NB] for t in range(NB // TILE)], axis=0
            )
            if k >= 2:
                plain = plain + jnp.where(eye, extra_total[k - 2 : k - 1, :], 0.0)
            flipped = plain.T
            rows = pl.ds(k * NB, NB)
            direct_ref[rows, :] = (flipped if k < 2 else plain).astype(BF16)
            turned_ref[rows, :] = (plain if k < 2 else flipped).astype(BF16)


def sums(incoming):
    shape = jax.ShapeDtypeStruct((HELD, NB), BF16)
    return pl.pallas_call(
        sum_kernel,
        out_shape=(shape, shape),
        grid=(NDEV // CHUNK,),
        in_specs=[pl.BlockSpec((CHUNK, ROWS, NB), lambda i: (i, 0, 0))],
        out_specs=(pl.BlockSpec((HELD, NB), lambda i: (0, 0)),) * 2,
        scratch_shapes=[pltpu.VMEM((4 * TILE, NB // TILE * NB), F32), pltpu.VMEM((2, NB), F32)],
        cost_estimate=pl.CostEstimate(flops=300_000_000, bytes_accessed=4_700_000, transcendentals=0),
        name="sums",
    )(incoming)


def diagonal_block(col, half, direct, turned):
    other = lax.rem(col + LOC * half + NBLK - NDOM, NBLK) // LOC
    first = direct[pl.ds((2 + half) * NB, NB), :].astype(F32)
    second = turned[pl.ds(pl.multiple_of((2 + other) * NB, NB), NB), :].astype(F32)
    above = jnp.where(upper(True), first + second, 0.0)
    eye = upper(False) & ~upper(True)
    return jnp.where(eye, first, above + above.T)


def column_blocks(kind, col, direct, turned, put):
    near = jnp.where(kind == 0, LOC // 2, kind)
    other_col = lax.rem(col + near, NCOL)
    for half in range(2):
        mine = col + LOC * half
        theirs = other_col + LOC * half
        put(wrap(mine - near, NBLK), half, direct[pl.ds(half * NB, NB), :])
        put(theirs, wrap(theirs - near, NBLK) // LOC, turned[pl.ds(half * NB, NB), :])

    @pl.when(kind > 0)
    def _():
        for half in range(2):
            mine = col + LOC * half
            theirs = other_col + LOC * half
            rows = pl.ds((2 + half) * NB, NB)
            put(wrap(mine + LOC - kind, NBLK), half, direct[rows, :])
            put(theirs, wrap(theirs + LOC - kind, NBLK) // LOC, turned[rows, :])

    @pl.when(kind == 0)
    def _():
        for half in range(2):
            mine = col + LOC * half
            put(mine, half, diagonal_block(col, half, direct, turned).astype(BF16))
            put(wrap(mine + LOC, NBLK), half, jnp.zeros((NB, NB), BF16))


def owned_kernel(in_ref, out_ref):
    for row in range(4):
        for half in range(2):
            block = in_ref[half * NB : (half + 1) * NB, row * NB : (row + 1) * NB]
            out_ref[row, half] = block.astype(F32).T.astype(BF16)


def owned(slab):
    return pl.pallas_call(
        owned_kernel,
        out_shape=jax.ShapeDtypeStruct((4, 2, NB, NB), BF16),
        in_specs=[VMEM],
        out_specs=VMEM,
        cost_estimate=pl.CostEstimate(flops=1_000_000, bytes_accessed=550_000, transcendentals=0),
        name="owned",
    )(slab)


def ring_place(place_on_ring, core, k):
    even = jnp.where(lax.rem(place_on_ring, 2) == 0, place_on_ring + 1, place_on_ring - 1)
    odd = 3 - place_on_ring
    first, second = jnp.where(core == 0, even, odd), jnp.where(core == 0, odd, even)
    return (place_on_ring, first, second, wrap(place_on_ring + 2, 4))[k]


def product_kernel(*refs):
    upper_panel, lower_panel, direct, turned = refs[0:2], refs[2:4], refs[4:6], refs[6:8]
    mine_ref, other_ref, slab_ref, left = refs[8:12]
    dom, col, _ = place()
    y, core = dom // 2, lax.rem(dom, 2)
    depth = 2 * NB

    def put(block_row, half, block):
        slot = (lax.rem(block_row, NDOM) // 2) * 4 + block_row // NDOM
        rows = pl.ds(half * NB if isinstance(half, int) else pl.multiple_of(half * NB, NB), NB)
        left[rows, pl.ds(pl.multiple_of(slot * NB, NB), NB)] = block

    for k in range(4):
        kind = home(2 * ring_place(y, core, k) + core, col)
        column_blocks(kind, col, direct[k // 2].at[k % 2], turned[k // 2].at[k % 2], put)
    slab_ref[...] = left[:, pl.ds(pl.multiple_of(y * (2 * depth), depth), 2 * depth)]
    z, x = col // 4, lax.rem(col, 4)
    for x_step in range(4):
        part = jnp.zeros((2 * NB, NB), F32)
        for z_step in range(4):
            start = pl.multiple_of(ring_place(z, core, z_step) * (2 * depth), depth)
            part = part + jnp.dot(
                left[:, pl.ds(start, depth)],
                upper_panel[x_step // 2][x_step % 2, z_step],
                preferred_element_type=F32,
            )
            part = part + jnp.dot(
                left[:, pl.ds(pl.multiple_of(start + depth, depth), depth)],
                lower_panel[z_step // 2][z_step % 2, x_step],
                preferred_element_type=F32,
            )
        part = part.reshape(2, NB, NB)
        j = ring_place(x, core, x_step)

        @pl.when(core == j // 2)
        def _():
            mine_ref[:, lax.rem(j, 2)] = part

        @pl.when(core != j // 2)
        def _():
            other_ref[:, lax.rem(j, 2)] = part


def product_parts(panels, direct, turned):
    shape = jax.ShapeDtypeStruct((2, 2, NB, NB), F32)
    return pl.pallas_call(
        product_kernel,
        out_shape=(shape, shape, jax.ShapeDtypeStruct((2 * NB, 4 * NB), BF16)),
        in_specs=[VMEM] * 8,
        out_specs=(VMEM, VMEM, VMEM),
        scratch_shapes=[pltpu.VMEM((2 * NB, 16 * NB), BF16)],
        compiler_params=pltpu.CompilerParams(vmem_limit_bytes=32 << 20),
        cost_estimate=pl.CostEstimate(flops=540_000_000, bytes_accessed=4_000_000, transcendentals=0),
        name="product",
    )(*panels, *direct, *turned)


def device(y, core, col):
    return (2 * y + core) * NCOL + col


PLACES = [(y, core, col) for y in range(4) for core in range(2) for col in range(NCOL)]
TO_ROW = [(device(y, core, col), device(col // 4, core, 4 * y + col % 4)) for y, core, col in PLACES]
TO_OTHER_CORE = [(device(y, core, col), device(y, 1 - core, col)) for y, core, col in PLACES]


def from_partner():
    pairs = []
    for kind in range(NDOM):
        for col in range(NCOL):
            source = (col + (kind or LOC // 2)) % NCOL
            pairs.append((home(kind, source) * NCOL + source, home(kind, col) * NCOL + col))
    return pairs


def exchange(axis, step):
    pairs = []
    for y, core, col in PLACES:
        at = dict(y=y, z=col // 4, x=col % 4)
        at[axis] = at[axis] ^ 1 if core == step else 3 - at[axis]
        pairs.append((device(y, core, col), device(at["y"], core, 4 * at["z"] + at["x"])))
    return pairs


def first_near(value, axis):
    return jnp.stack([value, lax.ppermute(value, AXES, exchange(axis, 0))])


def second_near(pair, axis):
    return lax.ppermute(pair, AXES, exchange(axis, 1))


def shards(orbitals, potential, domain_start, margin_pairs, coefficients):
    own = lax.ppermute(coefficients.reshape(4 * NB, NB), AXES, TO_ROW)
    outgoing = messages(domain_start, margin_pairs[0], potential, orbitals)
    outgoing, own = lax.optimization_barrier((outgoing, own))
    incoming = lax.all_to_all(outgoing, AXES, split_axis=0, concat_axis=0, tiled=True)
    above, below = first_near(own[: 2 * NB], "z"), first_near(own[2 * NB :], "x")
    incoming, above, below = lax.optimization_barrier((incoming, above, below))
    above = jnp.concatenate([above, second_near(above, "z")])
    below = jnp.concatenate([below, second_near(below, "x")])
    direct, turned = sums(incoming)
    direct, turned, above, below = lax.optimization_barrier((direct, turned, above, below))
    turned = lax.ppermute(turned, AXES, from_partner())
    direct = first_near(direct, "y")
    above, below = first_near(above, "x"), first_near(below, "z")
    turned, direct, above, below = lax.optimization_barrier((turned, direct, above, below))
    turned = first_near(turned, "y")
    direct = direct, second_near(direct, "y")
    panels = above, second_near(above, "x"), below, second_near(below, "z")
    turned = turned, second_near(turned, "y")
    mine, other, slab = product_parts(panels, direct, turned)
    product = mine + lax.ppermute(other, AXES, TO_OTHER_CORE)
    potential_blocks = owned(slab).reshape(4, 1, 2, 1, NB, NB)
    return potential_blocks, jnp.swapaxes(product, 1, 2).reshape(2, 1, NB, 2, NB)


def solution(mesh):
    placed = (
        P(AXES, None, None, None),
        P(AXES, None),
        P(AXES),
        P(AXES, None, None),
        P(None, "dom", None, "col", None),
    )
    return jax.shard_map(
        shards,
        mesh=mesh,
        in_specs=placed,
        out_specs=(P(None, "dom", None, "col", None, None), P(None, "col", None, "dom", None)),
        check_vma=False,
    )
```

time: 157 us -> 123 us (0.78)
  between operations: 14.8 us -> 1.42 us
  waiting for transfers between devices: 72.8 us -> 60.4 us
  local copies, waits for them, and re-layouts: 9.66 us -> 1.64 us
  Pallas kernels: 22.2 us -> 18.8 us
  starting transfers between devices: 37.4 us -> 39.3 us
    ppermute x9 -> x15, waiting for transfers between devices: 0.02 us -> 57.8 us  [the longest x6 49.1 us: first_near(): return jnp.stack([value, lax.ppermute(value, AXES, exchange(axis, 0))])]
    all_to_all x1, waiting for transfers between devices: 52.6 us -> 2.67 us  [shards(): lax.all_to_all(outgoing, AXES, split_axis=0, concat_axis=0, tiled=True)]
    all_gather x1 -> x0, waiting for transfers between devices: 20.1 us -> none  [shards(): panel = lax.all_gather(rows, 'col', axis=0, tiled=False)]
    unnamed x19 -> x3, local copies, waits for them, and re-layouts: 9.66 us -> 1.6 us
    pallas_call x1, Pallas kernels: 10.6 us -> 4.34 us  [sums(): pl.pallas_call(sum_kernel, out_shape=(shape, shape), grid=(NDEV // CHUNK,...]
    pallas_call x2, Pallas kernels: 9.65 us -> 12.7 us  [the longest x1 10.4 us: messages(): pl.pallas_call(message_kernel, out_shape=pltpu.HBM((NDEV, ROWS, NB), BF16...]
    all_to_all x1, starting transfers between devices: 11.9 us -> 13.7 us  [shards(): lax.all_to_all(outgoing, AXES, split_axis=0, concat_axis=0, tiled=True)]
    ppermute x9 -> x15, starting transfers between devices: 25.5 us -> 25.6 us  [the longest x6 10.9 us: first_near(): return jnp.stack([value, lax.ppermute(value, AXES, exchange(axis, 0))])]
  transfers between devices with their start and end apart: 11 -> 16, of which waited for: 2 -> 8; matrix products, arithmetic and copies ran while one was open for 0% -> 1% of each run, Pallas kernels for 8% -> 13%
where the time goes in v2:
time: 123 us
  waiting for transfers between devices  60.4 us (49%)
  starting transfers between devices  39.3 us (32%)
  Pallas kernels  18.8 us (15%)
  local copies, waits for them, and re-layouts  1.64 us (1%)
  between operations  1.42 us (1%)
    ppermute x6, waiting for transfers between devices, first_near(): return jnp.stack([value, lax.ppermute(value, AXES, exchange(axis, 0))])  49.1 us
    all_to_all x1, starting transfers between devices, shards(): lax.all_to_all(outgoing, AXES, split_axis=0, concat_axis=0, tiled=True)  13.7 us
    ppermute x6, starting transfers between devices, first_near(): return jnp.stack([value, lax.ppermute(value, AXES, exchange(axis, 0))])  10.9 us
    pallas_call x1, Pallas kernels, messages(): pl.pallas_call(message_kernel, out_shape=pltpu.HBM((NDEV, ROWS, NB), BF16...  10.4 us
    ppermute x6, waiting for transfers between devices, second_near(): return lax.ppermute(pair, AXES, exchange(axis, 1))  7.07 us
    ppermute x1, starting transfers between devices, shards(): product = mine + lax.ppermute(other, AXES, TO_OTHER_CORE)  6.53 us
    pallas_call x1, Pallas kernels, sums(): pl.pallas_call(sum_kernel, out_shape=(shape, shape), grid=(NDEV // CHUNK,...  4.34 us
    ppermute x1, starting transfers between devices, shards(): turned = lax.ppermute(turned, AXES, from_partner())  3.97 us
  transfers between devices with their start and end apart: 16, of which 8 were waited for; matrix products, arithmetic and copies ran while one was open for 1% of the time, Pallas kernels for 13%

profile of v2, /device:TPU:1, one launch (start us, length us, event | category | flops | bytes accessed | tf_op | source)
XLA Modules:
  0.0 122.8 jit_solution(11607435140617235629)
XLA Ops:
  0.6 1.6 %collective-permute-start = (bf16[512,128]{1,0:T(8,128)(2,1)}, bf16[512,128]{1,0:T(8,128)(2,1)S(1)}, u32[]{:S(2)}, u32[]{:S(2)}) collective-permute-start(bf16[512,128]{1,0:T(8,128)(2,1)} %bitcast.36), channel_id=1, source_target_pairs={{0,0},{1,1},{2,2},{3,3},{4,32},{5,33},{6,34},{7,35},{8,64},{9,65},... | collective-permute-start | bytes 393224 | tf_op jit(solution)/shard_map/ppermute | solution.py:355
  2.8 10.4 %blocks.1 = bf16[128,136,128]{2,1,0:T(8,128)(2,1)} custom-call(s32[1]{0:T(128)S(6)} %copy.9.start_ref, s32[2,228]{1,0:T(2,128)} %bitcast.37, f32[1,1024]{1,0:T(1,128)} %potential_ref.1, bf16[2048,1024]{1,0:T(8,128)(2,1)} %bitcast.35), custom_call_target="tpu_custom_call" | custom-call | flops 5000000000 | bytes 9000000 | tf_op jit(solution)/shard_map/blocks/pallas_call | solution.py:113
  13.3 13.7 %all-to-all-start = ((bf16[128,136,128]{2,1,0:T(8,128)(2,1)}), bf16[128,136,128]{2,1,0:T(8,128)(2,1)}, u32[]{:S(2)}, u32[]{:S(2)}) async-start(bf16[128,136,128]{2,1,0:T(8,128)(2,1)} %blocks.1), calls=%async_computation | async-start | bytes 8912896 | tf_op jit(solution)/shard_map/all_to_all | solution.py:358
  27.0 2.7 %collective-permute-start.2 = (bf16[256,128]{1,0:T(8,128)(2,1)S(1)}, bf16[256,128]{1,0:T(8,128)(2,1)S(1)}, u32[]{:S(2)}, u32[]{:S(2)}) collective-permute-start(bf16[256,128]{1,0:T(8,128)(2,1)S(1)} %get-tuple-element.42), channel_id=1, source_target_pairs={{0,1},{1,0},{2,3},{3,2},{4,5},{5,4},{6,7},{7,6},{8,9},{9,8},{10,11... | collective-permute-start | bytes 196616 | tf_op jit(solution)/shard_map/ppermute | solution.py:347
  29.7 3.1 %collective-permute-start.1 = (bf16[256,128]{1,0:T(8,128)(2,1)S(1)}, bf16[256,128]{1,0:T(8,128)(2,1)S(1)}, u32[]{:S(2)}, u32[]{:S(2)}) collective-permute-start(bf16[256,128]{1,0:T(8,128)(2,1)S(1)} %get-tuple-element.43), channel_id=1, source_target_pairs={{0,4},{1,5},{2,6},{3,7},{4,0},{5,1},{6,2},{7,3},{8,12},{9,13},{10,... | collective-permute-start | bytes 196616 | tf_op jit(solution)/shard_map/ppermute | solution.py:347
  32.8 45.5 %collective-permute-done.2 = bf16[256,128]{1,0:T(8,128)(2,1)S(1)} collective-permute-done((bf16[256,128]{1,0:T(8,128)(2,1)S(1)}, bf16[256,128]{1,0:T(8,128)(2,1)S(1)}, u32[]{:S(2)}, u32[]{:S(2)}) %collective-permute-start.2) | collective-permute-done | bytes 65568 | tf_op jit(solution)/shard_map/ppermute | solution.py:347
  78.4 2.7 %all-to-all-done.in_ref = bf16[128,136,128]{2,1,0:T(8,128)(2,1)} async-done(((bf16[128,136,128]{2,1,0:T(8,128)(2,1)}), bf16[128,136,128]{2,1,0:T(8,128)(2,1)}, u32[]{:S(2)}, u32[]{:S(2)}) %all-to-all-start) | async-done | bytes 4456480 | tf_op jit(solution)/shard_map/all_to_all | solution.py:358
  81.1 1.5 %collective-permute-start.3 = (bf16[2,256,128]{2,1,0:T(8,128)(2,1)S(1)}, bf16[2,256,128]{2,1,0:T(8,128)(2,1)S(1)}, u32[]{:S(2)}, u32[]{:S(2)}) collective-permute-start(bf16[2,256,128]{2,1,0:T(8,128)(2,1)S(1)} %pad_maximum_fusion.6), channel_id=1, source_target_pairs={{0,12},{1,13},{2,14},{3,15},{4,8},{5,9},{6,10},{7,11},{8,4},{9,5},... | collective-permute-start | bytes 393224 | tf_op jit(solution)/shard_map/ppermute | solution.py:351
  82.5 0.3 collective-permute-start.4
  82.9 4.3 %sums.1 = (bf16[512,128]{1,0:T(8,128)(2,1)}, bf16[512,128]{1,0:T(8,128)(2,1)}) custom-call(bf16[128,136,128]{2,1,0:T(8,128)(2,1)} %all-to-all-done.in_ref), custom_call_target="tpu_custom_call" | custom-call | flops 300000000 | bytes 4700000 | tf_op jit(solution)/shard_map/sums/pallas_call | solution.py:190
  87.3 1.5 %collective-permute-start.7 = (bf16[4,256,128]{2,1,0:T(8,128)(2,1)S(1)}, bf16[4,256,128]{2,1,0:T(8,128)(2,1)S(1)}, u32[]{:S(2)}, u32[]{:S(2)}) collective-permute-start(bf16[4,256,128]{2,1,0:T(8,128)(2,1)S(1)} %pad_maximum_fusion.2), channel_id=1, source_target_pairs={{0,1},{1,0},{2,3},{3,2},{4,5},{5,4},{6,7},{7,6},{8,9},{9,8},{10,11... | collective-permute-start | bytes 786440 | tf_op jit(solution)/shard_map/ppermute | solution.py:347
  88.8 0.7 collective-permute-start.6
  89.5 0.4 collective-permute-start.8
  89.9 4.0 %collective-permute-start.5 = (bf16[512,128]{1,0:T(8,128)(2,1)}, bf16[512,128]{1,0:T(8,128)(2,1)S(1)}, u32[]{:S(2)}, u32[]{:S(2)}) collective-permute-start(bf16[512,128]{1,0:T(8,128)(2,1)} %get-tuple-element.27), channel_id=1, source_target_pairs={{8,0},{25,17},{10,2},{27,19},{12,4},{29,21},{14,6},{31,23},{0,8},{... | collective-permute-start | bytes 393224 | tf_op jit(solution)/shard_map/ppermute | solution.py:365
  93.9 0.1 collective-permute-done.6
  94.0 0.9 pad_maximum_fusion.4.refs_4_
  94.9 0.1 pad_maximum_fusion.refs_0_
  95.0 0.9 collective-permute-done.8
  95.9 0.1 pad_maximum_fusion.1.refs_2_
  96.0 1.6 %collective-permute-done.5 = bf16[512,128]{1,0:T(8,128)(2,1)S(1)} collective-permute-done((bf16[512,128]{1,0:T(8,128)(2,1)}, bf16[512,128]{1,0:T(8,128)(2,1)S(1)}, u32[]{:S(2)}, u32[]{:S(2)}) %collective-permute-start.5) | collective-permute-done | bytes 131104 | tf_op jit(solution)/shard_map/ppermute | solution.py:365
  97.6 0.8 collective-permute-start.9
  98.3 2.5 %collective-permute-start.12 = (bf16[512,128]{1,0:T(8,128)(2,1)S(1)}, bf16[512,128]{1,0:T(8,128)(2,1)S(1)}, u32[]{:S(2)}, u32[]{:S(2)}) collective-permute-start(bf16[512,128]{1,0:T(8,128)(2,1)S(1)} %collective-permute-done.5), channel_id=1, source_target_pairs={{0,32},{1,33},{2,34},{3,35},{4,36},{5,37},{6,38},{7,39},{8,40},{9,... | collective-permute-start | bytes 393224 | tf_op jit(solution)/shard_map/ppermute | solution.py:347
  100.8 2.5 %collective-permute-done.12 = bf16[512,128]{1,0:T(8,128)(2,1)S(1)} collective-permute-done((bf16[512,128]{1,0:T(8,128)(2,1)S(1)}, bf16[512,128]{1,0:T(8,128)(2,1)S(1)}, u32[]{:S(2)}, u32[]{:S(2)}) %collective-permute-start.12) | collective-permute-done | bytes 131104 | tf_op jit(solution)/shard_map/ppermute | solution.py:347
  103.4 0.1 collective-permute-start.13
  103.5 3.1 %collective-permute-done.11.refs_5_ = bf16[2,512,128]{2,1,0:T(8,128)(2,1)S(1)} collective-permute-done((bf16[2,512,128]{2,1,0:T(8,128)(2,1)S(1)}, bf16[2,512,128]{2,1,0:T(8,128)(2,1)S(1)}, u32[]{:S(2)}, u32[]{:S(2)}) %collective-permute-start.11) | collective-permute-done | bytes 262176 | tf_op jit(solution)/shard_map/ppermute | solution.py:351
  106.6 4.0 %collective-permute-done.13.refs_7_ = bf16[2,512,128]{2,1,0:T(8,128)(2,1)S(1)} collective-permute-done((bf16[2,512,128]{2,1,0:T(8,128)(2,1)S(1)}, bf16[2,512,128]{2,1,0:T(8,128)(2,1)S(1)}, u32[]{:S(2)}, u32[]{:S(2)}) %collective-permute-start.13) | collective-permute-done | bytes 262176 | tf_op jit(solution)/shard_map/ppermute | solution.py:351
  110.6 2.3 %product.1 = (f32[2,2,128,128]{3,2,1,0:T(8,128)S(1)}, f32[2,2,128,128]{3,2,1,0:T(8,128)S(1)}, bf16[256,512]{1,0:T(8,128)(2,1)S(1)}) custom-call(bf16[2,4,256,128]{3,2,1,0:T(8,128)(2,1)S(1)} %pad_maximum_fusion.refs_0_, bf16[2,4,256,128]{3,2,1,0:T(8,128)(2,1)S(1)} %collective-permute-done.9.refs_1_, bf16[2,4,256,128]{3,2,1,0:T(8,128)(2,1)S(1)} %pad_maximum_fusion.1.refs_2_, ...), custom_call_target="tpu_custom_call" | custom-call | flops 540000000 | bytes 4000000 | tf_op jit(solution)/shard_map/product/pallas_call | solution.py:307
  112.9 0.0 copy-start
  112.9 0.7 copy-done
  113.6 6.5 %collective-permute-start.14 = (f32[2,2,128,128]{3,2,1,0:T(8,128)S(1)}, f32[2,2,128,128]{3,2,1,0:T(8,128)S(1)}, u32[]{:S(2)}, u32[]{:S(2)}) collective-permute-start(f32[2,2,128,128]{3,2,1,0:T(8,128)S(1)} %get-tuple-element.37), channel_id=1, source_target_pairs={{0,16},{1,17},{2,18},{3,19},{4,20},{5,21},{6,22},{7,23},{8,24},{9,... | collective-permute-start | bytes 786440 | tf_op jit(solution)/shard_map/ppermute | solution.py:374
  120.1 1.8 %owned.1 = bf16[4,2,128,128]{3,2,1,0:T(8,128)(2,1)} custom-call(bf16[256,512]{1,0:T(8,128)(2,1)} %copy-done), custom_call_target="tpu_custom_call" | custom-call | flops 1000000 | bytes 550000 | tf_op jit(solution)/shard_map/owned/pallas_call | solution.py:245
  121.9 0.9 copy.8
  (17 shorter events, 0.2 us)
Async XLA Ops:
  0.6 12.6 %collective-permute-start = (bf16[512,128]{1,0:T(8,128)(2,1)}, bf16[512,128]{1,0:T(8,128)(2,1)S(1)}, u32[]{:S(2)}, u32[]{:S(2)}) collective-permute-start(bf16[512,128]{1,0:T(8,128)(2,1)} %bitcast.36), channel_id=1, source_target_pairs={{0,0},{1,1},{2,2},{3,3},{4,32},{5,33},{6,34},{7,35},{8,64},{9,65},... | collective-permute-start | bytes 393224 | tf_op jit(solution)/shard_map/ppermute | solution.py:355
  13.3 67.8 %all-to-all-start = ((bf16[128,136,128]{2,1,0:T(8,128)(2,1)}), bf16[128,136,128]{2,1,0:T(8,128)(2,1)}, u32[]{:S(2)}, u32[]{:S(2)}) async-start(bf16[128,136,128]{2,1,0:T(8,128)(2,1)} %blocks.1), calls=%async_computation | async-start | bytes 8912896 | tf_op jit(solution)/shard_map/all_to_all | solution.py:358
  27.0 51.3 %collective-permute-start.2 = (bf16[256,128]{1,0:T(8,128)(2,1)S(1)}, bf16[256,128]{1,0:T(8,128)(2,1)S(1)}, u32[]{:S(2)}, u32[]{:S(2)}) collective-permute-start(bf16[256,128]{1,0:T(8,128)(2,1)S(1)} %get-tuple-element.42), channel_id=1, source_target_pairs={{0,1},{1,0},{2,3},{3,2},{4,5},{5,4},{6,7},{7,6},{8,9},{9,8},{10,11... | collective-permute-start | bytes 196616 | tf_op jit(solution)/shard_map/ppermute | solution.py:347
  29.7 48.6 %collective-permute-start.1 = (bf16[256,128]{1,0:T(8,128)(2,1)S(1)}, bf16[256,128]{1,0:T(8,128)(2,1)S(1)}, u32[]{:S(2)}, u32[]{:S(2)}) collective-permute-start(bf16[256,128]{1,0:T(8,128)(2,1)S(1)} %get-tuple-element.43), channel_id=1, source_target_pairs={{0,4},{1,5},{2,6},{3,7},{4,0},{5,1},{6,2},{7,3},{8,12},{9,13},{10,... | collective-permute-start | bytes 196616 | tf_op jit(solution)/shard_map/ppermute | solution.py:347
  81.1 6.1 %collective-permute-start.3 = (bf16[2,256,128]{2,1,0:T(8,128)(2,1)S(1)}, bf16[2,256,128]{2,1,0:T(8,128)(2,1)S(1)}, u32[]{:S(2)}, u32[]{:S(2)}) collective-permute-start(bf16[2,256,128]{2,1,0:T(8,128)(2,1)S(1)} %pad_maximum_fusion.6), channel_id=1, source_target_pairs={{0,12},{1,13},{2,14},{3,15},{4,8},{5,9},{6,10},{7,11},{8,4},{9,5},... | collective-permute-start | bytes 393224 | tf_op jit(solution)/shard_map/ppermute | solution.py:351
  82.5 4.7 %collective-permute-start.4 = (bf16[2,256,128]{2,1,0:T(8,128)(2,1)S(1)}, bf16[2,256,128]{2,1,0:T(8,128)(2,1)S(1)}, u32[]{:S(2)}, u32[]{:S(2)}) collective-permute-start(bf16[2,256,128]{2,1,0:T(8,128)(2,1)S(1)} %pad_maximum_fusion.7), channel_id=1, source_target_pairs={{0,3},{1,2},{2,1},{3,0},{4,7},{5,6},{6,5},{7,4},{8,11},{9,10},{10,... | collective-permute-start | bytes 393224 | tf_op jit(solution)/shard_map/ppermute | solution.py:351
  87.3 7.7 %collective-permute-start.7 = (bf16[4,256,128]{2,1,0:T(8,128)(2,1)S(1)}, bf16[4,256,128]{2,1,0:T(8,128)(2,1)S(1)}, u32[]{:S(2)}, u32[]{:S(2)}) collective-permute-start(bf16[4,256,128]{2,1,0:T(8,128)(2,1)S(1)} %pad_maximum_fusion.2), channel_id=1, source_target_pairs={{0,1},{1,0},{2,3},{3,2},{4,5},{5,4},{6,7},{7,6},{8,9},{9,8},{10,11... | collective-permute-start | bytes 786440 | tf_op jit(solution)/shard_map/ppermute | solution.py:347
  88.8 5.2 %collective-permute-start.6 = (bf16[512,128]{1,0:T(8,128)(2,1)}, bf16[512,128]{1,0:T(8,128)(2,1)S(1)}, u32[]{:S(2)}, u32[]{:S(2)}) collective-permute-start(bf16[512,128]{1,0:T(8,128)(2,1)} %get-tuple-element.28), channel_id=1, source_target_pairs={{0,32},{1,33},{2,34},{3,35},{4,36},{5,37},{6,38},{7,39},{8,40},{9,... | collective-permute-start | bytes 393224 | tf_op jit(solution)/shard_map/ppermute | solution.py:347
  89.5 6.4 %collective-permute-start.8 = (bf16[4,256,128]{2,1,0:T(8,128)(2,1)S(1)}, bf16[4,256,128]{2,1,0:T(8,128)(2,1)S(1)}, u32[]{:S(2)}, u32[]{:S(2)}) collective-permute-start(bf16[4,256,128]{2,1,0:T(8,128)(2,1)S(1)} %pad_maximum_fusion.3), channel_id=1, source_target_pairs={{0,4},{1,5},{2,6},{3,7},{4,0},{5,1},{6,2},{7,3},{8,12},{9,13},{10,... | collective-permute-start | bytes 786440 | tf_op jit(solution)/shard_map/ppermute | solution.py:347
  89.9 7.7 %collective-permute-start.5 = (bf16[512,128]{1,0:T(8,128)(2,1)}, bf16[512,128]{1,0:T(8,128)(2,1)S(1)}, u32[]{:S(2)}, u32[]{:S(2)}) collective-permute-start(bf16[512,128]{1,0:T(8,128)(2,1)} %get-tuple-element.27), channel_id=1, source_target_pairs={{8,0},{25,17},{10,2},{27,19},{12,4},{29,21},{14,6},{31,23},{0,8},{... | collective-permute-start | bytes 393224 | tf_op jit(solution)/shard_map/ppermute | solution.py:365
  97.6 13.0 %collective-permute-start.9 = (bf16[2,4,256,128]{3,2,1,0:T(8,128)(2,1)S(1)}, bf16[2,4,256,128]{3,2,1,0:T(8,128)(2,1)S(1)}, u32[]{:S(2)}, u32[]{:S(2)}) collective-permute-start(bf16[2,4,256,128]{3,2,1,0:T(8,128)(2,1)S(1)} %pad_maximum_fusion.refs_0_), channel_id=1, source_target_pairs={{0,3},{1,2},{2,1},{3,0},{4,7},{5,6},{6,5},{7,4},{8,11},{9,10},{10,... | collective-permute-start | bytes 1572872 | tf_op jit(solution)/shard_map/ppermute | solution.py:351
  98.3 12.2 %collective-permute-start.10 = (bf16[2,4,256,128]{3,2,1,0:T(8,128)(2,1)S(1)}, bf16[2,4,256,128]{3,2,1,0:T(8,128)(2,1)S(1)}, u32[]{:S(2)}, u32[]{:S(2)}) collective-permute-start(bf16[2,4,256,128]{3,2,1,0:T(8,128)(2,1)S(1)} %pad_maximum_fusion.1.refs_2_), channel_id=1, source_target_pairs={{0,12},{1,13},{2,14},{3,15},{4,8},{5,9},{6,10},{7,11},{8,4},{9,5},... | collective-permute-start | bytes 1572872 | tf_op jit(solution)/shard_map/ppermute | solution.py:351
  98.3 5.0 %collective-permute-start.12 = (bf16[512,128]{1,0:T(8,128)(2,1)S(1)}, bf16[512,128]{1,0:T(8,128)(2,1)S(1)}, u32[]{:S(2)}, u32[]{:S(2)}) collective-permute-start(bf16[512,128]{1,0:T(8,128)(2,1)S(1)} %collective-permute-done.5), channel_id=1, source_target_pairs={{0,32},{1,33},{2,34},{3,35},{4,36},{5,37},{6,38},{7,39},{8,40},{9,... | collective-permute-start | bytes 393224 | tf_op jit(solution)/shard_map/ppermute | solution.py:347
  100.8 5.8 %collective-permute-start.11 = (bf16[2,512,128]{2,1,0:T(8,128)(2,1)S(1)}, bf16[2,512,128]{2,1,0:T(8,128)(2,1)S(1)}, u32[]{:S(2)}, u32[]{:S(2)}) collective-permute-start(bf16[2,512,128]{2,1,0:T(8,128)(2,1)S(1)} %pad_maximum_fusion.4.refs_4_), channel_id=1, source_target_pairs={{0,96},{1,97},{2,98},{3,99},{4,100},{5,101},{6,102},{7,103},{8,104... | collective-permute-start | bytes 786440 | tf_op jit(solution)/shard_map/ppermute | solution.py:351
  103.4 7.2 %collective-permute-start.13 = (bf16[2,512,128]{2,1,0:T(8,128)(2,1)S(1)}, bf16[2,512,128]{2,1,0:T(8,128)(2,1)S(1)}, u32[]{:S(2)}, u32[]{:S(2)}) collective-permute-start(bf16[2,512,128]{2,1,0:T(8,128)(2,1)S(1)} %pad_maximum_fusion.5.refs_6_), channel_id=1, source_target_pairs={{0,96},{1,97},{2,98},{3,99},{4,100},{5,101},{6,102},{7,103},{8,104... | collective-permute-start | bytes 786440 | tf_op jit(solution)/shard_map/ppermute | solution.py:351
  112.9 0.7 copy-start
  113.6 8.3 %collective-permute-start.14 = (f32[2,2,128,128]{3,2,1,0:T(8,128)S(1)}, f32[2,2,128,128]{3,2,1,0:T(8,128)S(1)}, u32[]{:S(2)}, u32[]{:S(2)}) collective-permute-start(f32[2,2,128,128]{3,2,1,0:T(8,128)S(1)} %get-tuple-element.37), channel_id=1, source_target_pairs={{0,16},{1,17},{2,18},{3,19},{4,20},{5,21},{6,22},{7,23},{8,24},{9,... | collective-permute-start | bytes 786440 | tf_op jit(solution)/shard_map/ppermute | solution.py:374

commit v3 on v2

--- a/solution.py
+++ b/solution.py
@@ -17,7 +17,9 @@
 NCOL = 16
 NDEV = NDOM * NCOL
 HELD = 4 * NB
-ROWS = NB + 8
+SUB = 8
+TILES = NB // SUB
+ROWS = NB + SUB
 CHUNK = 64
 TILE = 16
 VMEM = pl.BlockSpec(memory_space=pltpu.VMEM)
@@ -36,7 +38,8 @@
 
 
 def message_kernel(
-    start_ref, pairs_ref, potential_ref, orbitals_ref, out_ref, held, weighted, diagonal, pairs, potential, sems
+    start_ref, pairs_ref, potential_ref, orbitals_ref, out_ref,
+    held, weighted, diagonal, outgoing, pairs, potential, sems, out_sem,
 ):
     step_rows = 2 * NB
     steps = LOC // 2
@@ -61,13 +64,18 @@
     codes = pairs[0:1, :] * LOC + pairs[1:2, :]
     scale = potential[...]
 
+    slots = {}
+
     def send(kind, col, block, last_rows):
-        col = lax.rem(col, NCOL)
-        target = home(kind, col) * NCOL + col
+        slot = slots.setdefault((kind, col), len(slots))
         if block is not None:
-            out_ref[target, 0:NB, :] = block.astype(BF16)
-        if last_rows is not None:
-            out_ref[target, NB:ROWS, :] = last_rows.astype(BF16)
+            outgoing[slot, 0:TILES] = block.reshape(TILES, SUB, NB).astype(BF16)
+        if last_rows is None:
+            return
+        outgoing[slot, TILES] = last_rows.astype(BF16)
+        column = lax.rem(start + col, NCOL)
+        target = home(kind, column) * NCOL + column
+        pltpu.make_async_copy(outgoing.at[slot], out_ref.at[target], out_sem).start()
 
     for right in range(steps):
         copies[right].wait()
@@ -91,16 +99,17 @@
                         diagonal[a] = block
                     elif gap == 0:
                         low = a - LOC // 2
-                        send(0, start + low, jnp.where(upper(False), diagonal[low], block), tail)
+                        send(0, low, jnp.where(upper(False), diagonal[low], block), tail)
                         extra = jnp.sum(jnp.where(eye, block, 0.0), axis=0, keepdims=True)
-                        send(0, start + a, None, jnp.where(tail_row == 0, extra, tail))
+                        send(0, a, None, jnp.where(tail_row == 0, extra, tail))
                     elif gap < LOC // 2:
-                        send(gap, start + b, block, tail)
+                        send(gap, b, block, tail)
                     elif gap == LOC // 2:
-                        send(0, start + b, block, None)
+                        send(0, b, block, None)
                     else:
                         listed = jnp.max(jnp.where(codes == a * LOC + b, 1.0, 0.0), axis=1, keepdims=True)
-                        send(LOC - gap, start + a, block * listed, tail)
+                        send(LOC - gap, a, block * listed, tail)
+    pltpu.make_async_copy(outgoing, out_ref, out_sem).wait()
 
 
 def in_hbm(value):
@@ -112,21 +121,23 @@
     grid_points = orbitals.shape[-1]
     return pl.pallas_call(
         message_kernel,
-        out_shape=pltpu.HBM((NDEV, ROWS, NB), BF16),
+        out_shape=pltpu.HBM((NDEV, TILES + 1, SUB, NB), BF16),
         in_specs=[SMEM, HBM, HBM, HBM],
-        out_specs=VMEM,
+        out_specs=HBM,
         scratch_shapes=[
             pltpu.VMEM((rows, grid_points), BF16),
             pltpu.VMEM((rows, grid_points), BF16),
             pltpu.VMEM((LOC // 2, NB, NB), F32),
+            pltpu.VMEM((NDEV, TILES + 1, SUB, NB), BF16),
             pltpu.VMEM(margin_pairs.shape, jnp.int32),
             pltpu.VMEM(potential.shape, F32),
             pltpu.SemaphoreType.DMA((LOC // 2 + 2,)),
+            pltpu.SemaphoreType.DMA,
         ],
         compiler_params=pltpu.CompilerParams(vmem_limit_bytes=40 << 20),
         cost_estimate=pl.CostEstimate(flops=5_000_000_000, bytes_accessed=9_000_000, transcendentals=0),
         name="blocks",
-    )(domain_start, in_hbm(margin_pairs), in_hbm(potential), in_hbm(orbitals.reshape(rows, grid_points)))
+    )(domain_start, in_hbm(margin_pairs), in_hbm(potential), in_hbm(orbitals.reshape(rows, grid_points))).reshape(NDEV, ROWS, NB)
 
 
 def wrap(value, size):
@@ -234,24 +245,6 @@
             put(wrap(mine + LOC, NBLK), half, jnp.zeros((NB, NB), BF16))
 
 
-def owned_kernel(in_ref, out_ref):
-    for row in range(4):
-        for half in range(2):
-            block = in_ref[half * NB : (half + 1) * NB, row * NB : (row + 1) * NB]
-            out_ref[row, half] = block.astype(F32).T.astype(BF16)
-
-
-def owned(slab):
-    return pl.pallas_call(
-        owned_kernel,
-        out_shape=jax.ShapeDtypeStruct((4, 2, NB, NB), BF16),
-        in_specs=[VMEM],
-        out_specs=VMEM,
-        cost_estimate=pl.CostEstimate(flops=1_000_000, bytes_accessed=550_000, transcendentals=0),
-        name="owned",
-    )(slab)
-
-
 def ring_place(place_on_ring, core, k):
     even = jnp.where(lax.rem(place_on_ring, 2) == 0, place_on_ring + 1, place_on_ring - 1)
     odd = 3 - place_on_ring
@@ -259,12 +252,43 @@
     return (place_on_ring, first, second, wrap(place_on_ring + 2, 4))[k]
 
 
-def product_kernel(*refs):
-    upper_panel, lower_panel, direct, turned = refs[0:2], refs[2:4], refs[4:6], refs[6:8]
-    mine_ref, other_ref, slab_ref, left = refs[8:12]
+def half_product(panels, left, core, z, x, wanted, out_ref):
+    upper_panel, lower_panel = panels[0:2], panels[2:4]
+    depth = 2 * NB
+
+    def add_up(steps):
+        part = jnp.zeros((2 * NB, 2 * NB), F32)
+        for z_step in range(4):
+            start = pl.multiple_of(ring_place(z, core, z_step) * (2 * depth), depth)
+            above = [upper_panel[k // 2][k % 2, z_step] for k in steps]
+            below = [lower_panel[z_step // 2][z_step % 2, k] for k in steps]
+            part = part + jnp.dot(
+                left[:, pl.ds(start, depth)], jnp.concatenate(above, axis=1), preferred_element_type=F32
+            )
+            part = part + jnp.dot(
+                left[:, pl.ds(pl.multiple_of(start + depth, depth), depth)],
+                jnp.concatenate(below, axis=1),
+                preferred_element_type=F32,
+            )
+        for i, k in enumerate(steps):
+            place_of = lax.rem(ring_place(x, core, k), 2)
+            out_ref[:, place_of] = part[:, i * NB : (i + 1) * NB].reshape(2, NB, NB)
+
+    near = wanted == x // 2
+    for on, steps in (
+        (near & (core == 0), (0, 1)),
+        (~near & (core == 0), (2, 3)),
+        (near & (core == 1), (0, 2)),
+        (~near & (core == 1), (1, 3)),
+    ):
+        pl.when(on)(functools.partial(add_up, steps))
+
+
+def other_kernel(*refs):
+    panels, direct, turned = refs[0:4], refs[4:6], refs[6:8]
+    other_ref, left = refs[8:10]
     dom, col, _ = place()
     y, core = dom // 2, lax.rem(dom, 2)
-    depth = 2 * NB
 
     def put(block_row, half, block):
         slot = (lax.rem(block_row, NDOM) // 2) * 4 + block_row // NDOM
@@ -274,46 +298,43 @@
     for k in range(4):
         kind = home(2 * ring_place(y, core, k) + core, col)
         column_blocks(kind, col, direct[k // 2].at[k % 2], turned[k // 2].at[k % 2], put)
-    slab_ref[...] = left[:, pl.ds(pl.multiple_of(y * (2 * depth), depth), 2 * depth)]
-    z, x = col // 4, lax.rem(col, 4)
-    for x_step in range(4):
-        part = jnp.zeros((2 * NB, NB), F32)
-        for z_step in range(4):
-            start = pl.multiple_of(ring_place(z, core, z_step) * (2 * depth), depth)
-            part = part + jnp.dot(
-                left[:, pl.ds(start, depth)],
-                upper_panel[x_step // 2][x_step % 2, z_step],
-                preferred_element_type=F32,
-            )
-            part = part + jnp.dot(
-                left[:, pl.ds(pl.multiple_of(start + depth, depth), depth)],
-                lower_panel[z_step // 2][z_step % 2, x_step],
-                preferred_element_type=F32,
-            )
-        part = part.reshape(2, NB, NB)
-        j = ring_place(x, core, x_step)
-
-        @pl.when(core == j // 2)
-        def _():
-            mine_ref[:, lax.rem(j, 2)] = part
-
-        @pl.when(core != j // 2)
-        def _():
-            other_ref[:, lax.rem(j, 2)] = part
-
-
-def product_parts(panels, direct, turned):
-    shape = jax.ShapeDtypeStruct((2, 2, NB, NB), F32)
+    half_product(panels, left, core, col // 4, lax.rem(col, 4), 1 - core, other_ref)
+
+
+def mine_kernel(*refs):
+    panels, left, mine_ref, blocks_ref = refs[0:4], refs[4], refs[5], refs[6]
+    dom, col, _ = place()
+    y, core = dom // 2, lax.rem(dom, 2)
+    half_product(panels, left, core, col // 4, lax.rem(col, 4), core, mine_ref)
+    for row in range(4):
+        column = pl.ds(pl.multiple_of((y * 4 + row) * NB, NB), NB)
+        for half in range(2):
+            block = left[half * NB : (half + 1) * NB, column]
+            blocks_ref[row, half] = block.astype(F32).T.astype(BF16)
+
+
+def product_for_other(panels, direct, turned):
     return pl.pallas_call(
-        product_kernel,
-        out_shape=(shape, shape, jax.ShapeDtypeStruct((2 * NB, 4 * NB), BF16)),
+        other_kernel,
+        out_shape=(jax.ShapeDtypeStruct((2, 2, NB, NB), F32), jax.ShapeDtypeStruct((2 * NB, 16 * NB), BF16)),
         in_specs=[VMEM] * 8,
-        out_specs=(VMEM, VMEM, VMEM),
-        scratch_shapes=[pltpu.VMEM((2 * NB, 16 * NB), BF16)],
+        out_specs=(VMEM, VMEM),
         compiler_params=pltpu.CompilerParams(vmem_limit_bytes=32 << 20),
-        cost_estimate=pl.CostEstimate(flops=540_000_000, bytes_accessed=4_000_000, transcendentals=0),
-        name="product",
+        cost_estimate=pl.CostEstimate(flops=270_000_000, bytes_accessed=4_000_000, transcendentals=0),
+        name="other",
     )(*panels, *direct, *turned)
+
+
+def product_for_me(panels, left):
+    return pl.pallas_call(
+        mine_kernel,
+        out_shape=(jax.ShapeDtypeStruct((2, 2, NB, NB), F32), jax.ShapeDtypeStruct((4, 2, NB, NB), BF16)),
+        in_specs=[VMEM] * 5,
+        out_specs=(VMEM, VMEM),
+        compiler_params=pltpu.CompilerParams(vmem_limit_bytes=32 << 20),
+        cost_estimate=pl.CostEstimate(flops=270_000_000, bytes_accessed=4_000_000, transcendentals=0),
+        name="mine",
+    )(*panels, left)
 
 
 def device(y, core, col):
@@ -357,22 +378,24 @@
     outgoing, own = lax.optimization_barrier((outgoing, own))
     incoming = lax.all_to_all(outgoing, AXES, split_axis=0, concat_axis=0, tiled=True)
     above, below = first_near(own[: 2 * NB], "z"), first_near(own[2 * NB :], "x")
-    incoming, above, below = lax.optimization_barrier((incoming, above, below))
     above = jnp.concatenate([above, second_near(above, "z")])
     below = jnp.concatenate([below, second_near(below, "x")])
+    incoming, above, below = lax.optimization_barrier((incoming, above, below))
+    above, below = first_near(above, "x"), first_near(below, "z")
     direct, turned = sums(incoming)
     direct, turned, above, below = lax.optimization_barrier((direct, turned, above, below))
     turned = lax.ppermute(turned, AXES, from_partner())
     direct = first_near(direct, "y")
-    above, below = first_near(above, "x"), first_near(below, "z")
-    turned, direct, above, below = lax.optimization_barrier((turned, direct, above, below))
+    panels = above, second_near(above, "x"), below, second_near(below, "z")
+    turned, direct = lax.optimization_barrier((turned, direct))
     turned = first_near(turned, "y")
     direct = direct, second_near(direct, "y")
-    panels = above, second_near(above, "x"), below, second_near(below, "z")
     turned = turned, second_near(turned, "y")
-    mine, other, slab = product_parts(panels, direct, turned)
-    product = mine + lax.ppermute(other, AXES, TO_OTHER_CORE)
-    potential_blocks = owned(slab).reshape(4, 1, 2, 1, NB, NB)
+    other, left = product_for_other(panels, direct, turned)
+    theirs = lax.ppermute(other, AXES, TO_OTHER_CORE)
+    mine, owned = product_for_me(panels, left)
+    product = mine + theirs
+    potential_blocks = owned.reshape(4, 1, 2, 1, NB, NB)
     return potential_blocks, jnp.swapaxes(product, 1, 2).reshape(2, 1, NB, 2, NB)
 
 

time: 123 us -> 119 us (0.967)
  Pallas kernels: 18.8 us -> 15.8 us
    pallas_call x3, Pallas kernels: 14.5 us -> 11.5 us  [the longest x1 8.97 us: messages(): pl.pallas_call(message_kernel, out_shape=pltpu.HBM((NDEV, TILES + 1, SUB,...]
    all_to_all x1, waiting for transfers between devices: 2.67 us -> 0.01 us  [shards(): lax.all_to_all(outgoing, AXES, split_axis=0, concat_axis=0, tiled=True)]
    ppermute x6, starting transfers between devices: 10.9 us -> 13 us  [first_near(): return jnp.stack([value, lax.ppermute(value, AXES, exchange(axis, 0))])]
    ppermute x1, starting transfers between devices: 6.53 us -> 4.78 us  [shards(): theirs = lax.ppermute(other, AXES, TO_OTHER_CORE)]
  transfers between devices with their start and end apart: 16 -> 16, of which waited for: 8 -> 7; matrix products, arithmetic and copies ran while one was open for 1% -> 1% of each run, Pallas kernels for 13% -> 12%
where the time goes in v3:
time: 119 us
  waiting for transfers between devices  60.5 us (51%)
  starting transfers between devices  38.9 us (33%)
  Pallas kernels  15.8 us (13%)
  between operations  1.42 us (1%)
    ppermute x6, waiting for transfers between devices, first_near(): return jnp.stack([value, lax.ppermute(value, AXES, exchange(axis, 0))])  49.9 us
    all_to_all x1, starting transfers between devices, shards(): lax.all_to_all(outgoing, AXES, split_axis=0, concat_axis=0, tiled=True)  13.7 us
    ppermute x6, starting transfers between devices, first_near(): return jnp.stack([value, lax.ppermute(value, AXES, exchange(axis, 0))])  13 us
    pallas_call x1, Pallas kernels, messages(): pl.pallas_call(message_kernel, out_shape=pltpu.HBM((NDEV, TILES + 1, SUB,...  8.97 us
    ppermute x6, waiting for transfers between devices, second_near(): return lax.ppermute(pair, AXES, exchange(axis, 1))  7.94 us
    ppermute x1, starting transfers between devices, shards(): theirs = lax.ppermute(other, AXES, TO_OTHER_CORE)  4.78 us
    pallas_call x1, Pallas kernels, sums(): pl.pallas_call(sum_kernel, out_shape=(shape, shape), grid=(NDEV // CHUNK,...  4.34 us
    ppermute x1, starting transfers between devices, shards(): turned = lax.ppermute(turned, AXES, from_partner())  4.22 us
  transfers between devices with their start and end apart: 16, of which 7 were waited for; matrix products, arithmetic and copies ran while one was open for 1% of the time, Pallas kernels for 12%

profile of v3, /device:TPU:1, one launch (start us, length us, event | category | flops | bytes accessed | tf_op | source)
XLA Modules:
  0.0 118.8 jit_solution(13169111381088802269)
XLA Ops:
  0.6 1.6 %collective-permute-start = (bf16[512,128]{1,0:T(8,128)(2,1)}, bf16[512,128]{1,0:T(8,128)(2,1)S(1)}, u32[]{:S(2)}, u32[]{:S(2)}) collective-permute-start(bf16[512,128]{1,0:T(8,128)(2,1)} %bitcast.40), channel_id=1, source_target_pairs={{0,0},{1,1},{2,2},{3,3},{4,32},{5,33},{6,34},{7,35},{8,64},{9,65},... | collective-permute-start | bytes 393224 | tf_op jit(solution)/shard_map/ppermute | solution.py:376
  2.8 9.0 %blocks.1 = bf16[128,17,8,128]{3,2,1,0:T(8,128)(2,1)} custom-call(s32[1]{0:T(128)S(6)} %copy.9.start_ref, s32[2,228]{1,0:T(2,128)} %bitcast.41, f32[1,1024]{1,0:T(1,128)} %potential_ref.1, bf16[2048,1024]{1,0:T(8,128)(2,1)} %bitcast.38), custom_call_target="tpu_custom_call" | custom-call | flops 5000000000 | bytes 9000000 | tf_op jit(solution)/shard_map/blocks/pallas_call | solution.py:122
  11.8 13.7 %all-to-all-start = ((bf16[128,136,128]{2,1,0:T(8,128)(2,1)}), bf16[128,136,128]{2,1,0:T(8,128)(2,1)}, u32[]{:S(2)}, u32[]{:S(2)}) async-start(bf16[128,136,128]{2,1,0:T(8,128)(2,1)} %bitcast.25), calls=%async_computation | async-start | bytes 8912896 | tf_op jit(solution)/shard_map/all_to_all | solution.py:379
  25.6 2.7 %collective-permute-start.3 = (bf16[256,128]{1,0:T(8,128)(2,1)S(1)}, bf16[256,128]{1,0:T(8,128)(2,1)S(1)}, u32[]{:S(2)}, u32[]{:S(2)}) collective-permute-start(bf16[256,128]{1,0:T(8,128)(2,1)S(1)} %get-tuple-element.40), channel_id=1, source_target_pairs={{0,1},{1,0},{2,3},{3,2},{4,5},{5,4},{6,7},{7,6},{8,9},{9,8},{10,11... | collective-permute-start | bytes 196616 | tf_op jit(solution)/shard_map/ppermute | solution.py:368
  28.3 3.1 %collective-permute-start.1 = (bf16[256,128]{1,0:T(8,128)(2,1)S(1)}, bf16[256,128]{1,0:T(8,128)(2,1)S(1)}, u32[]{:S(2)}, u32[]{:S(2)}) collective-permute-start(bf16[256,128]{1,0:T(8,128)(2,1)S(1)} %get-tuple-element.41), channel_id=1, source_target_pairs={{0,4},{1,5},{2,6},{3,7},{4,0},{5,1},{6,2},{7,3},{8,12},{9,13},{10,... | collective-permute-start | bytes 196616 | tf_op jit(solution)/shard_map/ppermute | solution.py:368
  31.4 45.5 %collective-permute-done.3 = bf16[256,128]{1,0:T(8,128)(2,1)S(1)} collective-permute-done((bf16[256,128]{1,0:T(8,128)(2,1)S(1)}, bf16[256,128]{1,0:T(8,128)(2,1)S(1)}, u32[]{:S(2)}, u32[]{:S(2)}) %collective-permute-start.3) | collective-permute-done | bytes 65568 | tf_op jit(solution)/shard_map/ppermute | solution.py:368
  76.9 0.1 collective-permute-start.4
  77.1 1.4 %collective-permute-start.2 = (bf16[2,256,128]{2,1,0:T(8,128)(2,1)S(1)}, bf16[2,256,128]{2,1,0:T(8,128)(2,1)S(1)}, u32[]{:S(2)}, u32[]{:S(2)}) collective-permute-start(bf16[2,256,128]{2,1,0:T(8,128)(2,1)S(1)} %pad_maximum_fusion.6), channel_id=1, source_target_pairs={{0,12},{1,13},{2,14},{3,15},{4,8},{5,9},{6,10},{7,11},{8,4},{9,5},... | collective-permute-start | bytes 393224 | tf_op jit(solution)/shard_map/ppermute | solution.py:372
  78.5 2.6 %collective-permute-done.4 = bf16[2,256,128]{2,1,0:T(8,128)(2,1)S(1)} collective-permute-done((bf16[2,256,128]{2,1,0:T(8,128)(2,1)S(1)}, bf16[2,256,128]{2,1,0:T(8,128)(2,1)S(1)}, u32[]{:S(2)}, u32[]{:S(2)}) %collective-permute-start.4) | collective-permute-done | bytes 131104 | tf_op jit(solution)/shard_map/ppermute | solution.py:372
  81.2 0.1 collective-permute-done.2
  81.3 1.0 collective-permute-start.5
  82.3 2.7 %collective-permute-start.6 = (bf16[4,256,128]{2,1,0:T(8,128)(2,1)S(1)}, bf16[4,256,128]{2,1,0:T(8,128)(2,1)S(1)}, u32[]{:S(2)}, u32[]{:S(2)}) collective-permute-start(bf16[4,256,128]{2,1,0:T(8,128)(2,1)S(1)} %pad_maximum_fusion.3), channel_id=1, source_target_pairs={{0,4},{1,5},{2,6},{3,7},{4,0},{5,1},{6,2},{7,3},{8,12},{9,13},{10,... | collective-permute-start | bytes 786440 | tf_op jit(solution)/shard_map/ppermute | solution.py:368
  85.0 4.3 %sums.1 = (bf16[512,128]{1,0:T(8,128)(2,1)}, bf16[512,128]{1,0:T(8,128)(2,1)}) custom-call(bf16[128,136,128]{2,1,0:T(8,128)(2,1)} %all-to-all-done.in_ref), custom_call_target="tpu_custom_call" | custom-call | flops 300000000 | bytes 4700000 | tf_op jit(solution)/shard_map/sums/pallas_call | solution.py:201
  89.3 0.1 pad_maximum_fusion.refs_0_
  89.4 0.1 pad_maximum_fusion.1.refs_2_
  89.5 2.6 %collective-permute-start.10 = (bf16[512,128]{1,0:T(8,128)(2,1)}, bf16[512,128]{1,0:T(8,128)(2,1)S(1)}, u32[]{:S(2)}, u32[]{:S(2)}) collective-permute-start(bf16[512,128]{1,0:T(8,128)(2,1)} %get-tuple-element.29), channel_id=1, source_target_pairs={{0,32},{1,33},{2,34},{3,35},{4,36},{5,37},{6,38},{7,39},{8,40},{9,... | collective-permute-start | bytes 393224 | tf_op jit(solution)/shard_map/ppermute | solution.py:368
  92.0 4.2 %collective-permute-start.9 = (bf16[512,128]{1,0:T(8,128)(2,1)}, bf16[512,128]{1,0:T(8,128)(2,1)S(1)}, u32[]{:S(2)}, u32[]{:S(2)}) collective-permute-start(bf16[512,128]{1,0:T(8,128)(2,1)} %get-tuple-element.28), channel_id=1, source_target_pairs={{8,0},{25,17},{10,2},{27,19},{12,4},{29,21},{14,6},{31,23},{0,8},{... | collective-permute-start | bytes 393224 | tf_op jit(solution)/shard_map/ppermute | solution.py:387
  96.3 0.0 collective-permute-start.7
  96.3 0.0 collective-permute-start.8
  96.3 0.0 collective-permute-done.10
  96.3 0.9 pad_maximum_fusion.4.refs_4_
  97.2 2.7 %collective-permute-done.9 = bf16[512,128]{1,0:T(8,128)(2,1)S(1)} collective-permute-done((bf16[512,128]{1,0:T(8,128)(2,1)}, bf16[512,128]{1,0:T(8,128)(2,1)S(1)}, u32[]{:S(2)}, u32[]{:S(2)}) %collective-permute-start.9) | collective-permute-done | bytes 131104 | tf_op jit(solution)/shard_map/ppermute | solution.py:387
  99.9 1.0 collective-permute-start.12
  100.8 0.0 collective-permute-start.11
  100.9 4.3 %collective-permute-done.12 = bf16[512,128]{1,0:T(8,128)(2,1)S(1)} collective-permute-done((bf16[512,128]{1,0:T(8,128)(2,1)S(1)}, bf16[512,128]{1,0:T(8,128)(2,1)S(1)}, u32[]{:S(2)}, u32[]{:S(2)}) %collective-permute-start.12) | collective-permute-done | bytes 131104 | tf_op jit(solution)/shard_map/ppermute | solution.py:368
  105.2 0.1 collective-permute-start.13
  105.3 2.4 %collective-permute-done.11.refs_5_ = bf16[2,512,128]{2,1,0:T(8,128)(2,1)S(1)} collective-permute-done((bf16[2,512,128]{2,1,0:T(8,128)(2,1)S(1)}, bf16[2,512,128]{2,1,0:T(8,128)(2,1)S(1)}, u32[]{:S(2)}, u32[]{:S(2)}) %collective-permute-start.11) | collective-permute-done | bytes 262176 | tf_op jit(solution)/shard_map/ppermute | solution.py:372
  107.8 2.8 %collective-permute-done.13.refs_7_ = bf16[2,512,128]{2,1,0:T(8,128)(2,1)S(1)} collective-permute-done((bf16[2,512,128]{2,1,0:T(8,128)(2,1)S(1)}, bf16[2,512,128]{2,1,0:T(8,128)(2,1)S(1)}, u32[]{:S(2)}, u32[]{:S(2)}) %collective-permute-start.13) | collective-permute-done | bytes 262176 | tf_op jit(solution)/shard_map/ppermute | solution.py:372
  110.5 1.2 %other.1 = (f32[2,2,128,128]{3,2,1,0:T(8,128)S(1)}, bf16[256,2048]{1,0:T(8,128)(2,1)S(1)}) custom-call(bf16[2,4,256,128]{3,2,1,0:T(8,128)(2,1)S(1)} %pad_maximum_fusion.refs_0_, bf16[2,4,256,128]{3,2,1,0:T(8,128)(2,1)S(1)} %collective-permute-done.7.refs_1_, bf16[2,4,256,128]{3,2,1,0:T(8,128)(2,1)S(1)} %pad_maximum_fusion.1.refs_2_, ...), custom_call_target="tpu_custom_call" | custom-call | flops 270000000 | bytes 4000000 | tf_op jit(solution)/shard_map/other/pallas_call | solution.py:317
  111.8 4.8 %collective-permute-start.14 = (f32[2,2,128,128]{3,2,1,0:T(8,128)S(1)}, f32[2,2,128,128]{3,2,1,0:T(8,128)S(1)}, u32[]{:S(2)}, u32[]{:S(2)}) collective-permute-start(f32[2,2,128,128]{3,2,1,0:T(8,128)S(1)} %get-tuple-element.35), channel_id=1, source_target_pairs={{0,16},{1,17},{2,18},{3,19},{4,20},{5,21},{6,22},{7,23},{8,24},{9,... | collective-permute-start | bytes 786440 | tf_op jit(solution)/shard_map/ppermute | solution.py:395
  116.5 1.3 %mine.1 = (f32[2,2,128,128]{3,2,1,0:T(8,128)S(1)}, bf16[4,2,128,128]{3,2,1,0:T(8,128)(2,1)}) custom-call(bf16[2,4,256,128]{3,2,1,0:T(8,128)(2,1)S(1)} %pad_maximum_fusion.refs_0_, bf16[2,4,256,128]{3,2,1,0:T(8,128)(2,1)S(1)} %collective-permute-done.7.refs_1_, bf16[2,4,256,128]{3,2,1,0:T(8,128)(2,1)S(1)} %pad_maximum_fusion.1.refs_2_, ...), custom_call_target="tpu_custom_call" | custom-call | flops 270000000 | bytes 4000000 | tf_op jit(solution)/shard_map/mine/pallas_call | solution.py:329
  117.9 0.9 copy.8
  (15 shorter events, 0.2 us)
Async XLA Ops:
  0.6 11.2 %collective-permute-start = (bf16[512,128]{1,0:T(8,128)(2,1)}, bf16[512,128]{1,0:T(8,128)(2,1)S(1)}, u32[]{:S(2)}, u32[]{:S(2)}) collective-permute-start(bf16[512,128]{1,0:T(8,128)(2,1)} %bitcast.40), channel_id=1, source_target_pairs={{0,0},{1,1},{2,2},{3,3},{4,32},{5,33},{6,34},{7,35},{8,64},{9,65},... | collective-permute-start | bytes 393224 | tf_op jit(solution)/shard_map/ppermute | solution.py:376
  11.8 69.5 %all-to-all-start = ((bf16[128,136,128]{2,1,0:T(8,128)(2,1)}), bf16[128,136,128]{2,1,0:T(8,128)(2,1)}, u32[]{:S(2)}, u32[]{:S(2)}) async-start(bf16[128,136,128]{2,1,0:T(8,128)(2,1)} %bitcast.25), calls=%async_computation | async-start | bytes 8912896 | tf_op jit(solution)/shard_map/all_to_all | solution.py:379
  25.6 51.3 %collective-permute-start.3 = (bf16[256,128]{1,0:T(8,128)(2,1)S(1)}, bf16[256,128]{1,0:T(8,128)(2,1)S(1)}, u32[]{:S(2)}, u32[]{:S(2)}) collective-permute-start(bf16[256,128]{1,0:T(8,128)(2,1)S(1)} %get-tuple-element.40), channel_id=1, source_target_pairs={{0,1},{1,0},{2,3},{3,2},{4,5},{5,4},{6,7},{7,6},{8,9},{9,8},{10,11... | collective-permute-start | bytes 196616 | tf_op jit(solution)/shard_map/ppermute | solution.py:368
  28.3 48.7 %collective-permute-start.1 = (bf16[256,128]{1,0:T(8,128)(2,1)S(1)}, bf16[256,128]{1,0:T(8,128)(2,1)S(1)}, u32[]{:S(2)}, u32[]{:S(2)}) collective-permute-start(bf16[256,128]{1,0:T(8,128)(2,1)S(1)} %get-tuple-element.41), channel_id=1, source_target_pairs={{0,4},{1,5},{2,6},{3,7},{4,0},{5,1},{6,2},{7,3},{8,12},{9,13},{10,... | collective-permute-start | bytes 196616 | tf_op jit(solution)/shard_map/ppermute | solution.py:368
  76.9 4.2 %collective-permute-start.4 = (bf16[2,256,128]{2,1,0:T(8,128)(2,1)S(1)}, bf16[2,256,128]{2,1,0:T(8,128)(2,1)S(1)}, u32[]{:S(2)}, u32[]{:S(2)}) collective-permute-start(bf16[2,256,128]{2,1,0:T(8,128)(2,1)S(1)} %pad_maximum_fusion.7), channel_id=1, source_target_pairs={{0,3},{1,2},{2,1},{3,0},{4,7},{5,6},{6,5},{7,4},{8,11},{9,10},{10,... | collective-permute-start | bytes 393224 | tf_op jit(solution)/shard_map/ppermute | solution.py:372
  77.1 4.2 %collective-permute-start.2 = (bf16[2,256,128]{2,1,0:T(8,128)(2,1)S(1)}, bf16[2,256,128]{2,1,0:T(8,128)(2,1)S(1)}, u32[]{:S(2)}, u32[]{:S(2)}) collective-permute-start(bf16[2,256,128]{2,1,0:T(8,128)(2,1)S(1)} %pad_maximum_fusion.6), channel_id=1, source_target_pairs={{0,12},{1,13},{2,14},{3,15},{4,8},{5,9},{6,10},{7,11},{8,4},{9,5},... | collective-permute-start | bytes 393224 | tf_op jit(solution)/shard_map/ppermute | solution.py:372
  81.3 8.0 %collective-permute-start.5 = (bf16[4,256,128]{2,1,0:T(8,128)(2,1)S(1)}, bf16[4,256,128]{2,1,0:T(8,128)(2,1)S(1)}, u32[]{:S(2)}, u32[]{:S(2)}) collective-permute-start(bf16[4,256,128]{2,1,0:T(8,128)(2,1)S(1)} %pad_maximum_fusion.2), channel_id=1, source_target_pairs={{0,1},{1,0},{2,3},{3,2},{4,5},{5,4},{6,7},{7,6},{8,9},{9,8},{10,11... | collective-permute-start | bytes 786440 | tf_op jit(solution)/shard_map/ppermute | solution.py:368
  82.3 7.1 %collective-permute-start.6 = (bf16[4,256,128]{2,1,0:T(8,128)(2,1)S(1)}, bf16[4,256,128]{2,1,0:T(8,128)(2,1)S(1)}, u32[]{:S(2)}, u32[]{:S(2)}) collective-permute-start(bf16[4,256,128]{2,1,0:T(8,128)(2,1)S(1)} %pad_maximum_fusion.3), channel_id=1, source_target_pairs={{0,4},{1,5},{2,6},{3,7},{4,0},{5,1},{6,2},{7,3},{8,12},{9,13},{10,... | collective-permute-start | bytes 786440 | tf_op jit(solution)/shard_map/ppermute | solution.py:368
  89.5 6.8 %collective-permute-start.10 = (bf16[512,128]{1,0:T(8,128)(2,1)}, bf16[512,128]{1,0:T(8,128)(2,1)S(1)}, u32[]{:S(2)}, u32[]{:S(2)}) collective-permute-start(bf16[512,128]{1,0:T(8,128)(2,1)} %get-tuple-element.29), channel_id=1, source_target_pairs={{0,32},{1,33},{2,34},{3,35},{4,36},{5,37},{6,38},{7,39},{8,40},{9,... | collective-permute-start | bytes 393224 | tf_op jit(solution)/shard_map/ppermute | solution.py:368
  92.0 7.8 %collective-permute-start.9 = (bf16[512,128]{1,0:T(8,128)(2,1)}, bf16[512,128]{1,0:T(8,128)(2,1)S(1)}, u32[]{:S(2)}, u32[]{:S(2)}) collective-permute-start(bf16[512,128]{1,0:T(8,128)(2,1)} %get-tuple-element.28), channel_id=1, source_target_pairs={{8,0},{25,17},{10,2},{27,19},{12,4},{29,21},{14,6},{31,23},{0,8},{... | collective-permute-start | bytes 393224 | tf_op jit(solution)/shard_map/ppermute | solution.py:387
  96.3 11.5 %collective-permute-start.7 = (bf16[2,4,256,128]{3,2,1,0:T(8,128)(2,1)S(1)}, bf16[2,4,256,128]{3,2,1,0:T(8,128)(2,1)S(1)}, u32[]{:S(2)}, u32[]{:S(2)}) collective-permute-start(bf16[2,4,256,128]{3,2,1,0:T(8,128)(2,1)S(1)} %pad_maximum_fusion.refs_0_), channel_id=1, source_target_pairs={{0,3},{1,2},{2,1},{3,0},{4,7},{5,6},{6,5},{7,4},{8,11},{9,10},{10,... | collective-permute-start | bytes 1572872 | tf_op jit(solution)/shard_map/ppermute | solution.py:372
  96.3 11.5 %collective-permute-start.8 = (bf16[2,4,256,128]{3,2,1,0:T(8,128)(2,1)S(1)}, bf16[2,4,256,128]{3,2,1,0:T(8,128)(2,1)S(1)}, u32[]{:S(2)}, u32[]{:S(2)}) collective-permute-start(bf16[2,4,256,128]{3,2,1,0:T(8,128)(2,1)S(1)} %pad_maximum_fusion.1.refs_2_), channel_id=1, source_target_pairs={{0,12},{1,13},{2,14},{3,15},{4,8},{5,9},{6,10},{7,11},{8,4},{9,5},... | collective-permute-start | bytes 1572872 | tf_op jit(solution)/shard_map/ppermute | solution.py:372
  99.9 5.3 %collective-permute-start.12 = (bf16[512,128]{1,0:T(8,128)(2,1)S(1)}, bf16[512,128]{1,0:T(8,128)(2,1)S(1)}, u32[]{:S(2)}, u32[]{:S(2)}) collective-permute-start(bf16[512,128]{1,0:T(8,128)(2,1)S(1)} %collective-permute-done.9), channel_id=1, source_target_pairs={{0,32},{1,33},{2,34},{3,35},{4,36},{5,37},{6,38},{7,39},{8,40},{9,... | collective-permute-start | bytes 393224 | tf_op jit(solution)/shard_map/ppermute | solution.py:368
  100.8 6.9 %collective-permute-start.11 = (bf16[2,512,128]{2,1,0:T(8,128)(2,1)S(1)}, bf16[2,512,128]{2,1,0:T(8,128)(2,1)S(1)}, u32[]{:S(2)}, u32[]{:S(2)}) collective-permute-start(bf16[2,512,128]{2,1,0:T(8,128)(2,1)S(1)} %pad_maximum_fusion.4.refs_4_), channel_id=1, source_target_pairs={{0,96},{1,97},{2,98},{3,99},{4,100},{5,101},{6,102},{7,103},{8,104... | collective-permute-start | bytes 786440 | tf_op jit(solution)/shard_map/ppermute | solution.py:372
  105.2 5.3 %collective-permute-start.13 = (bf16[2,512,128]{2,1,0:T(8,128)(2,1)S(1)}, bf16[2,512,128]{2,1,0:T(8,128)(2,1)S(1)}, u32[]{:S(2)}, u32[]{:S(2)}) collective-permute-start(bf16[2,512,128]{2,1,0:T(8,128)(2,1)S(1)} %pad_maximum_fusion.5.refs_6_), channel_id=1, source_target_pairs={{0,96},{1,97},{2,98},{3,99},{4,100},{5,101},{6,102},{7,103},{8,104... | collective-permute-start | bytes 786440 | tf_op jit(solution)/shard_map/ppermute | solution.py:372
  111.8 6.1 %collective-permute-start.14 = (f32[2,2,128,128]{3,2,1,0:T(8,128)S(1)}, f32[2,2,128,128]{3,2,1,0:T(8,128)S(1)}, u32[]{:S(2)}, u32[]{:S(2)}) collective-permute-start(f32[2,2,128,128]{3,2,1,0:T(8,128)S(1)} %get-tuple-element.35), channel_id=1, source_target_pairs={{0,16},{1,17},{2,18},{3,19},{4,20},{5,21},{6,22},{7,23},{8,24},{9,... | collective-permute-start | bytes 786440 | tf_op jit(solution)/shard_map/ppermute | solution.py:395

commit v4 on v3

--- a/solution.py
+++ b/solution.py
@@ -56,8 +56,8 @@
     for copy in small + copies:
         copy.start()
     start = start_ref[0]
-    tail_row = lax.broadcasted_iota(jnp.int32, (8, NB), 0)
-    tail = jnp.where(tail_row == 1, start.astype(F32), 0.0)
+    tail_row = lax.broadcasted_iota(jnp.int32, (SUB, NB), 0)
+    my_lanes = lax.broadcasted_iota(jnp.int32, (SUB, NB), 1) // TILE == lax.rem(lax.axis_index("col"), NB // TILE)
     eye = upper(False) & ~upper(True)
     for copy in small:
         copy.wait()
@@ -66,14 +66,19 @@
 
     slots = {}
 
-    def send(kind, col, block, last_rows):
+    def send(kind, near, col, block, extra=None, now=True):
         slot = slots.setdefault((kind, col), len(slots))
         if block is not None:
             outgoing[slot, 0:TILES] = block.reshape(TILES, SUB, NB).astype(BF16)
-        if last_rows is None:
+        if not now:
             return
-        outgoing[slot, TILES] = last_rows.astype(BF16)
-        column = lax.rem(start + col, NCOL)
+        block_col = lax.rem(start + col, NBLK)
+        half = block_col // LOC
+        last = jnp.where((tail_row == 0) & my_lanes, (half + (0 if near else 2)).astype(F32), 0.0)
+        if extra is not None:
+            last = jnp.where(tail_row == half + 1, extra, last)
+        outgoing[slot, TILES] = last.astype(BF16)
+        column = lax.rem(block_col, NCOL)
         target = home(kind, column) * NCOL + column
         pltpu.make_async_copy(outgoing.at[slot], out_ref.at[target], out_sem).start()
 
@@ -99,16 +104,16 @@
                         diagonal[a] = block
                     elif gap == 0:
                         low = a - LOC // 2
-                        send(0, low, jnp.where(upper(False), diagonal[low], block), tail)
+                        send(0, False, low, jnp.where(upper(False), diagonal[low], block))
                         extra = jnp.sum(jnp.where(eye, block, 0.0), axis=0, keepdims=True)
-                        send(0, a, None, jnp.where(tail_row == 0, extra, tail))
+                        send(0, True, a, None, extra)
                     elif gap < LOC // 2:
-                        send(gap, b, block, tail)
+                        send(gap, True, b, block)
                     elif gap == LOC // 2:
-                        send(0, b, block, None)
+                        send(0, True, b, block, now=False)
                     else:
                         listed = jnp.max(jnp.where(codes == a * LOC + b, 1.0, 0.0), axis=1, keepdims=True)
-                        send(LOC - gap, a, block * listed, tail)
+                        send(LOC - gap, False, a, block * listed)
     pltpu.make_async_copy(outgoing, out_ref, out_sem).wait()
 
 
@@ -151,26 +156,17 @@
 
 def sum_kernel(in_ref, direct_ref, turned_ref, total, extra_total):
     step = pl.program_id(0)
-    _, col, kind = place()
-    near = jnp.where(kind == 0, LOC // 2, kind)
 
     @pl.when(step == 0)
     def _():
         total[...] = jnp.zeros_like(total)
         extra_total[...] = jnp.zeros_like(extra_total)
 
-    ends = in_ref[:, NB:ROWS, :].astype(F32)
-    start = ends[:, 1, :].astype(jnp.int32)
-    position = (col + NBLK - start) & (LOC - 1)
-    half = ((start + position) & (NBLK - 1)) // LOC
-    key = jnp.where(position >= near, 0, 2) + half
-    for k in range(2):
-        extra_total[k : k + 1, :] += jnp.sum(jnp.where(key == k, ends[:, 0, :], 0.0), axis=0, keepdims=True)
     depth = CHUNK * TILE
-    sublane = lax.broadcasted_iota(jnp.int32, (CHUNK, depth), 0)
-    lane = lax.broadcasted_iota(jnp.int32, (CHUNK, depth), 1)
-    keys = jnp.concatenate([key] * (depth // NB), axis=1)
-    lane_key = jnp.sum(jnp.where(sublane == lane // TILE, keys, 0), axis=0, keepdims=True)
+    group = NB // TILE
+    lasts = [jnp.sum(in_ref[m : m + group, NB:ROWS, :].astype(F32), axis=0) for m in range(0, CHUNK, group)]
+    extra_total[...] += sum(lasts)
+    lane_key = jnp.concatenate([last[0:1, :] for last in lasts], axis=1).astype(jnp.int32)
     row = lax.broadcasted_iota(jnp.int32, (4 * TILE, depth), 0)
     lane = lax.broadcasted_iota(jnp.int32, (4 * TILE, depth), 1)
     chosen = jnp.where((row // TILE == lane_key) & ((row & (TILE - 1)) == (lane & (TILE - 1))), 1.0, 0.0).astype(BF16)
@@ -189,7 +185,7 @@
                 [total[k * TILE : (k + 1) * TILE, t * NB : (t + 1) * NB] for t in range(NB // TILE)], axis=0
             )
             if k >= 2:
-                plain = plain + jnp.where(eye, extra_total[k - 2 : k - 1, :], 0.0)
+                plain = plain + jnp.where(eye, extra_total[k - 1 : k, :], 0.0)
             flipped = plain.T
             rows = pl.ds(k * NB, NB)
             direct_ref[rows, :] = (flipped if k < 2 else plain).astype(BF16)
@@ -204,7 +200,7 @@
         grid=(NDEV // CHUNK,),
         in_specs=[pl.BlockSpec((CHUNK, ROWS, NB), lambda i: (i, 0, 0))],
         out_specs=(pl.BlockSpec((HELD, NB), lambda i: (0, 0)),) * 2,
-        scratch_shapes=[pltpu.VMEM((4 * TILE, NB // TILE * NB), F32), pltpu.VMEM((2, NB), F32)],
+        scratch_shapes=[pltpu.VMEM((4 * TILE, NB // TILE * NB), F32), pltpu.VMEM((SUB, NB), F32)],
         cost_estimate=pl.CostEstimate(flops=300_000_000, bytes_accessed=4_700_000, transcendentals=0),
         name="sums",
     )(incoming)
@@ -259,7 +255,7 @@
     def add_up(steps):
         part = jnp.zeros((2 * NB, 2 * NB), F32)
         for z_step in range(4):
-            start = pl.multiple_of(ring_place(z, core, z_step) * (2 * depth), depth)
+            start = pl.multiple_of(wrap(ring_place(z, core, z_step) + 2, 4) * (2 * depth), depth)
             above = [upper_panel[k // 2][k % 2, z_step] for k in steps]
             below = [lower_panel[z_step // 2][z_step % 2, k] for k in steps]
             part = part + jnp.dot(
@@ -342,7 +338,7 @@
 
 
 PLACES = [(y, core, col) for y in range(4) for core in range(2) for col in range(NCOL)]
-TO_ROW = [(device(y, core, col), device(col // 4, core, 4 * y + col % 4)) for y, core, col in PLACES]
+TO_ROW = [(device(y, core, col), device(col // 4, core, (y + 2) % 4 * 4 + col % 4)) for y, core, col in PLACES]
 TO_OTHER_CORE = [(device(y, core, col), device(y, 1 - core, col)) for y, core, col in PLACES]
 
 

time: 119 us -> 117 us (0.983)
  starting transfers between devices: 38.9 us -> 37.1 us
    all_to_all x1, starting transfers between devices: 13.7 us -> 8.32 us  [shards(): lax.all_to_all(outgoing, AXES, split_axis=0, concat_axis=0, tiled=True)]
    ppermute x1, starting transfers between devices: 1.56 us -> 4.49 us  [shards(): own = lax.ppermute(coefficients.reshape(4 * NB, NB), AXES, TO_ROW)]
  transfers between devices with their start and end apart: 16 -> 16, of which waited for: 7 -> 8; matrix products, arithmetic and copies ran while one was open for 1% -> 1% of each run, Pallas kernels for 12% -> 12%
where the time goes in v4:
time: 117 us; the launch traced here: 116 us
  waiting for transfers between devices  60.7 us (52%)
  starting transfers between devices  37.1 us (32%)
  Pallas kernels  15.1 us (13%)
  between operations  1.41 us (1%)
  other arithmetic  1.17 us (1%)
    ppermute x6, waiting for transfers between devices, first_near(): return jnp.stack([value, lax.ppermute(value, AXES, exchange(axis, 0))])  50.1 us
    ppermute x6, starting transfers between devices, first_near(): return jnp.stack([value, lax.ppermute(value, AXES, exchange(axis, 0))])  12.9 us
    pallas_call x1, Pallas kernels, messages(): pl.pallas_call(message_kernel, out_shape=pltpu.HBM((NDEV, TILES + 1, SUB,...  9.01 us
    all_to_all x1, starting transfers between devices, shards(): lax.all_to_all(outgoing, AXES, split_axis=0, concat_axis=0, tiled=True)  8.32 us
    ppermute x6, waiting for transfers between devices, second_near(): return lax.ppermute(pair, AXES, exchange(axis, 1))  7.94 us
    ppermute x1, starting transfers between devices, shards(): theirs = lax.ppermute(other, AXES, TO_OTHER_CORE)  4.87 us
    ppermute x1, starting transfers between devices, shards(): turned = lax.ppermute(turned, AXES, from_partner())  4.87 us
    ppermute x1, starting transfers between devices, shards(): own = lax.ppermute(coefficients.reshape(4 * NB, NB), AXES, TO_ROW)  4.49 us
  transfers between devices with their start and end apart: 16, of which 8 were waited for; matrix products, arithmetic and copies ran while one was open for 1% of the time, Pallas kernels for 12%

profile of v4, /device:TPU:1, one launch (start us, length us, event | category | flops | bytes accessed | tf_op | source)
XLA Modules:
  0.0 116.4 jit_solution(5347495592381684613)
XLA Ops:
  0.6 4.5 %collective-permute-start = (bf16[512,128]{1,0:T(8,128)(2,1)}, bf16[512,128]{1,0:T(8,128)(2,1)S(1)}, u32[]{:S(2)}, u32[]{:S(2)}) collective-permute-start(bf16[512,128]{1,0:T(8,128)(2,1)} %bitcast.40), channel_id=1, source_target_pairs={{0,8},{1,9},{2,10},{3,11},{4,40},{5,41},{6,42},{7,43},{8,72},{9,73... | collective-permute-start | bytes 393224 | tf_op jit(solution)/shard_map/ppermute | solution.py:372
  5.8 9.0 %blocks.1 = bf16[128,17,8,128]{3,2,1,0:T(8,128)(2,1)} custom-call(s32[1]{0:T(128)S(6)} %copy.9.start_ref, s32[2,228]{1,0:T(2,128)} %bitcast.41, f32[1,1024]{1,0:T(1,128)} %potential_ref.1, bf16[2048,1024]{1,0:T(8,128)(2,1)} %bitcast.38), custom_call_target="tpu_custom_call" | custom-call | flops 5000000000 | bytes 9000000 | tf_op jit(solution)/shard_map/blocks/pallas_call | solution.py:127
  14.8 0.0 collective-permute-done
  14.8 8.3 %all-to-all-start = ((bf16[128,136,128]{2,1,0:T(8,128)(2,1)}), bf16[128,136,128]{2,1,0:T(8,128)(2,1)}, u32[]{:S(2)}, u32[]{:S(2)}) async-start(bf16[128,136,128]{2,1,0:T(8,128)(2,1)} %bitcast.25), calls=%async_computation | async-start | bytes 8912896 | tf_op jit(solution)/shard_map/all_to_all | solution.py:375
  23.2 2.7 %collective-permute-start.3 = (bf16[256,128]{1,0:T(8,128)(2,1)S(1)}, bf16[256,128]{1,0:T(8,128)(2,1)S(1)}, u32[]{:S(2)}, u32[]{:S(2)}) collective-permute-start(bf16[256,128]{1,0:T(8,128)(2,1)S(1)} %get-tuple-element.40), channel_id=1, source_target_pairs={{0,1},{1,0},{2,3},{3,2},{4,5},{5,4},{6,7},{7,6},{8,9},{9,8},{10,11... | collective-permute-start | bytes 196616 | tf_op jit(solution)/shard_map/ppermute | solution.py:364
  25.9 3.1 %collective-permute-start.1 = (bf16[256,128]{1,0:T(8,128)(2,1)S(1)}, bf16[256,128]{1,0:T(8,128)(2,1)S(1)}, u32[]{:S(2)}, u32[]{:S(2)}) collective-permute-start(bf16[256,128]{1,0:T(8,128)(2,1)S(1)} %get-tuple-element.41), channel_id=1, source_target_pairs={{0,4},{1,5},{2,6},{3,7},{4,0},{5,1},{6,2},{7,3},{8,12},{9,13},{10,... | collective-permute-start | bytes 196616 | tf_op jit(solution)/shard_map/ppermute | solution.py:364
  29.0 45.5 %collective-permute-done.3 = bf16[256,128]{1,0:T(8,128)(2,1)S(1)} collective-permute-done((bf16[256,128]{1,0:T(8,128)(2,1)S(1)}, bf16[256,128]{1,0:T(8,128)(2,1)S(1)}, u32[]{:S(2)}, u32[]{:S(2)}) %collective-permute-start.3) | collective-permute-done | bytes 65568 | tf_op jit(solution)/shard_map/ppermute | solution.py:364
  74.5 0.1 collective-permute-start.4
  74.6 1.4 %collective-permute-start.2 = (bf16[2,256,128]{2,1,0:T(8,128)(2,1)S(1)}, bf16[2,256,128]{2,1,0:T(8,128)(2,1)S(1)}, u32[]{:S(2)}, u32[]{:S(2)}) collective-permute-start(bf16[2,256,128]{2,1,0:T(8,128)(2,1)S(1)} %pad_maximum_fusion.6), channel_id=1, source_target_pairs={{0,12},{1,13},{2,14},{3,15},{4,8},{5,9},{6,10},{7,11},{8,4},{9,5},... | collective-permute-start | bytes 393224 | tf_op jit(solution)/shard_map/ppermute | solution.py:368
  76.0 2.6 %collective-permute-done.4 = bf16[2,256,128]{2,1,0:T(8,128)(2,1)S(1)} collective-permute-done((bf16[2,256,128]{2,1,0:T(8,128)(2,1)S(1)}, bf16[2,256,128]{2,1,0:T(8,128)(2,1)S(1)}, u32[]{:S(2)}, u32[]{:S(2)}) %collective-permute-start.4) | collective-permute-done | bytes 131104 | tf_op jit(solution)/shard_map/ppermute | solution.py:368
  78.7 0.1 collective-permute-done.2
  78.9 1.0 collective-permute-start.5
  79.9 2.7 %collective-permute-start.6 = (bf16[4,256,128]{2,1,0:T(8,128)(2,1)S(1)}, bf16[4,256,128]{2,1,0:T(8,128)(2,1)S(1)}, u32[]{:S(2)}, u32[]{:S(2)}) collective-permute-start(bf16[4,256,128]{2,1,0:T(8,128)(2,1)S(1)} %pad_maximum_fusion.3), channel_id=1, source_target_pairs={{0,4},{1,5},{2,6},{3,7},{4,0},{5,1},{6,2},{7,3},{8,12},{9,13},{10,... | collective-permute-start | bytes 786440 | tf_op jit(solution)/shard_map/ppermute | solution.py:364
  82.5 3.6 %sums.1 = (bf16[512,128]{1,0:T(8,128)(2,1)}, bf16[512,128]{1,0:T(8,128)(2,1)}) custom-call(bf16[128,136,128]{2,1,0:T(8,128)(2,1)} %all-to-all-done.in_ref), custom_call_target="tpu_custom_call" | custom-call | flops 300000000 | bytes 4700000 | tf_op jit(solution)/shard_map/sums/pallas_call | solution.py:197
  86.1 0.1 pad_maximum_fusion.refs_0_
  86.2 0.1 collective-permute-done.6
  86.3 0.1 pad_maximum_fusion.1.refs_2_
  86.4 2.6 %collective-permute-start.10 = (bf16[512,128]{1,0:T(8,128)(2,1)}, bf16[512,128]{1,0:T(8,128)(2,1)S(1)}, u32[]{:S(2)}, u32[]{:S(2)}) collective-permute-start(bf16[512,128]{1,0:T(8,128)(2,1)} %get-tuple-element.29), channel_id=1, source_target_pairs={{0,32},{1,33},{2,34},{3,35},{4,36},{5,37},{6,38},{7,39},{8,40},{9,... | collective-permute-start | bytes 393224 | tf_op jit(solution)/shard_map/ppermute | solution.py:364
  88.9 4.9 %collective-permute-start.9 = (bf16[512,128]{1,0:T(8,128)(2,1)}, bf16[512,128]{1,0:T(8,128)(2,1)S(1)}, u32[]{:S(2)}, u32[]{:S(2)}) collective-permute-start(bf16[512,128]{1,0:T(8,128)(2,1)} %get-tuple-element.28), channel_id=1, source_target_pairs={{8,0},{25,17},{10,2},{27,19},{12,4},{29,21},{14,6},{31,23},{0,8},{... | collective-permute-start | bytes 393224 | tf_op jit(solution)/shard_map/ppermute | solution.py:383
  93.8 0.0 collective-permute-start.7
  93.8 0.0 collective-permute-start.8
  93.8 0.9 pad_maximum_fusion.4.refs_4_
  94.8 2.7 %collective-permute-done.9 = bf16[512,128]{1,0:T(8,128)(2,1)S(1)} collective-permute-done((bf16[512,128]{1,0:T(8,128)(2,1)}, bf16[512,128]{1,0:T(8,128)(2,1)S(1)}, u32[]{:S(2)}, u32[]{:S(2)}) %collective-permute-start.9) | collective-permute-done | bytes 131104 | tf_op jit(solution)/shard_map/ppermute | solution.py:383
  97.4 0.9 collective-permute-start.12
  98.3 4.4 %collective-permute-done.12 = bf16[512,128]{1,0:T(8,128)(2,1)S(1)} collective-permute-done((bf16[512,128]{1,0:T(8,128)(2,1)S(1)}, bf16[512,128]{1,0:T(8,128)(2,1)S(1)}, u32[]{:S(2)}, u32[]{:S(2)}) %collective-permute-start.12) | collective-permute-done | bytes 131104 | tf_op jit(solution)/shard_map/ppermute | solution.py:364
  102.8 0.1 collective-permute-start.13
  102.9 2.4 %collective-permute-done.11.refs_5_ = bf16[2,512,128]{2,1,0:T(8,128)(2,1)S(1)} collective-permute-done((bf16[2,512,128]{2,1,0:T(8,128)(2,1)S(1)}, bf16[2,512,128]{2,1,0:T(8,128)(2,1)S(1)}, u32[]{:S(2)}, u32[]{:S(2)}) %collective-permute-start.11) | collective-permute-done | bytes 262176 | tf_op jit(solution)/shard_map/ppermute | solution.py:368
  105.3 2.8 %collective-permute-done.13.refs_7_ = bf16[2,512,128]{2,1,0:T(8,128)(2,1)S(1)} collective-permute-done((bf16[2,512,128]{2,1,0:T(8,128)(2,1)S(1)}, bf16[2,512,128]{2,1,0:T(8,128)(2,1)S(1)}, u32[]{:S(2)}, u32[]{:S(2)}) %collective-permute-start.13) | collective-permute-done | bytes 262176 | tf_op jit(solution)/shard_map/ppermute | solution.py:368
  108.1 1.2 %other.1 = (f32[2,2,128,128]{3,2,1,0:T(8,128)S(1)}, bf16[256,2048]{1,0:T(8,128)(2,1)S(1)}) custom-call(bf16[2,4,256,128]{3,2,1,0:T(8,128)(2,1)S(1)} %pad_maximum_fusion.refs_0_, bf16[2,4,256,128]{3,2,1,0:T(8,128)(2,1)S(1)} %collective-permute-done.7.refs_1_, bf16[2,4,256,128]{3,2,1,0:T(8,128)(2,1)S(1)} %pad_maximum_fusion.1.refs_2_, ...), custom_call_target="tpu_custom_call" | custom-call | flops 270000000 | bytes 4000000 | tf_op jit(solution)/shard_map/other/pallas_call | solution.py:313
  109.3 4.9 %collective-permute-start.14 = (f32[2,2,128,128]{3,2,1,0:T(8,128)S(1)}, f32[2,2,128,128]{3,2,1,0:T(8,128)S(1)}, u32[]{:S(2)}, u32[]{:S(2)}) collective-permute-start(f32[2,2,128,128]{3,2,1,0:T(8,128)S(1)} %get-tuple-element.35), channel_id=1, source_target_pairs={{0,16},{1,17},{2,18},{3,19},{4,20},{5,21},{6,22},{7,23},{8,24},{9,... | collective-permute-start | bytes 786440 | tf_op jit(solution)/shard_map/ppermute | solution.py:391
  114.2 1.3 %mine.1 = (f32[2,2,128,128]{3,2,1,0:T(8,128)S(1)}, bf16[4,2,128,128]{3,2,1,0:T(8,128)(2,1)}) custom-call(bf16[2,4,256,128]{3,2,1,0:T(8,128)(2,1)S(1)} %pad_maximum_fusion.refs_0_, bf16[2,4,256,128]{3,2,1,0:T(8,128)(2,1)S(1)} %collective-permute-done.7.refs_1_, bf16[2,4,256,128]{3,2,1,0:T(8,128)(2,1)S(1)} %pad_maximum_fusion.1.refs_2_, ...), custom_call_target="tpu_custom_call" | custom-call | flops 270000000 | bytes 4000000 | tf_op jit(solution)/shard_map/mine/pallas_call | solution.py:325
  115.5 0.9 copy.8
  (15 shorter events, 0.2 us)
Async XLA Ops:
  0.6 14.2 %collective-permute-start = (bf16[512,128]{1,0:T(8,128)(2,1)}, bf16[512,128]{1,0:T(8,128)(2,1)S(1)}, u32[]{:S(2)}, u32[]{:S(2)}) collective-permute-start(bf16[512,128]{1,0:T(8,128)(2,1)} %bitcast.40), channel_id=1, source_target_pairs={{0,8},{1,9},{2,10},{3,11},{4,40},{5,41},{6,42},{7,43},{8,72},{9,73... | collective-permute-start | bytes 393224 | tf_op jit(solution)/shard_map/ppermute | solution.py:372
  14.8 64.0 %all-to-all-start = ((bf16[128,136,128]{2,1,0:T(8,128)(2,1)}), bf16[128,136,128]{2,1,0:T(8,128)(2,1)}, u32[]{:S(2)}, u32[]{:S(2)}) async-start(bf16[128,136,128]{2,1,0:T(8,128)(2,1)} %bitcast.25), calls=%async_computation | async-start | bytes 8912896 | tf_op jit(solution)/shard_map/all_to_all | solution.py:375
  23.2 51.3 %collective-permute-start.3 = (bf16[256,128]{1,0:T(8,128)(2,1)S(1)}, bf16[256,128]{1,0:T(8,128)(2,1)S(1)}, u32[]{:S(2)}, u32[]{:S(2)}) collective-permute-start(bf16[256,128]{1,0:T(8,128)(2,1)S(1)} %get-tuple-element.40), channel_id=1, source_target_pairs={{0,1},{1,0},{2,3},{3,2},{4,5},{5,4},{6,7},{7,6},{8,9},{9,8},{10,11... | collective-permute-start | bytes 196616 | tf_op jit(solution)/shard_map/ppermute | solution.py:364
  25.9 48.7 %collective-permute-start.1 = (bf16[256,128]{1,0:T(8,128)(2,1)S(1)}, bf16[256,128]{1,0:T(8,128)(2,1)S(1)}, u32[]{:S(2)}, u32[]{:S(2)}) collective-permute-start(bf16[256,128]{1,0:T(8,128)(2,1)S(1)} %get-tuple-element.41), channel_id=1, source_target_pairs={{0,4},{1,5},{2,6},{3,7},{4,0},{5,1},{6,2},{7,3},{8,12},{9,13},{10,... | collective-permute-start | bytes 196616 | tf_op jit(solution)/shard_map/ppermute | solution.py:364
  74.5 4.2 %collective-permute-start.4 = (bf16[2,256,128]{2,1,0:T(8,128)(2,1)S(1)}, bf16[2,256,128]{2,1,0:T(8,128)(2,1)S(1)}, u32[]{:S(2)}, u32[]{:S(2)}) collective-permute-start(bf16[2,256,128]{2,1,0:T(8,128)(2,1)S(1)} %pad_maximum_fusion.7), channel_id=1, source_target_pairs={{0,3},{1,2},{2,1},{3,0},{4,7},{5,6},{6,5},{7,4},{8,11},{9,10},{10,... | collective-permute-start | bytes 393224 | tf_op jit(solution)/shard_map/ppermute | solution.py:368
  74.6 4.2 %collective-permute-start.2 = (bf16[2,256,128]{2,1,0:T(8,128)(2,1)S(1)}, bf16[2,256,128]{2,1,0:T(8,128)(2,1)S(1)}, u32[]{:S(2)}, u32[]{:S(2)}) collective-permute-start(bf16[2,256,128]{2,1,0:T(8,128)(2,1)S(1)} %pad_maximum_fusion.6), channel_id=1, source_target_pairs={{0,12},{1,13},{2,14},{3,15},{4,8},{5,9},{6,10},{7,11},{8,4},{9,5},... | collective-permute-start | bytes 393224 | tf_op jit(solution)/shard_map/ppermute | solution.py:368
  78.9 7.3 %collective-permute-start.5 = (bf16[4,256,128]{2,1,0:T(8,128)(2,1)S(1)}, bf16[4,256,128]{2,1,0:T(8,128)(2,1)S(1)}, u32[]{:S(2)}, u32[]{:S(2)}) collective-permute-start(bf16[4,256,128]{2,1,0:T(8,128)(2,1)S(1)} %pad_maximum_fusion.2), channel_id=1, source_target_pairs={{0,1},{1,0},{2,3},{3,2},{4,5},{5,4},{6,7},{7,6},{8,9},{9,8},{10,11... | collective-permute-start | bytes 786440 | tf_op jit(solution)/shard_map/ppermute | solution.py:364
  79.9 6.4 %collective-permute-start.6 = (bf16[4,256,128]{2,1,0:T(8,128)(2,1)S(1)}, bf16[4,256,128]{2,1,0:T(8,128)(2,1)S(1)}, u32[]{:S(2)}, u32[]{:S(2)}) collective-permute-start(bf16[4,256,128]{2,1,0:T(8,128)(2,1)S(1)} %pad_maximum_fusion.3), channel_id=1, source_target_pairs={{0,4},{1,5},{2,6},{3,7},{4,0},{5,1},{6,2},{7,3},{8,12},{9,13},{10,... | collective-permute-start | bytes 786440 | tf_op jit(solution)/shard_map/ppermute | solution.py:364
  86.4 7.5 %collective-permute-start.10 = (bf16[512,128]{1,0:T(8,128)(2,1)}, bf16[512,128]{1,0:T(8,128)(2,1)S(1)}, u32[]{:S(2)}, u32[]{:S(2)}) collective-permute-start(bf16[512,128]{1,0:T(8,128)(2,1)} %get-tuple-element.29), channel_id=1, source_target_pairs={{0,32},{1,33},{2,34},{3,35},{4,36},{5,37},{6,38},{7,39},{8,40},{9,... | collective-permute-start | bytes 393224 | tf_op jit(solution)/shard_map/ppermute | solution.py:364
  88.9 8.5 %collective-permute-start.9 = (bf16[512,128]{1,0:T(8,128)(2,1)}, bf16[512,128]{1,0:T(8,128)(2,1)S(1)}, u32[]{:S(2)}, u32[]{:S(2)}) collective-permute-start(bf16[512,128]{1,0:T(8,128)(2,1)} %get-tuple-element.28), channel_id=1, source_target_pairs={{8,0},{25,17},{10,2},{27,19},{12,4},{29,21},{14,6},{31,23},{0,8},{... | collective-permute-start | bytes 393224 | tf_op jit(solution)/shard_map/ppermute | solution.py:383
  93.8 11.4 %collective-permute-start.7 = (bf16[2,4,256,128]{3,2,1,0:T(8,128)(2,1)S(1)}, bf16[2,4,256,128]{3,2,1,0:T(8,128)(2,1)S(1)}, u32[]{:S(2)}, u32[]{:S(2)}) collective-permute-start(bf16[2,4,256,128]{3,2,1,0:T(8,128)(2,1)S(1)} %pad_maximum_fusion.refs_0_), channel_id=1, source_target_pairs={{0,3},{1,2},{2,1},{3,0},{4,7},{5,6},{6,5},{7,4},{8,11},{9,10},{10,... | collective-permute-start | bytes 1572872 | tf_op jit(solution)/shard_map/ppermute | solution.py:368
  93.8 11.4 %collective-permute-start.8 = (bf16[2,4,256,128]{3,2,1,0:T(8,128)(2,1)S(1)}, bf16[2,4,256,128]{3,2,1,0:T(8,128)(2,1)S(1)}, u32[]{:S(2)}, u32[]{:S(2)}) collective-permute-start(bf16[2,4,256,128]{3,2,1,0:T(8,128)(2,1)S(1)} %pad_maximum_fusion.1.refs_2_), channel_id=1, source_target_pairs={{0,12},{1,13},{2,14},{3,15},{4,8},{5,9},{6,10},{7,11},{8,4},{9,5},... | collective-permute-start | bytes 1572872 | tf_op jit(solution)/shard_map/ppermute | solution.py:368
  97.4 5.3 %collective-permute-start.12 = (bf16[512,128]{1,0:T(8,128)(2,1)S(1)}, bf16[512,128]{1,0:T(8,128)(2,1)S(1)}, u32[]{:S(2)}, u32[]{:S(2)}) collective-permute-start(bf16[512,128]{1,0:T(8,128)(2,1)S(1)} %collective-permute-done.9), channel_id=1, source_target_pairs={{0,32},{1,33},{2,34},{3,35},{4,36},{5,37},{6,38},{7,39},{8,40},{9,... | collective-permute-start | bytes 393224 | tf_op jit(solution)/shard_map/ppermute | solution.py:364
  98.3 6.9 %collective-permute-start.11 = (bf16[2,512,128]{2,1,0:T(8,128)(2,1)S(1)}, bf16[2,512,128]{2,1,0:T(8,128)(2,1)S(1)}, u32[]{:S(2)}, u32[]{:S(2)}) collective-permute-start(bf16[2,512,128]{2,1,0:T(8,128)(2,1)S(1)} %pad_maximum_fusion.4.refs_4_), channel_id=1, source_target_pairs={{0,96},{1,97},{2,98},{3,99},{4,100},{5,101},{6,102},{7,103},{8,104... | collective-permute-start | bytes 786440 | tf_op jit(solution)/shard_map/ppermute | solution.py:368
  102.8 5.3 %collective-permute-start.13 = (bf16[2,512,128]{2,1,0:T(8,128)(2,1)S(1)}, bf16[2,512,128]{2,1,0:T(8,128)(2,1)S(1)}, u32[]{:S(2)}, u32[]{:S(2)}) collective-permute-start(bf16[2,512,128]{2,1,0:T(8,128)(2,1)S(1)} %pad_maximum_fusion.5.refs_6_), channel_id=1, source_target_pairs={{0,96},{1,97},{2,98},{3,99},{4,100},{5,101},{6,102},{7,103},{8,104... | collective-permute-start | bytes 786440 | tf_op jit(solution)/shard_map/ppermute | solution.py:368
  109.3 6.2 %collective-permute-start.14 = (f32[2,2,128,128]{3,2,1,0:T(8,128)S(1)}, f32[2,2,128,128]{3,2,1,0:T(8,128)S(1)}, u32[]{:S(2)}, u32[]{:S(2)}) collective-permute-start(f32[2,2,128,128]{3,2,1,0:T(8,128)S(1)} %get-tuple-element.35), channel_id=1, source_target_pairs={{0,16},{1,17},{2,18},{3,19},{4,20},{5,21},{6,22},{7,23},{8,24},{9,... | collective-permute-start | bytes 786440 | tf_op jit(solution)/shard_map/ppermute | solution.py:391

commit v5 on v4

--- a/solution.py
+++ b/solution.py
@@ -82,21 +82,22 @@
         target = home(kind, column) * NCOL + column
         pltpu.make_async_copy(outgoing.at[slot], out_ref.at[target], out_sem).start()
 
-    for right in range(steps):
-        copies[right].wait()
-        right_rows = pl.ds(right * step_rows, step_rows)
-        right_side = held[right_rows, :]
-        weighted[right_rows, :] = (right_side.astype(F32) * scale).astype(BF16)
-        for left in range(right + 1):
+    wide = 2 * step_rows
+    for right in range(steps // 2):
+        for half_step in (2 * right, 2 * right + 1):
+            copies[half_step].wait()
+            rows = pl.ds(half_step * step_rows, step_rows)
+            weighted[rows, :] = (held[rows, :].astype(F32) * scale).astype(BF16)
+        for left in range(2 * right + 2):
             tile = lax.dot_general(
                 weighted[pl.ds(left * step_rows, step_rows), :],
-                right_side,
+                held[pl.ds(right * wide, wide), :],
                 (((1,), (1,)), ((), ())),
                 preferred_element_type=F32,
             )
             for a in (2 * left, 2 * left + 1):
-                for b in (2 * right, 2 * right + 1):
-                    block = tile[(a % 2) * NB : (a % 2 + 1) * NB, (b % 2) * NB : (b % 2 + 1) * NB]
+                for b in range(4 * right, 4 * right + 4):
+                    block = tile[(a % 2) * NB : (a % 2 + 1) * NB, (b % 4) * NB : (b % 4 + 1) * NB]
                     gap = b - a
                     if gap < 0:
                         continue
@@ -383,7 +384,6 @@
     turned = lax.ppermute(turned, AXES, from_partner())
     direct = first_near(direct, "y")
     panels = above, second_near(above, "x"), below, second_near(below, "z")
-    turned, direct = lax.optimization_barrier((turned, direct))
     turned = first_near(turned, "y")
     direct = direct, second_near(direct, "y")
     turned = turned, second_near(turned, "y")

time: 117 us -> 116 us (level)
  waiting for transfers between devices: 60.7 us -> 57 us
  starting transfers between devices: 37.1 us -> 39.6 us
    ppermute x1, waiting for transfers between devices: 2.68 us -> 0.01 us  [shards(): turned = lax.ppermute(turned, AXES, from_partner())]
    ppermute x6, waiting for transfers between devices: 50.1 us -> 48 us  [first_near(): return jnp.stack([value, lax.ppermute(value, AXES, exchange(axis, 0))])]
    ppermute x6, starting transfers between devices: 1.61 us -> 3.5 us  [second_near(): return lax.ppermute(pair, AXES, exchange(axis, 1))]
where the time goes in v5:
time: 116 us; the launch traced here: 115 us
  waiting for transfers between devices  57 us (49%)
  starting transfers between devices  39.6 us (34%)
  Pallas kernels  14.7 us (13%)
  between operations  1.4 us (1%)
  other arithmetic  1.17 us (1%)
    ppermute x6, waiting for transfers between devices, first_near(): return jnp.stack([value, lax.ppermute(value, AXES, exchange(axis, 0))])  48 us
    ppermute x6, starting transfers between devices, first_near(): return jnp.stack([value, lax.ppermute(value, AXES, exchange(axis, 0))])  13.6 us
    ppermute x6, waiting for transfers between devices, second_near(): return lax.ppermute(pair, AXES, exchange(axis, 1))  9.01 us
    pallas_call x1, Pallas kernels, messages(): pl.pallas_call(message_kernel, out_shape=pltpu.HBM((NDEV, TILES + 1, SUB,...  8.62 us
    all_to_all x1, starting transfers between devices, shards(): lax.all_to_all(outgoing, AXES, split_axis=0, concat_axis=0, tiled=True)  8.34 us
    ppermute x1, starting transfers between devices, shards(): turned = lax.ppermute(turned, AXES, from_partner())  5.91 us
    ppermute x1, starting transfers between devices, shards(): own = lax.ppermute(coefficients.reshape(4 * NB, NB), AXES, TO_ROW)  4.49 us
    ppermute x1, starting transfers between devices, shards(): theirs = lax.ppermute(other, AXES, TO_OTHER_CORE)  3.81 us
  transfers between devices with their start and end apart: 16, of which 8 were waited for; matrix products, arithmetic and copies ran while one was open for 1% of the time, Pallas kernels for 12%

profile of v5, /device:TPU:1, one launch (start us, length us, event | category | flops | bytes accessed | tf_op | source)
XLA Modules:
  0.0 114.8 jit_solution(14852037951807446828)
XLA Ops:
  0.6 4.5 %collective-permute-start = (bf16[512,128]{1,0:T(8,128)(2,1)}, bf16[512,128]{1,0:T(8,128)(2,1)S(1)}, u32[]{:S(2)}, u32[]{:S(2)}) collective-permute-start(bf16[512,128]{1,0:T(8,128)(2,1)} %bitcast.40), channel_id=1, source_target_pairs={{0,8},{1,9},{2,10},{3,11},{4,40},{5,41},{6,42},{7,43},{8,72},{9,73... | collective-permute-start | bytes 393224 | tf_op jit(solution)/shard_map/ppermute | solution.py:373
  5.8 8.6 %blocks.1 = bf16[128,17,8,128]{3,2,1,0:T(8,128)(2,1)} custom-call(s32[1]{0:T(128)S(6)} %copy.9.start_ref, s32[2,228]{1,0:T(2,128)} %bitcast.41, f32[1,1024]{1,0:T(1,128)} %potential_ref.1, bf16[2048,1024]{1,0:T(8,128)(2,1)} %bitcast.38), custom_call_target="tpu_custom_call" | custom-call | flops 5000000000 | bytes 9000000 | tf_op jit(solution)/shard_map/blocks/pallas_call | solution.py:128
  14.4 8.3 %all-to-all-start = ((bf16[128,136,128]{2,1,0:T(8,128)(2,1)}), bf16[128,136,128]{2,1,0:T(8,128)(2,1)}, u32[]{:S(2)}, u32[]{:S(2)}) async-start(bf16[128,136,128]{2,1,0:T(8,128)(2,1)} %bitcast.25), calls=%async_computation | async-start | bytes 8912896 | tf_op jit(solution)/shard_map/all_to_all | solution.py:376
  22.8 2.7 %collective-permute-start.3 = (bf16[256,128]{1,0:T(8,128)(2,1)S(1)}, bf16[256,128]{1,0:T(8,128)(2,1)S(1)}, u32[]{:S(2)}, u32[]{:S(2)}) collective-permute-start(bf16[256,128]{1,0:T(8,128)(2,1)S(1)} %get-tuple-element.36), channel_id=1, source_target_pairs={{0,1},{1,0},{2,3},{3,2},{4,5},{5,4},{6,7},{7,6},{8,9},{9,8},{10,11... | collective-permute-start | bytes 196616 | tf_op jit(solution)/shard_map/ppermute | solution.py:365
  25.5 3.1 %collective-permute-start.1 = (bf16[256,128]{1,0:T(8,128)(2,1)S(1)}, bf16[256,128]{1,0:T(8,128)(2,1)S(1)}, u32[]{:S(2)}, u32[]{:S(2)}) collective-permute-start(bf16[256,128]{1,0:T(8,128)(2,1)S(1)} %get-tuple-element.37), channel_id=1, source_target_pairs={{0,4},{1,5},{2,6},{3,7},{4,0},{5,1},{6,2},{7,3},{8,12},{9,13},{10,... | collective-permute-start | bytes 196616 | tf_op jit(solution)/shard_map/ppermute | solution.py:365
  28.6 45.5 %collective-permute-done.3 = bf16[256,128]{1,0:T(8,128)(2,1)S(1)} collective-permute-done((bf16[256,128]{1,0:T(8,128)(2,1)S(1)}, bf16[256,128]{1,0:T(8,128)(2,1)S(1)}, u32[]{:S(2)}, u32[]{:S(2)}) %collective-permute-start.3) | collective-permute-done | bytes 65568 | tf_op jit(solution)/shard_map/ppermute | solution.py:365
  74.1 0.1 collective-permute-start.4
  74.2 0.0 collective-permute-done.1
  74.2 1.4 %collective-permute-start.2 = (bf16[2,256,128]{2,1,0:T(8,128)(2,1)S(1)}, bf16[2,256,128]{2,1,0:T(8,128)(2,1)S(1)}, u32[]{:S(2)}, u32[]{:S(2)}) collective-permute-start(bf16[2,256,128]{2,1,0:T(8,128)(2,1)S(1)} %pad_maximum_fusion.6), channel_id=1, source_target_pairs={{0,12},{1,13},{2,14},{3,15},{4,8},{5,9},{6,10},{7,11},{8,4},{9,5},... | collective-permute-start | bytes 393224 | tf_op jit(solution)/shard_map/ppermute | solution.py:369
  75.7 2.6 %collective-permute-done.4 = bf16[2,256,128]{2,1,0:T(8,128)(2,1)S(1)} collective-permute-done((bf16[2,256,128]{2,1,0:T(8,128)(2,1)S(1)}, bf16[2,256,128]{2,1,0:T(8,128)(2,1)S(1)}, u32[]{:S(2)}, u32[]{:S(2)}) %collective-permute-start.4) | collective-permute-done | bytes 131104 | tf_op jit(solution)/shard_map/ppermute | solution.py:369
  78.3 0.1 collective-permute-done.2
  78.5 1.0 collective-permute-start.5
  79.5 2.7 %collective-permute-start.6 = (bf16[4,256,128]{2,1,0:T(8,128)(2,1)S(1)}, bf16[4,256,128]{2,1,0:T(8,128)(2,1)S(1)}, u32[]{:S(2)}, u32[]{:S(2)}) collective-permute-start(bf16[4,256,128]{2,1,0:T(8,128)(2,1)S(1)} %pad_maximum_fusion.3), channel_id=1, source_target_pairs={{0,4},{1,5},{2,6},{3,7},{4,0},{5,1},{6,2},{7,3},{8,12},{9,13},{10,... | collective-permute-start | bytes 786440 | tf_op jit(solution)/shard_map/ppermute | solution.py:365
  82.2 3.6 %sums.1 = (bf16[512,128]{1,0:T(8,128)(2,1)}, bf16[512,128]{1,0:T(8,128)(2,1)}) custom-call(bf16[128,136,128]{2,1,0:T(8,128)(2,1)} %all-to-all-done.in_ref), custom_call_target="tpu_custom_call" | custom-call | flops 300000000 | bytes 4700000 | tf_op jit(solution)/shard_map/sums/pallas_call | solution.py:198
  85.8 0.1 pad_maximum_fusion.refs_0_
  85.8 0.1 collective-permute-done.6
  85.9 0.1 pad_maximum_fusion.1.refs_2_
  86.0 5.9 %collective-permute-start.11 = (bf16[512,128]{1,0:T(8,128)(2,1)}, bf16[512,128]{1,0:T(8,128)(2,1)S(1)}, u32[]{:S(2)}, u32[]{:S(2)}) collective-permute-start(bf16[512,128]{1,0:T(8,128)(2,1)} %get-tuple-element.27), channel_id=1, source_target_pairs={{8,0},{25,17},{10,2},{27,19},{12,4},{29,21},{14,6},{31,23},{0,8},{... | collective-permute-start | bytes 393224 | tf_op jit(solution)/shard_map/ppermute | solution.py:384
  91.9 2.8 %collective-permute-start.9 = (bf16[512,128]{1,0:T(8,128)(2,1)}, bf16[512,128]{1,0:T(8,128)(2,1)S(1)}, u32[]{:S(2)}, u32[]{:S(2)}) collective-permute-start(bf16[512,128]{1,0:T(8,128)(2,1)} %get-tuple-element.26), channel_id=1, source_target_pairs={{0,32},{1,33},{2,34},{3,35},{4,36},{5,37},{6,38},{7,39},{8,40},{9,... | collective-permute-start | bytes 393224 | tf_op jit(solution)/shard_map/ppermute | solution.py:365
  94.7 1.1 collective-permute-start.8
  95.9 1.3 %collective-permute-start.12 = (bf16[512,128]{1,0:T(8,128)(2,1)S(1)}, bf16[512,128]{1,0:T(8,128)(2,1)S(1)}, u32[]{:S(2)}, u32[]{:S(2)}) collective-permute-start(bf16[512,128]{1,0:T(8,128)(2,1)S(1)} %collective-permute-done.11), channel_id=1, source_target_pairs={{0,32},{1,33},{2,34},{3,35},{4,36},{5,37},{6,38},{7,39},{8,40},{9,... | collective-permute-start | bytes 393224 | tf_op jit(solution)/shard_map/ppermute | solution.py:365
  97.2 0.1 collective-permute-done.9
  97.3 0.9 pad_maximum_fusion.4.refs_4_
  98.2 0.8 collective-permute-start.10
  99.0 2.2 %collective-permute-done.12 = bf16[512,128]{1,0:T(8,128)(2,1)S(1)} collective-permute-done((bf16[512,128]{1,0:T(8,128)(2,1)S(1)}, bf16[512,128]{1,0:T(8,128)(2,1)S(1)}, u32[]{:S(2)}, u32[]{:S(2)}) %collective-permute-start.12) | collective-permute-done | bytes 131104 | tf_op jit(solution)/shard_map/ppermute | solution.py:365
  101.2 0.1 collective-permute-start.13
  101.3 3.5 %collective-permute-done.10.refs_5_ = bf16[2,512,128]{2,1,0:T(8,128)(2,1)S(1)} collective-permute-done((bf16[2,512,128]{2,1,0:T(8,128)(2,1)S(1)}, bf16[2,512,128]{2,1,0:T(8,128)(2,1)S(1)}, u32[]{:S(2)}, u32[]{:S(2)}) %collective-permute-start.10) | collective-permute-done | bytes 262176 | tf_op jit(solution)/shard_map/ppermute | solution.py:369
  104.8 2.8 %collective-permute-done.13.refs_7_ = bf16[2,512,128]{2,1,0:T(8,128)(2,1)S(1)} collective-permute-done((bf16[2,512,128]{2,1,0:T(8,128)(2,1)S(1)}, bf16[2,512,128]{2,1,0:T(8,128)(2,1)S(1)}, u32[]{:S(2)}, u32[]{:S(2)}) %collective-permute-start.13) | collective-permute-done | bytes 262176 | tf_op jit(solution)/shard_map/ppermute | solution.py:369
  107.6 1.2 %other.1 = (f32[2,2,128,128]{3,2,1,0:T(8,128)S(1)}, bf16[256,2048]{1,0:T(8,128)(2,1)S(1)}) custom-call(bf16[2,4,256,128]{3,2,1,0:T(8,128)(2,1)S(1)} %pad_maximum_fusion.refs_0_, bf16[2,4,256,128]{3,2,1,0:T(8,128)(2,1)S(1)} %collective-permute-done.7.refs_1_, bf16[2,4,256,128]{3,2,1,0:T(8,128)(2,1)S(1)} %pad_maximum_fusion.1.refs_2_, ...), custom_call_target="tpu_custom_call" | custom-call | flops 270000000 | bytes 4000000 | tf_op jit(solution)/shard_map/other/pallas_call | solution.py:314
  108.8 3.8 %collective-permute-start.14 = (f32[2,2,128,128]{3,2,1,0:T(8,128)S(1)}, f32[2,2,128,128]{3,2,1,0:T(8,128)S(1)}, u32[]{:S(2)}, u32[]{:S(2)}) collective-permute-start(f32[2,2,128,128]{3,2,1,0:T(8,128)S(1)} %get-tuple-element.31), channel_id=1, source_target_pairs={{0,16},{1,17},{2,18},{3,19},{4,20},{5,21},{6,22},{7,23},{8,24},{9,... | collective-permute-start | bytes 786440 | tf_op jit(solution)/shard_map/ppermute | solution.py:391
  112.6 1.3 %mine.1 = (f32[2,2,128,128]{3,2,1,0:T(8,128)S(1)}, bf16[4,2,128,128]{3,2,1,0:T(8,128)(2,1)}) custom-call(bf16[2,4,256,128]{3,2,1,0:T(8,128)(2,1)S(1)} %pad_maximum_fusion.refs_0_, bf16[2,4,256,128]{3,2,1,0:T(8,128)(2,1)S(1)} %collective-permute-done.7.refs_1_, bf16[2,4,256,128]{3,2,1,0:T(8,128)(2,1)S(1)} %pad_maximum_fusion.1.refs_2_, ...), custom_call_target="tpu_custom_call" | custom-call | flops 270000000 | bytes 4000000 | tf_op jit(solution)/shard_map/mine/pallas_call | solution.py:326
  113.9 0.9 copy.8
  (15 shorter events, 0.2 us)
Async XLA Ops:
  0.6 13.8 %collective-permute-start = (bf16[512,128]{1,0:T(8,128)(2,1)}, bf16[512,128]{1,0:T(8,128)(2,1)S(1)}, u32[]{:S(2)}, u32[]{:S(2)}) collective-permute-start(bf16[512,128]{1,0:T(8,128)(2,1)} %bitcast.40), channel_id=1, source_target_pairs={{0,8},{1,9},{2,10},{3,11},{4,40},{5,41},{6,42},{7,43},{8,72},{9,73... | collective-permute-start | bytes 393224 | tf_op jit(solution)/shard_map/ppermute | solution.py:373
  14.4 64.1 %all-to-all-start = ((bf16[128,136,128]{2,1,0:T(8,128)(2,1)}), bf16[128,136,128]{2,1,0:T(8,128)(2,1)}, u32[]{:S(2)}, u32[]{:S(2)}) async-start(bf16[128,136,128]{2,1,0:T(8,128)(2,1)} %bitcast.25), calls=%async_computation | async-start | bytes 8912896 | tf_op jit(solution)/shard_map/all_to_all | solution.py:376
  22.8 51.3 %collective-permute-start.3 = (bf16[256,128]{1,0:T(8,128)(2,1)S(1)}, bf16[256,128]{1,0:T(8,128)(2,1)S(1)}, u32[]{:S(2)}, u32[]{:S(2)}) collective-permute-start(bf16[256,128]{1,0:T(8,128)(2,1)S(1)} %get-tuple-element.36), channel_id=1, source_target_pairs={{0,1},{1,0},{2,3},{3,2},{4,5},{5,4},{6,7},{7,6},{8,9},{9,8},{10,11... | collective-permute-start | bytes 196616 | tf_op jit(solution)/shard_map/ppermute | solution.py:365
  25.5 48.7 %collective-permute-start.1 = (bf16[256,128]{1,0:T(8,128)(2,1)S(1)}, bf16[256,128]{1,0:T(8,128)(2,1)S(1)}, u32[]{:S(2)}, u32[]{:S(2)}) collective-permute-start(bf16[256,128]{1,0:T(8,128)(2,1)S(1)} %get-tuple-element.37), channel_id=1, source_target_pairs={{0,4},{1,5},{2,6},{3,7},{4,0},{5,1},{6,2},{7,3},{8,12},{9,13},{10,... | collective-permute-start | bytes 196616 | tf_op jit(solution)/shard_map/ppermute | solution.py:365
  74.1 4.2 %collective-permute-start.4 = (bf16[2,256,128]{2,1,0:T(8,128)(2,1)S(1)}, bf16[2,256,128]{2,1,0:T(8,128)(2,1)S(1)}, u32[]{:S(2)}, u32[]{:S(2)}) collective-permute-start(bf16[2,256,128]{2,1,0:T(8,128)(2,1)S(1)} %pad_maximum_fusion.7), channel_id=1, source_target_pairs={{0,3},{1,2},{2,1},{3,0},{4,7},{5,6},{6,5},{7,4},{8,11},{9,10},{10,... | collective-permute-start | bytes 393224 | tf_op jit(solution)/shard_map/ppermute | solution.py:369
  74.2 4.2 %collective-permute-start.2 = (bf16[2,256,128]{2,1,0:T(8,128)(2,1)S(1)}, bf16[2,256,128]{2,1,0:T(8,128)(2,1)S(1)}, u32[]{:S(2)}, u32[]{:S(2)}) collective-permute-start(bf16[2,256,128]{2,1,0:T(8,128)(2,1)S(1)} %pad_maximum_fusion.6), channel_id=1, source_target_pairs={{0,12},{1,13},{2,14},{3,15},{4,8},{5,9},{6,10},{7,11},{8,4},{9,5},... | collective-permute-start | bytes 393224 | tf_op jit(solution)/shard_map/ppermute | solution.py:369
  78.5 7.3 %collective-permute-start.5 = (bf16[4,256,128]{2,1,0:T(8,128)(2,1)S(1)}, bf16[4,256,128]{2,1,0:T(8,128)(2,1)S(1)}, u32[]{:S(2)}, u32[]{:S(2)}) collective-permute-start(bf16[4,256,128]{2,1,0:T(8,128)(2,1)S(1)} %pad_maximum_fusion.2), channel_id=1, source_target_pairs={{0,1},{1,0},{2,3},{3,2},{4,5},{5,4},{6,7},{7,6},{8,9},{9,8},{10,11... | collective-permute-start | bytes 786440 | tf_op jit(solution)/shard_map/ppermute | solution.py:365
  79.5 6.4 %collective-permute-start.6 = (bf16[4,256,128]{2,1,0:T(8,128)(2,1)S(1)}, bf16[4,256,128]{2,1,0:T(8,128)(2,1)S(1)}, u32[]{:S(2)}, u32[]{:S(2)}) collective-permute-start(bf16[4,256,128]{2,1,0:T(8,128)(2,1)S(1)} %pad_maximum_fusion.3), channel_id=1, source_target_pairs={{0,4},{1,5},{2,6},{3,7},{4,0},{5,1},{6,2},{7,3},{8,12},{9,13},{10,... | collective-permute-start | bytes 786440 | tf_op jit(solution)/shard_map/ppermute | solution.py:365
  86.0 9.9 %collective-permute-start.11 = (bf16[512,128]{1,0:T(8,128)(2,1)}, bf16[512,128]{1,0:T(8,128)(2,1)S(1)}, u32[]{:S(2)}, u32[]{:S(2)}) collective-permute-start(bf16[512,128]{1,0:T(8,128)(2,1)} %get-tuple-element.27), channel_id=1, source_target_pairs={{8,0},{25,17},{10,2},{27,19},{12,4},{29,21},{14,6},{31,23},{0,8},{... | collective-permute-start | bytes 393224 | tf_op jit(solution)/shard_map/ppermute | solution.py:384
  91.9 5.4 %collective-permute-start.9 = (bf16[512,128]{1,0:T(8,128)(2,1)}, bf16[512,128]{1,0:T(8,128)(2,1)S(1)}, u32[]{:S(2)}, u32[]{:S(2)}) collective-permute-start(bf16[512,128]{1,0:T(8,128)(2,1)} %get-tuple-element.26), channel_id=1, source_target_pairs={{0,32},{1,33},{2,34},{3,35},{4,36},{5,37},{6,38},{7,39},{8,40},{9,... | collective-permute-start | bytes 393224 | tf_op jit(solution)/shard_map/ppermute | solution.py:365
  94.7 10.1 %collective-permute-start.7 = (bf16[2,4,256,128]{3,2,1,0:T(8,128)(2,1)S(1)}, bf16[2,4,256,128]{3,2,1,0:T(8,128)(2,1)S(1)}, u32[]{:S(2)}, u32[]{:S(2)}) collective-permute-start(bf16[2,4,256,128]{3,2,1,0:T(8,128)(2,1)S(1)} %pad_maximum_fusion.refs_0_), channel_id=1, source_target_pairs={{0,3},{1,2},{2,1},{3,0},{4,7},{5,6},{6,5},{7,4},{8,11},{9,10},{10,... | collective-permute-start | bytes 1572872 | tf_op jit(solution)/shard_map/ppermute | solution.py:369
  94.7 10.1 %collective-permute-start.8 = (bf16[2,4,256,128]{3,2,1,0:T(8,128)(2,1)S(1)}, bf16[2,4,256,128]{3,2,1,0:T(8,128)(2,1)S(1)}, u32[]{:S(2)}, u32[]{:S(2)}) collective-permute-start(bf16[2,4,256,128]{3,2,1,0:T(8,128)(2,1)S(1)} %pad_maximum_fusion.1.refs_2_), channel_id=1, source_target_pairs={{0,12},{1,13},{2,14},{3,15},{4,8},{5,9},{6,10},{7,11},{8,4},{9,5},... | collective-permute-start | bytes 1572872 | tf_op jit(solution)/shard_map/ppermute | solution.py:369
  95.9 5.3 %collective-permute-start.12 = (bf16[512,128]{1,0:T(8,128)(2,1)S(1)}, bf16[512,128]{1,0:T(8,128)(2,1)S(1)}, u32[]{:S(2)}, u32[]{:S(2)}) collective-permute-start(bf16[512,128]{1,0:T(8,128)(2,1)S(1)} %collective-permute-done.11), channel_id=1, source_target_pairs={{0,32},{1,33},{2,34},{3,35},{4,36},{5,37},{6,38},{7,39},{8,40},{9,... | collective-permute-start | bytes 393224 | tf_op jit(solution)/shard_map/ppermute | solution.py:365
  98.2 6.6 %collective-permute-start.10 = (bf16[2,512,128]{2,1,0:T(8,128)(2,1)S(1)}, bf16[2,512,128]{2,1,0:T(8,128)(2,1)S(1)}, u32[]{:S(2)}, u32[]{:S(2)}) collective-permute-start(bf16[2,512,128]{2,1,0:T(8,128)(2,1)S(1)} %pad_maximum_fusion.4.refs_4_), channel_id=1, source_target_pairs={{0,96},{1,97},{2,98},{3,99},{4,100},{5,101},{6,102},{7,103},{8,104... | collective-permute-start | bytes 786440 | tf_op jit(solution)/shard_map/ppermute | solution.py:369
  101.2 6.4 %collective-permute-start.13 = (bf16[2,512,128]{2,1,0:T(8,128)(2,1)S(1)}, bf16[2,512,128]{2,1,0:T(8,128)(2,1)S(1)}, u32[]{:S(2)}, u32[]{:S(2)}) collective-permute-start(bf16[2,512,128]{2,1,0:T(8,128)(2,1)S(1)} %pad_maximum_fusion.5.refs_6_), channel_id=1, source_target_pairs={{0,96},{1,97},{2,98},{3,99},{4,100},{5,101},{6,102},{7,103},{8,104... | collective-permute-start | bytes 786440 | tf_op jit(solution)/shard_map/ppermute | solution.py:369
  108.8 5.1 %collective-permute-start.14 = (f32[2,2,128,128]{3,2,1,0:T(8,128)S(1)}, f32[2,2,128,128]{3,2,1,0:T(8,128)S(1)}, u32[]{:S(2)}, u32[]{:S(2)}) collective-permute-start(f32[2,2,128,128]{3,2,1,0:T(8,128)S(1)} %get-tuple-element.31), channel_id=1, source_target_pairs={{0,16},{1,17},{2,18},{3,19},{4,20},{5,21},{6,22},{7,23},{8,24},{9,... | collective-permute-start | bytes 786440 | tf_op jit(solution)/shard_map/ppermute | solution.py:391

commit v6 on v5

--- a/solution.py
+++ b/solution.py
@@ -249,14 +249,16 @@
     return (place_on_ring, first, second, wrap(place_on_ring + 2, 4))[k]
 
 
-def half_product(panels, left, core, z, x, wanted, out_ref):
+def half_product(panels, left, y, core, z, x, wanted, out_ref):
     upper_panel, lower_panel = panels[0:2], panels[2:4]
     depth = 2 * NB
 
     def add_up(steps):
         part = jnp.zeros((2 * NB, 2 * NB), F32)
         for z_step in range(4):
-            start = pl.multiple_of(wrap(ring_place(z, core, z_step) + 2, 4) * (2 * depth), depth)
+            their_z = ring_place(z, core, z_step)
+            their_y = wrap(jnp.where(core == 0, their_z, 2 * y - their_z) + 2, 4)
+            start = pl.multiple_of(their_y * (2 * depth), depth)
             above = [upper_panel[k // 2][k % 2, z_step] for k in steps]
             below = [lower_panel[z_step // 2][z_step % 2, k] for k in steps]
             part = part + jnp.dot(
@@ -294,15 +296,15 @@
 
     for k in range(4):
         kind = home(2 * ring_place(y, core, k) + core, col)
-        column_blocks(kind, col, direct[k // 2].at[k % 2], turned[k // 2].at[k % 2], put)
-    half_product(panels, left, core, col // 4, lax.rem(col, 4), 1 - core, other_ref)
+        column_blocks(kind, col, direct[k % 2].at[k // 2], turned[k // 2].at[k % 2], put)
+    half_product(panels, left, y, core, col // 4, lax.rem(col, 4), 1 - core, other_ref)
 
 
 def mine_kernel(*refs):
     panels, left, mine_ref, blocks_ref = refs[0:4], refs[4], refs[5], refs[6]
     dom, col, _ = place()
     y, core = dom // 2, lax.rem(dom, 2)
-    half_product(panels, left, core, col // 4, lax.rem(col, 4), core, mine_ref)
+    half_product(panels, left, y, core, col // 4, lax.rem(col, 4), core, mine_ref)
     for row in range(4):
         column = pl.ds(pl.multiple_of((y * 4 + row) * NB, NB), NB)
         for half in range(2):
@@ -339,7 +341,10 @@
 
 
 PLACES = [(y, core, col) for y in range(4) for core in range(2) for col in range(NCOL)]
-TO_ROW = [(device(y, core, col), device(col // 4, core, (y + 2) % 4 * 4 + col % 4)) for y, core, col in PLACES]
+TO_ROW = [
+    (device(y, core, col), device(col // 4, core, ((2 * (col // 4) - y if core else y) + 2) % 4 * 4 + col % 4))
+    for y, core, col in PLACES
+]
 TO_OTHER_CORE = [(device(y, core, col), device(y, 1 - core, col)) for y, core, col in PLACES]
 
 
@@ -361,12 +366,12 @@
     return pairs
 
 
-def first_near(value, axis):
-    return jnp.stack([value, lax.ppermute(value, AXES, exchange(axis, 0))])
-
-
-def second_near(pair, axis):
-    return lax.ppermute(pair, AXES, exchange(axis, 1))
+def first_near(value, axis, step=0):
+    return jnp.stack([value, lax.ppermute(value, AXES, exchange(axis, step))])
+
+
+def second_near(pair, axis, step=1):
+    return lax.ppermute(pair, AXES, exchange(axis, step))
 
 
 def shards(orbitals, potential, domain_start, margin_pairs, coefficients):
@@ -382,10 +387,10 @@
     direct, turned = sums(incoming)
     direct, turned, above, below = lax.optimization_barrier((direct, turned, above, below))
     turned = lax.ppermute(turned, AXES, from_partner())
-    direct = first_near(direct, "y")
+    direct = first_near(direct, "y", 1)
     panels = above, second_near(above, "x"), below, second_near(below, "z")
     turned = first_near(turned, "y")
-    direct = direct, second_near(direct, "y")
+    direct = direct, second_near(direct, "y", 0)
     turned = turned, second_near(turned, "y")
     other, left = product_for_other(panels, direct, turned)
     theirs = lax.ppermute(other, AXES, TO_OTHER_CORE)

time: 116 us -> 115 us (level)
  waiting for transfers between devices: 57 us -> 55.1 us
    ppermute x12, waiting for transfers between devices: 57 us -> 54.9 us  [the longest x6 45.6 us: first_near(): return jnp.stack([value, lax.ppermute(value, AXES, exchange(axis, step))])]
    ppermute x12, starting transfers between devices: 17.1 us -> 19.1 us  [the longest x6 14.5 us: first_near(): return jnp.stack([value, lax.ppermute(value, AXES, exchange(axis, step))])]
    ppermute x1, starting transfers between devices: 3.81 us -> 2.59 us  [shards(): theirs = lax.ppermute(other, AXES, TO_OTHER_CORE)]
  transfers between devices with their start and end apart: 16 -> 16, of which waited for: 8 -> 7; matrix products, arithmetic and copies ran while one was open for 1% -> 1% of each run, Pallas kernels for 12% -> 12%
where the time goes in v6:
time: 115 us; the launch traced here: 114 us
  waiting for transfers between devices  55.1 us (48%)
  starting transfers between devices  40.4 us (35%)
  Pallas kernels  14.7 us (13%)
  between operations  1.4 us (1%)
  other arithmetic  1.17 us (1%)
    ppermute x6, waiting for transfers between devices, first_near(): return jnp.stack([value, lax.ppermute(value, AXES, exchange(axis, step))])  45.6 us
    ppermute x6, starting transfers between devices, first_near(): return jnp.stack([value, lax.ppermute(value, AXES, exchange(axis, step))])  14.5 us
    ppermute x6, waiting for transfers between devices, second_near(): return lax.ppermute(pair, AXES, exchange(axis, step))  9.27 us
    pallas_call x1, Pallas kernels, messages(): pl.pallas_call(message_kernel, out_shape=pltpu.HBM((NDEV, TILES + 1, SUB,...  8.62 us
    all_to_all x1, starting transfers between devices, shards(): lax.all_to_all(outgoing, AXES, split_axis=0, concat_axis=0, tiled=True)  8.33 us
    ppermute x1, starting transfers between devices, shards(): turned = lax.ppermute(turned, AXES, from_partner())  5.91 us
    ppermute x6, starting transfers between devices, second_near(): return lax.ppermute(pair, AXES, exchange(axis, step))  4.61 us
    ppermute x1, starting transfers between devices, shards(): own = lax.ppermute(coefficients.reshape(4 * NB, NB), AXES, TO_ROW)  4.49 us
  transfers between devices with their start and end apart: 16, of which 7 were waited for; matrix products, arithmetic and copies ran while one was open for 1% of the time, Pallas kernels for 12%

profile of v6, /device:TPU:1, one launch (start us, length us, event | category | flops | bytes accessed | tf_op | source)
XLA Modules:
  0.0 113.8 jit_solution(2352452649981247443)
XLA Ops:
  0.6 4.5 %collective-permute-start = (bf16[512,128]{1,0:T(8,128)(2,1)}, bf16[512,128]{1,0:T(8,128)(2,1)S(1)}, u32[]{:S(2)}, u32[]{:S(2)}) collective-permute-start(bf16[512,128]{1,0:T(8,128)(2,1)} %bitcast.40), channel_id=1, source_target_pairs={{0,8},{1,9},{2,10},{3,11},{4,40},{5,41},{6,42},{7,43},{8,72},{9,73... | collective-permute-start | bytes 393224 | tf_op jit(solution)/shard_map/ppermute | solution.py:378
  5.8 8.6 %blocks.1 = bf16[128,17,8,128]{3,2,1,0:T(8,128)(2,1)} custom-call(s32[1]{0:T(128)S(6)} %copy.9.start_ref, s32[2,228]{1,0:T(2,128)} %bitcast.41, f32[1,1024]{1,0:T(1,128)} %potential_ref.1, bf16[2048,1024]{1,0:T(8,128)(2,1)} %bitcast.38), custom_call_target="tpu_custom_call" | custom-call | flops 5000000000 | bytes 9000000 | tf_op jit(solution)/shard_map/blocks/pallas_call | solution.py:128
  14.4 8.3 %all-to-all-start = ((bf16[128,136,128]{2,1,0:T(8,128)(2,1)}), bf16[128,136,128]{2,1,0:T(8,128)(2,1)}, u32[]{:S(2)}, u32[]{:S(2)}) async-start(bf16[128,136,128]{2,1,0:T(8,128)(2,1)} %bitcast.25), calls=%async_computation | async-start | bytes 8912896 | tf_op jit(solution)/shard_map/all_to_all | solution.py:381
  22.8 2.7 %collective-permute-start.3 = (bf16[256,128]{1,0:T(8,128)(2,1)S(1)}, bf16[256,128]{1,0:T(8,128)(2,1)S(1)}, u32[]{:S(2)}, u32[]{:S(2)}) collective-permute-start(bf16[256,128]{1,0:T(8,128)(2,1)S(1)} %get-tuple-element.36), channel_id=1, source_target_pairs={{0,1},{1,0},{2,3},{3,2},{4,5},{5,4},{6,7},{7,6},{8,9},{9,8},{10,11... | collective-permute-start | bytes 196616 | tf_op jit(solution)/shard_map/ppermute | solution.py:370
  25.5 3.1 %collective-permute-start.1 = (bf16[256,128]{1,0:T(8,128)(2,1)S(1)}, bf16[256,128]{1,0:T(8,128)(2,1)S(1)}, u32[]{:S(2)}, u32[]{:S(2)}) collective-permute-start(bf16[256,128]{1,0:T(8,128)(2,1)S(1)} %get-tuple-element.37), channel_id=1, source_target_pairs={{0,4},{1,5},{2,6},{3,7},{4,0},{5,1},{6,2},{7,3},{8,12},{9,13},{10,... | collective-permute-start | bytes 196616 | tf_op jit(solution)/shard_map/ppermute | solution.py:370
  28.6 45.5 %collective-permute-done.3 = bf16[256,128]{1,0:T(8,128)(2,1)S(1)} collective-permute-done((bf16[256,128]{1,0:T(8,128)(2,1)S(1)}, bf16[256,128]{1,0:T(8,128)(2,1)S(1)}, u32[]{:S(2)}, u32[]{:S(2)}) %collective-permute-start.3) | collective-permute-done | bytes 65568 | tf_op jit(solution)/shard_map/ppermute | solution.py:370
  74.1 0.1 collective-permute-start.4
  74.2 1.4 %collective-permute-start.2 = (bf16[2,256,128]{2,1,0:T(8,128)(2,1)S(1)}, bf16[2,256,128]{2,1,0:T(8,128)(2,1)S(1)}, u32[]{:S(2)}, u32[]{:S(2)}) collective-permute-start(bf16[2,256,128]{2,1,0:T(8,128)(2,1)S(1)} %pad_maximum_fusion.6), channel_id=1, source_target_pairs={{0,12},{1,13},{2,14},{3,15},{4,8},{5,9},{6,10},{7,11},{8,4},{9,5},... | collective-permute-start | bytes 393224 | tf_op jit(solution)/shard_map/ppermute | solution.py:374
  75.7 2.6 %collective-permute-done.4 = bf16[2,256,128]{2,1,0:T(8,128)(2,1)S(1)} collective-permute-done((bf16[2,256,128]{2,1,0:T(8,128)(2,1)S(1)}, bf16[2,256,128]{2,1,0:T(8,128)(2,1)S(1)}, u32[]{:S(2)}, u32[]{:S(2)}) %collective-permute-start.4) | collective-permute-done | bytes 131104 | tf_op jit(solution)/shard_map/ppermute | solution.py:374
  78.3 0.1 collective-permute-done.2
  78.5 1.0 collective-permute-start.5
  79.5 2.7 %collective-permute-start.6 = (bf16[4,256,128]{2,1,0:T(8,128)(2,1)S(1)}, bf16[4,256,128]{2,1,0:T(8,128)(2,1)S(1)}, u32[]{:S(2)}, u32[]{:S(2)}) collective-permute-start(bf16[4,256,128]{2,1,0:T(8,128)(2,1)S(1)} %pad_maximum_fusion.3), channel_id=1, source_target_pairs={{0,4},{1,5},{2,6},{3,7},{4,0},{5,1},{6,2},{7,3},{8,12},{9,13},{10,... | collective-permute-start | bytes 786440 | tf_op jit(solution)/shard_map/ppermute | solution.py:370
  82.2 3.6 %sums.1 = (bf16[512,128]{1,0:T(8,128)(2,1)}, bf16[512,128]{1,0:T(8,128)(2,1)}) custom-call(bf16[128,136,128]{2,1,0:T(8,128)(2,1)} %all-to-all-done.in_ref), custom_call_target="tpu_custom_call" | custom-call | flops 300000000 | bytes 4700000 | tf_op jit(solution)/shard_map/sums/pallas_call | solution.py:198
  85.7 0.0 collective-permute-done.5
  85.7 0.1 pad_maximum_fusion.refs_0_
  85.8 0.1 collective-permute-done.6
  85.9 0.1 pad_maximum_fusion.1.refs_2_
  86.0 5.9 %collective-permute-start.11 = (bf16[512,128]{1,0:T(8,128)(2,1)}, bf16[512,128]{1,0:T(8,128)(2,1)S(1)}, u32[]{:S(2)}, u32[]{:S(2)}) collective-permute-start(bf16[512,128]{1,0:T(8,128)(2,1)} %get-tuple-element.27), channel_id=1, source_target_pairs={{8,0},{25,17},{10,2},{27,19},{12,4},{29,21},{14,6},{31,23},{0,8},{... | collective-permute-start | bytes 393224 | tf_op jit(solution)/shard_map/ppermute | solution.py:389
  91.9 2.0 %collective-permute-start.9 = (bf16[512,128]{1,0:T(8,128)(2,1)}, bf16[512,128]{1,0:T(8,128)(2,1)S(1)}, u32[]{:S(2)}, u32[]{:S(2)}) collective-permute-start(bf16[512,128]{1,0:T(8,128)(2,1)} %get-tuple-element.26), channel_id=1, source_target_pairs={{0,96},{1,97},{2,98},{3,99},{4,100},{5,101},{6,102},{7,103},{8,104... | collective-permute-start | bytes 393224 | tf_op jit(solution)/shard_map/ppermute | solution.py:370
  93.9 0.0 collective-permute-start.7
  93.9 0.0 collective-permute-start.8
  93.9 0.2 collective-permute-done.11
  94.1 3.0 %collective-permute-start.12 = (bf16[512,128]{1,0:T(8,128)(2,1)S(1)}, bf16[512,128]{1,0:T(8,128)(2,1)S(1)}, u32[]{:S(2)}, u32[]{:S(2)}) collective-permute-start(bf16[512,128]{1,0:T(8,128)(2,1)S(1)} %collective-permute-done.11), channel_id=1, source_target_pairs={{0,32},{1,33},{2,34},{3,35},{4,36},{5,37},{6,38},{7,39},{8,40},{9,... | collective-permute-start | bytes 393224 | tf_op jit(solution)/shard_map/ppermute | solution.py:370
  97.1 0.9 pad_maximum_fusion.4.refs_4_
  98.1 2.0 %collective-permute-start.10 = (bf16[2,512,128]{2,1,0:T(8,128)(2,1)S(1)}, bf16[2,512,128]{2,1,0:T(8,128)(2,1)S(1)}, u32[]{:S(2)}, u32[]{:S(2)}) collective-permute-start(bf16[2,512,128]{2,1,0:T(8,128)(2,1)S(1)} %pad_maximum_fusion.4.refs_4_), channel_id=1, source_target_pairs={{0,32},{1,33},{2,34},{3,35},{4,36},{5,37},{6,38},{7,39},{8,40},{9,... | collective-permute-start | bytes 786440 | tf_op jit(solution)/shard_map/ppermute | solution.py:374
  100.1 1.1 collective-permute-start.13
  101.2 3.7 %collective-permute-done.10.refs_5_ = bf16[2,512,128]{2,1,0:T(8,128)(2,1)S(1)} collective-permute-done((bf16[2,512,128]{2,1,0:T(8,128)(2,1)S(1)}, bf16[2,512,128]{2,1,0:T(8,128)(2,1)S(1)}, u32[]{:S(2)}, u32[]{:S(2)}) %collective-permute-start.10) | collective-permute-done | bytes 262176 | tf_op jit(solution)/shard_map/ppermute | solution.py:374
  104.9 2.8 %collective-permute-done.13.refs_7_ = bf16[2,512,128]{2,1,0:T(8,128)(2,1)S(1)} collective-permute-done((bf16[2,512,128]{2,1,0:T(8,128)(2,1)S(1)}, bf16[2,512,128]{2,1,0:T(8,128)(2,1)S(1)}, u32[]{:S(2)}, u32[]{:S(2)}) %collective-permute-start.13) | collective-permute-done | bytes 262176 | tf_op jit(solution)/shard_map/ppermute | solution.py:374
  107.7 1.2 %other.1 = (f32[2,2,128,128]{3,2,1,0:T(8,128)S(1)}, bf16[256,2048]{1,0:T(8,128)(2,1)S(1)}) custom-call(bf16[2,4,256,128]{3,2,1,0:T(8,128)(2,1)S(1)} %pad_maximum_fusion.refs_0_, bf16[2,4,256,128]{3,2,1,0:T(8,128)(2,1)S(1)} %collective-permute-done.7.refs_1_, bf16[2,4,256,128]{3,2,1,0:T(8,128)(2,1)S(1)} %pad_maximum_fusion.1.refs_2_, ...), custom_call_target="tpu_custom_call" | custom-call | flops 270000000 | bytes 4000000 | tf_op jit(solution)/shard_map/other/pallas_call | solution.py:316
  108.9 2.6 %collective-permute-start.14 = (f32[2,2,128,128]{3,2,1,0:T(8,128)S(1)}, f32[2,2,128,128]{3,2,1,0:T(8,128)S(1)}, u32[]{:S(2)}, u32[]{:S(2)}) collective-permute-start(f32[2,2,128,128]{3,2,1,0:T(8,128)S(1)} %get-tuple-element.31), channel_id=1, source_target_pairs={{0,16},{1,17},{2,18},{3,19},{4,20},{5,21},{6,22},{7,23},{8,24},{9,... | collective-permute-start | bytes 786440 | tf_op jit(solution)/shard_map/ppermute | solution.py:396
  111.5 1.3 %mine.1 = (f32[2,2,128,128]{3,2,1,0:T(8,128)S(1)}, bf16[4,2,128,128]{3,2,1,0:T(8,128)(2,1)}) custom-call(bf16[2,4,256,128]{3,2,1,0:T(8,128)(2,1)S(1)} %pad_maximum_fusion.refs_0_, bf16[2,4,256,128]{3,2,1,0:T(8,128)(2,1)S(1)} %collective-permute-done.7.refs_1_, bf16[2,4,256,128]{3,2,1,0:T(8,128)(2,1)S(1)} %pad_maximum_fusion.1.refs_2_, ...), custom_call_target="tpu_custom_call" | custom-call | flops 270000000 | bytes 4000000 | tf_op jit(solution)/shard_map/mine/pallas_call | solution.py:328
  112.9 0.9 copy.8
  (15 shorter events, 0.2 us)
Async XLA Ops:
  0.6 13.8 %collective-permute-start = (bf16[512,128]{1,0:T(8,128)(2,1)}, bf16[512,128]{1,0:T(8,128)(2,1)S(1)}, u32[]{:S(2)}, u32[]{:S(2)}) collective-permute-start(bf16[512,128]{1,0:T(8,128)(2,1)} %bitcast.40), channel_id=1, source_target_pairs={{0,8},{1,9},{2,10},{3,11},{4,40},{5,41},{6,42},{7,43},{8,72},{9,73... | collective-permute-start | bytes 393224 | tf_op jit(solution)/shard_map/ppermute | solution.py:378
  14.4 64.0 %all-to-all-start = ((bf16[128,136,128]{2,1,0:T(8,128)(2,1)}), bf16[128,136,128]{2,1,0:T(8,128)(2,1)}, u32[]{:S(2)}, u32[]{:S(2)}) async-start(bf16[128,136,128]{2,1,0:T(8,128)(2,1)} %bitcast.25), calls=%async_computation | async-start | bytes 8912896 | tf_op jit(solution)/shard_map/all_to_all | solution.py:381
  22.8 51.3 %collective-permute-start.3 = (bf16[256,128]{1,0:T(8,128)(2,1)S(1)}, bf16[256,128]{1,0:T(8,128)(2,1)S(1)}, u32[]{:S(2)}, u32[]{:S(2)}) collective-permute-start(bf16[256,128]{1,0:T(8,128)(2,1)S(1)} %get-tuple-element.36), channel_id=1, source_target_pairs={{0,1},{1,0},{2,3},{3,2},{4,5},{5,4},{6,7},{7,6},{8,9},{9,8},{10,11... | collective-permute-start | bytes 196616 | tf_op jit(solution)/shard_map/ppermute | solution.py:370
  25.5 48.7 %collective-permute-start.1 = (bf16[256,128]{1,0:T(8,128)(2,1)S(1)}, bf16[256,128]{1,0:T(8,128)(2,1)S(1)}, u32[]{:S(2)}, u32[]{:S(2)}) collective-permute-start(bf16[256,128]{1,0:T(8,128)(2,1)S(1)} %get-tuple-element.37), channel_id=1, source_target_pairs={{0,4},{1,5},{2,6},{3,7},{4,0},{5,1},{6,2},{7,3},{8,12},{9,13},{10,... | collective-permute-start | bytes 196616 | tf_op jit(solution)/shard_map/ppermute | solution.py:370
  74.1 4.2 %collective-permute-start.4 = (bf16[2,256,128]{2,1,0:T(8,128)(2,1)S(1)}, bf16[2,256,128]{2,1,0:T(8,128)(2,1)S(1)}, u32[]{:S(2)}, u32[]{:S(2)}) collective-permute-start(bf16[2,256,128]{2,1,0:T(8,128)(2,1)S(1)} %pad_maximum_fusion.7), channel_id=1, source_target_pairs={{0,3},{1,2},{2,1},{3,0},{4,7},{5,6},{6,5},{7,4},{8,11},{9,10},{10,... | collective-permute-start | bytes 393224 | tf_op jit(solution)/shard_map/ppermute | solution.py:374
  74.2 4.2 %collective-permute-start.2 = (bf16[2,256,128]{2,1,0:T(8,128)(2,1)S(1)}, bf16[2,256,128]{2,1,0:T(8,128)(2,1)S(1)}, u32[]{:S(2)}, u32[]{:S(2)}) collective-permute-start(bf16[2,256,128]{2,1,0:T(8,128)(2,1)S(1)} %pad_maximum_fusion.6), channel_id=1, source_target_pairs={{0,12},{1,13},{2,14},{3,15},{4,8},{5,9},{6,10},{7,11},{8,4},{9,5},... | collective-permute-start | bytes 393224 | tf_op jit(solution)/shard_map/ppermute | solution.py:374
  78.5 7.3 %collective-permute-start.5 = (bf16[4,256,128]{2,1,0:T(8,128)(2,1)S(1)}, bf16[4,256,128]{2,1,0:T(8,128)(2,1)S(1)}, u32[]{:S(2)}, u32[]{:S(2)}) collective-permute-start(bf16[4,256,128]{2,1,0:T(8,128)(2,1)S(1)} %pad_maximum_fusion.2), channel_id=1, source_target_pairs={{0,1},{1,0},{2,3},{3,2},{4,5},{5,4},{6,7},{7,6},{8,9},{9,8},{10,11... | collective-permute-start | bytes 786440 | tf_op jit(solution)/shard_map/ppermute | solution.py:370
  79.5 6.4 %collective-permute-start.6 = (bf16[4,256,128]{2,1,0:T(8,128)(2,1)S(1)}, bf16[4,256,128]{2,1,0:T(8,128)(2,1)S(1)}, u32[]{:S(2)}, u32[]{:S(2)}) collective-permute-start(bf16[4,256,128]{2,1,0:T(8,128)(2,1)S(1)} %pad_maximum_fusion.3), channel_id=1, source_target_pairs={{0,4},{1,5},{2,6},{3,7},{4,0},{5,1},{6,2},{7,3},{8,12},{9,13},{10,... | collective-permute-start | bytes 786440 | tf_op jit(solution)/shard_map/ppermute | solution.py:370
  86.0 8.2 %collective-permute-start.11 = (bf16[512,128]{1,0:T(8,128)(2,1)}, bf16[512,128]{1,0:T(8,128)(2,1)S(1)}, u32[]{:S(2)}, u32[]{:S(2)}) collective-permute-start(bf16[512,128]{1,0:T(8,128)(2,1)} %get-tuple-element.27), channel_id=1, source_target_pairs={{8,0},{25,17},{10,2},{27,19},{12,4},{29,21},{14,6},{31,23},{0,8},{... | collective-permute-start | bytes 393224 | tf_op jit(solution)/shard_map/ppermute | solution.py:389
  91.9 5.3 %collective-permute-start.9 = (bf16[512,128]{1,0:T(8,128)(2,1)}, bf16[512,128]{1,0:T(8,128)(2,1)S(1)}, u32[]{:S(2)}, u32[]{:S(2)}) collective-permute-start(bf16[512,128]{1,0:T(8,128)(2,1)} %get-tuple-element.26), channel_id=1, source_target_pairs={{0,96},{1,97},{2,98},{3,99},{4,100},{5,101},{6,102},{7,103},{8,104... | collective-permute-start | bytes 393224 | tf_op jit(solution)/shard_map/ppermute | solution.py:370
  93.9 11.0 %collective-permute-start.7 = (bf16[2,4,256,128]{3,2,1,0:T(8,128)(2,1)S(1)}, bf16[2,4,256,128]{3,2,1,0:T(8,128)(2,1)S(1)}, u32[]{:S(2)}, u32[]{:S(2)}) collective-permute-start(bf16[2,4,256,128]{3,2,1,0:T(8,128)(2,1)S(1)} %pad_maximum_fusion.refs_0_), channel_id=1, source_target_pairs={{0,3},{1,2},{2,1},{3,0},{4,7},{5,6},{6,5},{7,4},{8,11},{9,10},{10,... | collective-permute-start | bytes 1572872 | tf_op jit(solution)/shard_map/ppermute | solution.py:374
  93.9 11.0 %collective-permute-start.8 = (bf16[2,4,256,128]{3,2,1,0:T(8,128)(2,1)S(1)}, bf16[2,4,256,128]{3,2,1,0:T(8,128)(2,1)S(1)}, u32[]{:S(2)}, u32[]{:S(2)}) collective-permute-start(bf16[2,4,256,128]{3,2,1,0:T(8,128)(2,1)S(1)} %pad_maximum_fusion.1.refs_2_), channel_id=1, source_target_pairs={{0,12},{1,13},{2,14},{3,15},{4,8},{5,9},{6,10},{7,11},{8,4},{9,5},... | collective-permute-start | bytes 1572872 | tf_op jit(solution)/shard_map/ppermute | solution.py:374
  94.1 5.9 %collective-permute-start.12 = (bf16[512,128]{1,0:T(8,128)(2,1)S(1)}, bf16[512,128]{1,0:T(8,128)(2,1)S(1)}, u32[]{:S(2)}, u32[]{:S(2)}) collective-permute-start(bf16[512,128]{1,0:T(8,128)(2,1)S(1)} %collective-permute-done.11), channel_id=1, source_target_pairs={{0,32},{1,33},{2,34},{3,35},{4,36},{5,37},{6,38},{7,39},{8,40},{9,... | collective-permute-start | bytes 393224 | tf_op jit(solution)/shard_map/ppermute | solution.py:370
  98.1 6.8 %collective-permute-start.10 = (bf16[2,512,128]{2,1,0:T(8,128)(2,1)S(1)}, bf16[2,512,128]{2,1,0:T(8,128)(2,1)S(1)}, u32[]{:S(2)}, u32[]{:S(2)}) collective-permute-start(bf16[2,512,128]{2,1,0:T(8,128)(2,1)S(1)} %pad_maximum_fusion.4.refs_4_), channel_id=1, source_target_pairs={{0,32},{1,33},{2,34},{3,35},{4,36},{5,37},{6,38},{7,39},{8,40},{9,... | collective-permute-start | bytes 786440 | tf_op jit(solution)/shard_map/ppermute | solution.py:374
  100.1 7.7 %collective-permute-start.13 = (bf16[2,512,128]{2,1,0:T(8,128)(2,1)S(1)}, bf16[2,512,128]{2,1,0:T(8,128)(2,1)S(1)}, u32[]{:S(2)}, u32[]{:S(2)}) collective-permute-start(bf16[2,512,128]{2,1,0:T(8,128)(2,1)S(1)} %pad_maximum_fusion.5.refs_6_), channel_id=1, source_target_pairs={{0,96},{1,97},{2,98},{3,99},{4,100},{5,101},{6,102},{7,103},{8,104... | collective-permute-start | bytes 786440 | tf_op jit(solution)/shard_map/ppermute | solution.py:374
  108.9 3.9 %collective-permute-start.14 = (f32[2,2,128,128]{3,2,1,0:T(8,128)S(1)}, f32[2,2,128,128]{3,2,1,0:T(8,128)S(1)}, u32[]{:S(2)}, u32[]{:S(2)}) collective-permute-start(f32[2,2,128,128]{3,2,1,0:T(8,128)S(1)} %get-tuple-element.31), channel_id=1, source_target_pairs={{0,16},{1,17},{2,18},{3,19},{4,20},{5,21},{6,22},{7,23},{8,24},{9,... | collective-permute-start | bytes 786440 | tf_op jit(solution)/shard_map/ppermute | solution.py:396
